TPU v7x, 32 devices: a whole 2x2x4 slice. The times are simulated.
32 devices in a mesh: shot: 2 (over x), slab: 16 (over z, y, core).
Axes of the slice: x: 2, y: 2, z: 4, core: 2. Of those that a mesh axis runs over, the one named last changes fastest.
Arguments:
- wavefield: float32 [2, 2, 2048, 2048], P('shot', None, 'slab'), parts along dimension 0, may hold values from -5 to 5
- frequencies: float32 [2], P('shot'), parts along dimension 0, may hold values from 1 to 3
- velocity: float32 [1, 2048, 2048], P(None, 'slab'), may hold values from 1 to 2.25, as said below
- bracket: int32 [1, 2048, 2048], P(None, 'slab'), may hold values from 0 to 1
Outputs:
- propagated: float32 [2, 2, 2048, 2048], P('shot', None, 'slab'), parts along dimension 0
- image: float32 [2, 2048, 2048], P('shot', 'slab'), parts along dimension 0
There are 2 independent parts, one for each index of `shot`. A program takes and returns all parts, laid end to end along the dimension named above; an argument that names none is the same for every part. Nothing has to cross between parts.
Inputs may be any that keep to these rules, and one draw needn't show every extreme that they name: velocity[d, y, x] lies between the reference speeds c_b and c_(b+1) with b = bracket[d, x, y].
All inputs are finite; a program needn't handle non-finite values.
Results may differ from a plain program's by a relative error of at most 0.0003.
Values sent between devices are 32-bit elements; how exact they have to be, the bound alone decides.
No kernel may reach another device: no remote copies, remote signals or barrier semaphores. Data moves between devices by JAX's collectives and lax.ppermute only.
A program may use at most 64 MiB of HBM per device.

v0:
```python
import math

import jax
import jax.numpy as jnp
import ml_dtypes
import numpy as np
from jax import lax
from jax.experimental import pallas as pl
from jax.experimental.pallas import tpu as pltpu
from jax.sharding import PartitionSpec as P

ref_speeds = (1.0, 1.5, 2.25)
step_length = 1.0
highest = lax.Precision.HIGHEST


def dft_table(height, breadth, modulus, direction):
    down_index = lax.iota(jnp.int32, height)[:, None]
    across_index = lax.iota(jnp.int32, breadth)[None, :]
    angles = (down_index * across_index % modulus).astype(jnp.float32) * (
        direction * 2.0 * math.pi / modulus
    )
    return (jnp.cos(angles), jnp.sin(angles))


def contract(pattern, left_pair, right_pair):

    def product(one_side, other_side):
        return jnp.einsum(pattern, one_side, other_side, precision=highest)

    return (
        product(left_pair[0], right_pair[0]) - product(left_pair[1], right_pair[1]),
        product(left_pair[0], right_pair[1]) + product(left_pair[1], right_pair[0]),
    )


def rotate(values, factor_pair):
    return (
        values[0] * factor_pair[0] - values[1] * factor_pair[1],
        values[0] * factor_pair[1] + values[1] * factor_pair[0],
    )


def forward_lines(fields):
    item_count, row_count, extent = fields[0].shape
    devices = lax.axis_size("slab")
    line_count = extent // devices
    reshaped = tuple(
        (part_now.reshape(item_count, row_count, line_count, devices) for part_now in fields)
    )
    section_one = contract(
        "nrab,ak->nrkb", reshaped, dft_table(line_count, line_count, line_count, -1.0)
    )
    twisted = rotate(
        section_one,
        tuple((turning[None, None] for turning in dft_table(line_count, devices, extent, -1.0))),
    )
    section_two = contract("nrkb,bq->nkqr", twisted, dft_table(devices, devices, devices, -1.0))
    return tuple(
        (part_now.reshape(item_count, line_count, devices * row_count) for part_now in section_two)
    )


def forward_rows(fields):
    item_count, line_count, extent = fields[0].shape
    devices = lax.axis_size("slab")
    row_count = extent // devices
    reshaped = tuple(
        (part_now.reshape(item_count, line_count, devices, row_count) for part_now in fields)
    )
    section_one = contract("ncab,ak->nckb", reshaped, dft_table(devices, devices, devices, -1.0))
    twisted = rotate(
        section_one,
        tuple((turning[None, None] for turning in dft_table(devices, row_count, extent, -1.0))),
    )
    section_two = contract(
        "nckb,bq->nckq", twisted, dft_table(row_count, row_count, row_count, -1.0)
    )
    return tuple((part_now.reshape(item_count, line_count, extent) for part_now in section_two))


def inverse_rows(fields):
    item_count, line_count, extent = fields[0].shape
    devices = lax.axis_size("slab")
    row_count = extent // devices
    reshaped = tuple(
        (part_now.reshape(item_count, line_count, devices, row_count) for part_now in fields)
    )
    section_one = contract(
        "nckq,bq->nckb", reshaped, dft_table(row_count, row_count, row_count, 1.0)
    )
    twisted = rotate(
        section_one,
        tuple((turning[None, None] for turning in dft_table(devices, row_count, extent, 1.0))),
    )
    section_two = contract("nckb,ak->ncab", twisted, dft_table(devices, devices, devices, 1.0))
    return tuple(
        (
            part_now.reshape(item_count, line_count, extent) * (1.0 / extent)
            for part_now in section_two
        )
    )


def inverse_lines(fields):
    item_count, line_count, extent = fields[0].shape
    devices = lax.axis_size("slab")
    row_count = extent // devices
    total_lines = line_count * devices
    reshaped = tuple(
        (part_now.reshape(item_count, line_count, devices, row_count) for part_now in fields)
    )
    section_one = contract("nkqr,bq->nkbr", reshaped, dft_table(devices, devices, devices, 1.0))
    twisted = rotate(
        section_one,
        tuple(
            (
                turning[None, :, :, None]
                for turning in dft_table(line_count, devices, total_lines, 1.0)
            )
        ),
    )
    section_two = contract(
        "nkbr,ak->nrab", twisted, dft_table(line_count, line_count, line_count, 1.0)
    )
    return tuple(
        (
            part_now.reshape(item_count, row_count, total_lines) * (1.0 / total_lines)
            for part_now in section_two
        )
    )


def phase_shift(values, wave_square, angular):
    slowness = 1.0 / jnp.array(ref_speeds, jnp.float32)
    wave_number = angular[:, None] * slowness[None, :]
    vertical = (wave_number * wave_number)[:, :, None, None] - wave_square[None, None]
    root_abs = jnp.sqrt(jnp.abs(vertical))
    real_part = jnp.where(
        vertical >= 0, jnp.cos(step_length * root_abs), jnp.exp(-step_length * root_abs)
    )
    imag_part = jnp.where(vertical >= 0, jnp.sin(step_length * root_abs), 0.0)
    shifted = rotate((values[0][:, None], values[1][:, None]), (real_part, imag_part))
    item_count = values[0].shape[0]
    return tuple(
        (
            part_now.reshape((item_count * len(ref_speeds),) + values[0].shape[1:])
            for part_now in shifted
        )
    )


def weights(speed_grid, chosen):
    speeds = jnp.array(ref_speeds, jnp.float32)
    lower_speed = jnp.zeros_like(speed_grid)
    upper_speed = jnp.zeros_like(speed_grid)
    for ref_index in range(len(ref_speeds) - 1):
        lower_speed = lower_speed + jnp.where(chosen == ref_index, speeds[ref_index], 0.0)
        upper_speed = upper_speed + jnp.where(chosen == ref_index, speeds[ref_index + 1], 0.0)
    fraction = (speed_grid - lower_speed) / (upper_speed - lower_speed)
    residual_phase = 1.0 / speed_grid - ((1.0 - fraction) / lower_speed + fraction / upper_speed)
    coefficients = []
    for ref_index in range(len(ref_speeds)):
        coefficients.append(
            jnp.where(chosen == ref_index, 1.0 - fraction, 0.0)
            + jnp.where(chosen == ref_index - 1, fraction, 0.0)
        )
    return (jnp.stack(coefficients), residual_phase)


def advance(fields, angular, coefficients, residual_phase, spec_square):
    item_count, row_count, extent = fields[0].shape
    prepared = forward_lines(fields)
    spectrum = forward_rows(
        (
            lax.all_to_all(prepared[0], "slab", split_axis=2, concat_axis=2, tiled=True),
            lax.all_to_all(prepared[1], "slab", split_axis=2, concat_axis=2, tiled=True),
        )
    )
    returned = inverse_rows(phase_shift(spectrum, spec_square, angular))
    waves = inverse_lines(
        (
            lax.all_to_all(returned[0], "slab", split_axis=2, concat_axis=2, tiled=True),
            lax.all_to_all(returned[1], "slab", split_axis=2, concat_axis=2, tiled=True),
        )
    )
    ref_count = len(ref_speeds)
    wave_real = waves[0].reshape(item_count, ref_count, row_count, extent)
    wave_imag = waves[1].reshape(item_count, ref_count, row_count, extent)
    blended_real = jnp.sum(coefficients[None] * wave_real, axis=1)
    blended_imag = jnp.sum(coefficients[None] * wave_imag, axis=1)
    angles = angular[:, None, None] * step_length * residual_phase[None]
    return rotate((blended_real, blended_imag), (jnp.cos(angles), jnp.sin(angles)))


def folded(indices, modulus):
    return jnp.minimum(indices, modulus - indices).astype(jnp.float32) * (2.0 * math.pi / modulus)


def per_device_general(wavefield, frequencies, velocity, bracket):
    devices = lax.axis_size("slab")
    device_index = lax.axis_index("slab")
    row_count = wavefield.shape[2]
    extent_y = wavefield.shape[3]
    extent_x = row_count * devices
    line_count = extent_y // devices
    speed_columns = lax.all_to_all(velocity, "slab", split_axis=2, concat_axis=1, tiled=True)
    speed_rows = jnp.transpose(speed_columns, (0, 2, 1))
    column = lax.iota(jnp.int32, extent_x)
    line_index = lax.iota(jnp.int32, line_count)
    spec_first = folded(column // row_count + devices * (column % row_count), extent_x)
    spec_second = folded(device_index * line_count + line_index, extent_y)
    spec_square = (
        spec_first[None, :] * spec_first[None, :] + spec_second[:, None] * spec_second[:, None]
    )
    current = (wavefield[:, 0], wavefield[:, 1])
    coefficients, residual_phase = weights(speed_rows[0], bracket[0])
    single = (current[0], current[1])
    pieces = [advance(single, frequencies, coefficients, residual_phase, spec_square)]
    current = (
        jnp.concatenate([piece[0] for piece in pieces], axis=0),
        jnp.concatenate([piece[1] for piece in pieces], axis=0),
    )
    image_rows = [jnp.sum(current[0], axis=0)]
    return (jnp.stack(current, axis=1), jnp.stack(image_rows))


radix = 16
lane = 128
full = radix * lane
row_block = 32
blocks = lane // row_block
piece = 2 * row_block + row_block // 2
vmem_bytes = 56 * 1024 * 1024


def split_table(table):
    upper = table.astype(ml_dtypes.bfloat16)
    lower = (table - upper.astype(np.float64)).astype(ml_dtypes.bfloat16)
    return upper, lower


def line_matrices(direction):
    angles = 2.0 * np.pi / lane * (np.outer(np.arange(lane), np.arange(lane)) % lane)
    cosine, sine = np.cos(angles), direction * np.sin(angles)
    return np.block([[cosine, sine], [-sine, cosine]])


def right_table(direction):
    upper, lower = split_table(line_matrices(direction))
    return np.concatenate([upper, upper, lower], axis=0)


def left_table(direction):
    upper, lower = split_table(line_matrices(direction).T)
    return np.concatenate([upper, upper, lower], axis=1)


def twiddle(direction, scale):
    angles = 2.0 * np.pi / full * np.outer(np.arange(radix), np.arange(lane))
    return np.stack([np.cos(angles), direction * np.sin(angles)], axis=1) * scale


def lane_twiddle(direction, scale):
    table = twiddle(direction, scale)[:, :, None, :]
    return np.ascontiguousarray(np.broadcast_to(table, (radix, 2, 8, lane))).astype(np.float32)


def sublane_twiddle(direction, scale):
    table = twiddle(direction, scale)[:, :, :, None]
    return np.ascontiguousarray(np.broadcast_to(table, (radix, 2, lane, lane))).astype(np.float32)


def root_series(offset, degree):
    nodes = np.polynomial.chebyshev.Chebyshev.interpolate(
        lambda q: np.sinc(np.sqrt(q) / np.pi) if offset else np.cos(np.sqrt(q)), degree, domain=[0.0, 9.0]
    )
    return [float(value) for value in nodes.convert(kind=np.polynomial.Polynomial).coef]


cos_series = root_series(0, 7)
sinc_series = root_series(1, 6)


def horner(series, argument):
    total = jnp.full_like(argument, series[-1])
    for value in series[-2::-1]:
        total = total * argument + value
    return total


def times(left, right):
    return left[0] * right[0] - left[1] * right[1], left[0] * right[1] + left[1] * right[0]


def quarter(values, direction):
    (a_re, a_im), (b_re, b_im), (c_re, c_im), (d_re, d_im) = values
    p_re, p_im, m_re, m_im = a_re + c_re, a_im + c_im, a_re - c_re, a_im - c_im
    q_re, q_im, n_re, n_im = b_re + d_re, b_im + d_im, b_re - d_re, b_im - d_im
    if direction < 0:
        turn_re, turn_im = n_im, -n_re
    else:
        turn_re, turn_im = -n_im, n_re
    return [
        (p_re + q_re, p_im + q_im),
        (m_re + turn_re, m_im + turn_im),
        (p_re - q_re, p_im - q_im),
        (m_re - turn_re, m_im - turn_im),
    ]


def turned(value, power, direction):
    re, im = value
    power %= 16
    if power == 0:
        return value
    if power == 4:
        return (-direction * im, direction * re) if direction < 0 else (-im, re)
    half = math.sqrt(0.5)
    if power == 2:
        return ((re - direction * im) * half, (im + direction * re) * half)
    if power == 6:
        return ((-re - direction * im) * half, (direction * re - im) * half)
    cosine, sine = math.cos(math.pi * power / 8), direction * math.sin(math.pi * power / 8)
    return re * cosine - im * sine, re * sine + im * cosine


def sixteen(values, direction):
    first = [quarter([values[4 * a + b] for a in range(4)], direction) for b in range(4)]
    result = [None] * 16
    for c in range(4):
        outs = quarter([turned(first[b][c], b * c, direction) for b in range(4)], direction)
        for d in range(4):
            result[c + 4 * d] = outs[d]
    return result


def halves(values):
    upper = values.astype(jnp.bfloat16)
    lower = (values - upper.astype(jnp.float32)).astype(jnp.bfloat16)
    return upper, lower


def right_product(values, table):
    upper, lower = halves(values)
    return jnp.dot(jnp.concatenate([upper, lower, upper], axis=1), table, preferred_element_type=jnp.float32)


def left_product(table, values):
    upper, lower = halves(values)
    return jnp.dot(table, jnp.concatenate([upper, lower, upper], axis=0), preferred_element_type=jnp.float32)


def tile(index):
    return slice(index * lane, (index + 1) * lane)


def lines_kernel(field_ref, speed_ref, turn_ref, table_ref, out_ref, work_ref):
    step = pl.program_id(0)

    def rows(index, carry):
        here = pl.ds(pl.multiple_of(index * 8, 8), 8)
        parts = sixteen(
            [(field_ref[0, 0, here, tile(j)], field_ref[0, 1, here, tile(j)]) for j in range(radix)], -1
        )
        for k in range(radix):
            re, im = times(parts[k], (turn_ref[k, 0], turn_ref[k, 1]))
            work_ref[k, here, 0:lane] = re
            work_ref[k, here, lane : 2 * lane] = im
        return carry

    lax.fori_loop(0, row_block // 8, rows, 0)
    lines = right_product(work_ref[...].reshape(radix * row_block, 2 * lane), table_ref[...])
    half = row_block // 2
    begin = lax.axis_index("shot") * (lane // 2) + step * half
    speed_rows = pl.ds(pl.multiple_of(begin, 8), half)
    for k in range(radix):
        block = lines[k * row_block : (k + 1) * row_block]
        out_ref[k, 0, 0:row_block] = block[:, 0:lane]
        out_ref[k, 0, row_block : 2 * row_block] = block[:, lane : 2 * lane]
        out_ref[k, 0, 2 * row_block : piece] = speed_ref[0, speed_rows, tile(k)]


def lines_call(wavefield, velocity):
    return pl.pallas_call(
        lines_kernel,
        grid=(blocks,),
        in_specs=[
            pl.BlockSpec((1, 2, row_block, full), lambda g: (0, 0, g, 0)),
            pl.BlockSpec((1, lane, full), lambda g: (0, 0, 0)),
            pl.BlockSpec((radix, 2, 8, lane), lambda g: (0, 0, 0, 0)),
            pl.BlockSpec((6 * lane, 2 * lane), lambda g: (0, 0)),
        ],
        out_specs=pl.BlockSpec((radix, 1, piece, lane), lambda g: (0, g, 0, 0)),
        out_shape=jax.ShapeDtypeStruct((radix, blocks, piece, lane), jnp.float32),
        scratch_shapes=[pltpu.VMEM((radix, row_block, 2 * lane), jnp.float32)],
        compiler_params=pltpu.CompilerParams(vmem_limit_bytes=vmem_bytes),
        name="forward_lines",
    )(wavefield, velocity, lane_twiddle(-1, 1.0), right_table(-1))


def phase_kernel(angular_ref, out_ref):
    device = lax.axis_index("slab")
    scale = 2.0 * math.pi / full
    column = lax.broadcasted_iota(jnp.int32, (32, lane), 1) * radix + device
    second = jnp.minimum(column, full - column).astype(jnp.float32) * scale
    second = second * second
    row = lax.broadcasted_iota(jnp.int32, (32, lane), 0)
    squares = []
    for speed in ref_speeds:
        number = angular_ref[0] * np.float32(1.0 / np.float32(speed))
        squares.append(number * number)

    def chunk(index, carry):
        k = index // 4
        begin = pl.multiple_of((index % 4) * 32, 32)
        here = pl.ds(begin, 32)
        there = pl.ds(pl.multiple_of(k * lane, lane), lane)
        position = (row + begin) * radix + k
        first = jnp.minimum(position, full - position).astype(jnp.float32) * scale
        wave_square = first * first + second
        for j in range(len(ref_speeds)):
            vertical = squares[j] - wave_square
            root = jnp.sqrt(jnp.abs(vertical))
            moving = vertical >= 0.0
            out_ref[j, 0, here, there] = jnp.where(moving, horner(cos_series, vertical), jnp.exp(-root))
            out_ref[j, 1, here, there] = jnp.where(moving, root * horner(sinc_series, vertical), 0.0)
        return carry

    lax.fori_loop(0, radix * 4, chunk, 0)


def phase_call(frequencies):
    count = len(ref_speeds)
    return pl.pallas_call(
        phase_kernel,
        in_specs=[pl.BlockSpec(memory_space=pltpu.SMEM)],
        out_specs=pl.BlockSpec((count, 2, lane, full), lambda: (0, 0, 0, 0)),
        out_shape=jax.ShapeDtypeStruct((count, 2, lane, full), jnp.float32),
        compiler_params=pltpu.CompilerParams(vmem_limit_bytes=vmem_bytes),
        cost_estimate=pl.CostEstimate(flops=60 * count * lane * full, bytes_accessed=8 * count * lane * full, transcendentals=0),
        name="phase_factors",
    )(frequencies)


def rows_kernel(in_ref, phase_ref, ahead_ref, back_ref, ahead_table_ref, back_table_ref, out_ref, work_ref, spec_ref):
    @pl.when(pl.program_id(0) == 0)
    def _():
        def rows(index, carry):
            group = index // (row_block // 8)
            local = pl.multiple_of((index % (row_block // 8)) * 8, 8)
            here = pl.ds(pl.multiple_of(index * 8, 8), 8)
            there = pl.ds(pl.multiple_of(index * 8 + lane, 8), 8)
            parts = sixteen(
                [
                    (in_ref[s, group, pl.ds(local, 8), :], in_ref[s, group, pl.ds(local + row_block, 8), :])
                    for s in range(radix)
                ],
                -1,
            )
            for k in range(radix):
                re, im = times(parts[k], (ahead_ref[k, 0, here, :], ahead_ref[k, 1, here, :]))
                work_ref[here, tile(k)] = re
                work_ref[there, tile(k)] = im
            return carry

        lax.fori_loop(0, lane // 8, rows, 0)

        def pairs(index, carry):
            columns = pl.ds(pl.multiple_of(index * 2 * lane, 2 * lane), 2 * lane)
            spec_ref[:, columns] = left_product(ahead_table_ref[...], work_ref[:, columns])
            return carry

        lax.fori_loop(0, radix // 2, pairs, 0)

    def shifted(index, carry):
        columns = pl.ds(pl.multiple_of(index * 2 * lane, 2 * lane), 2 * lane)
        re, im = times(
            (spec_ref[0:lane, columns], spec_ref[lane : 2 * lane, columns]),
            (phase_ref[0, 0, :, columns], phase_ref[0, 1, :, columns]),
        )
        work_ref[:, columns] = left_product(back_table_ref[...], jnp.concatenate([re, im], axis=0))
        return carry

    lax.fori_loop(0, radix // 2, shifted, 0)

    def back(index, carry):
        here = pl.ds(pl.multiple_of(index * 8, 8), 8)
        there = pl.ds(pl.multiple_of(index * 8 + lane, 8), 8)
        parts = sixteen(
            [
                times(
                    (work_ref[here, tile(k)], work_ref[there, tile(k)]),
                    (back_ref[k, 0, here, :], back_ref[k, 1, here, :]),
                )
                for k in range(radix)
            ],
            1,
        )
        for s in range(radix):
            out_ref[s, 0, 0, here, :] = parts[s][0]
            out_ref[s, 0, 1, here, :] = parts[s][1]
        return carry

    lax.fori_loop(0, lane // 8, back, 0)


def rows_call(arrived, phase):
    count = len(ref_speeds)
    whole4 = lambda j: (0, 0, 0, 0)
    whole2 = lambda j: (0, 0)
    return pl.pallas_call(
        rows_kernel,
        grid=(count,),
        in_specs=[
            pl.BlockSpec((radix, blocks, piece, lane), whole4),
            pl.BlockSpec((1, 2, lane, full), lambda j: (j, 0, 0, 0)),
            pl.BlockSpec((radix, 2, lane, lane), whole4),
            pl.BlockSpec((radix, 2, lane, lane), whole4),
            pl.BlockSpec((2 * lane, 6 * lane), whole2),
            pl.BlockSpec((2 * lane, 6 * lane), whole2),
        ],
        out_specs=pl.BlockSpec((radix, 1, 2, lane, lane), lambda j: (0, j, 0, 0, 0)),
        out_shape=jax.ShapeDtypeStruct((radix, count, 2, lane, lane), jnp.float32),
        scratch_shapes=[
            pltpu.VMEM((2 * lane, full), jnp.float32),
            pltpu.VMEM((2 * lane, full), jnp.float32),
        ],
        compiler_params=pltpu.CompilerParams(vmem_limit_bytes=vmem_bytes),
        name="rows_there_and_back",
    )(
        arrived,
        phase,
        sublane_twiddle(-1, 1.0),
        sublane_twiddle(1, 1.0 / full),
        left_table(-1),
        left_table(1),
    )


def blend_kernel(angular_ref, own_ref, other_ref, bracket_ref, out_ref, tile_ref):
    shot = lax.axis_index("shot")
    half = row_block // 2
    for d in range(radix):
        for g in range(blocks):
            own = pl.ds(pl.multiple_of(shot * (lane // 2) + g * half, 8), half)
            other = pl.ds(pl.multiple_of((1 - shot) * (lane // 2) + g * half, 8), half)
            tile_ref[own, :] = own_ref[d, g]
            tile_ref[other, :] = other_ref[d, g]
        speed = jnp.transpose(tile_ref[...])
        lower = bracket_ref[0, :, tile(d)]
        first = lower == 0
        low = jnp.where(first, ref_speeds[0], ref_speeds[1])
        width = jnp.where(first, 1.0 / (ref_speeds[1] - ref_speeds[0]), 1.0 / (ref_speeds[2] - ref_speeds[1]))
        fraction = (speed - low) * width
        low_slowness = jnp.where(first, 1.0 / ref_speeds[0], 1.0 / ref_speeds[1])
        high_slowness = jnp.where(first, 1.0 / ref_speeds[1], 1.0 / ref_speeds[2])
        residual = 1.0 / speed - ((1.0 - fraction) * low_slowness + fraction * high_slowness)
        angle = angular_ref[0] * step_length * residual
        square = angle * angle
        cosine = horner([1.0, -1 / 2, 1 / 24, -1 / 720, 1 / 40320], square)
        sine = angle * horner([1.0, -1 / 6, 1 / 120, -1 / 5040, 1 / 362880], square)
        out_ref[0, :, tile(d)] = fraction + jnp.where(first, 0.0, 1.0)
        out_ref[1, :, tile(d)] = cosine
        out_ref[2, :, tile(d)] = sine


def blend_call(frequencies, own, other, bracket):
    return pl.pallas_call(
        blend_kernel,
        in_specs=[
            pl.BlockSpec(memory_space=pltpu.SMEM),
            pl.BlockSpec((radix, blocks, row_block // 2, lane), lambda: (0, 0, 0, 0)),
            pl.BlockSpec((radix, blocks, row_block // 2, lane), lambda: (0, 0, 0, 0)),
            pl.BlockSpec((1, lane, full), lambda: (0, 0, 0)),
        ],
        out_specs=pl.BlockSpec((3, lane, full), lambda: (0, 0, 0)),
        out_shape=jax.ShapeDtypeStruct((3, lane, full), jnp.float32),
        scratch_shapes=[pltpu.VMEM((lane, lane), jnp.float32)],
        compiler_params=pltpu.CompilerParams(vmem_limit_bytes=vmem_bytes),
        cost_estimate=pl.CostEstimate(flops=60 * lane * full, bytes_accessed=24 * lane * full, transcendentals=0),
        name="blend_factors",
    )(frequencies, own, other, bracket)


def finish_kernel(in_ref, blend_ref, turn_ref, table_ref, out_ref, image_ref, work_ref, wave_ref):
    count = len(ref_speeds)
    for j in range(count):
        values = jnp.concatenate([in_ref[:, j, 0], in_ref[:, j, 1]], axis=2)
        product = right_product(values.reshape(radix * row_block, 2 * lane), table_ref[...])
        work_ref[j] = product.reshape(radix, row_block, 2 * lane)

    def rows(index, carry):
        here = pl.ds(pl.multiple_of(index * 8, 8), 8)
        for j in range(count):
            parts = sixteen(
                [
                    times(
                        (work_ref[j, k, here, 0:lane], work_ref[j, k, here, lane : 2 * lane]),
                        (turn_ref[k, 0], turn_ref[k, 1]),
                    )
                    for k in range(radix)
                ],
                1,
            )
            for s in range(radix):
                wave_ref[j, 0, :, tile(s)] = parts[s][0]
                wave_ref[j, 1, :, tile(s)] = parts[s][1]
        for s in range(radix):
            place = blend_ref[0, here, tile(s)]
            weights_now = (
                jnp.maximum(1.0 - place, 0.0),
                1.0 - jnp.abs(place - 1.0),
                jnp.maximum(place - 1.0, 0.0),
            )
            mixed = [
                sum(weights_now[j] * wave_ref[j, part, :, tile(s)] for j in range(count)) for part in range(2)
            ]
            re, im = times(mixed, (blend_ref[1, here, tile(s)], blend_ref[2, here, tile(s)]))
            out_ref[0, 0, here, tile(s)] = re
            out_ref[0, 1, here, tile(s)] = im
            image_ref[0, here, tile(s)] = re
        return carry

    lax.fori_loop(0, row_block // 8, rows, 0)


def finish_call(returned, blend):
    count = len(ref_speeds)
    return pl.pallas_call(
        finish_kernel,
        grid=(blocks,),
        in_specs=[
            pl.BlockSpec((radix, count, 2, row_block, lane), lambda g: (0, 0, 0, g, 0)),
            pl.BlockSpec((3, row_block, full), lambda g: (0, g, 0)),
            pl.BlockSpec((radix, 2, 8, lane), lambda g: (0, 0, 0, 0)),
            pl.BlockSpec((6 * lane, 2 * lane), lambda g: (0, 0)),
        ],
        out_specs=[
            pl.BlockSpec((1, 2, row_block, full), lambda g: (0, 0, g, 0)),
            pl.BlockSpec((1, row_block, full), lambda g: (0, g, 0)),
        ],
        out_shape=[
            jax.ShapeDtypeStruct((1, 2, lane, full), jnp.float32),
            jax.ShapeDtypeStruct((1, lane, full), jnp.float32),
        ],
        scratch_shapes=[
            pltpu.VMEM((count, radix, row_block, 2 * lane), jnp.float32),
            pltpu.VMEM((count, 2, 8, full), jnp.float32),
        ],
        compiler_params=pltpu.CompilerParams(vmem_limit_bytes=vmem_bytes),
        name="inverse_lines",
    )(returned, blend, lane_twiddle(1, 1.0 / full), right_table(1))


def exchange(values):
    return lax.all_to_all(values, "slab", split_axis=0, concat_axis=0, tiled=True)


def per_device(wavefield, frequencies, velocity, bracket):
    sent = lines_call(wavefield, velocity)
    phase = phase_call(frequencies)
    arrived = exchange(sent)
    own = arrived[:, :, 2 * row_block :, :]
    other = lax.ppermute(own, "shot", [(0, 1), (1, 0)])
    returned = exchange(rows_call(arrived, phase))
    blend = blend_call(frequencies, own, other, bracket)
    propagated, image = finish_call(returned, blend)
    return propagated, image


def fits(mesh, shapes):
    wavefield, velocity = shapes
    return (
        mesh.shape["slab"] == radix
        and mesh.shape["shot"] == 2
        and wavefield == (2, 2, full, full)
        and velocity == (1, full, full)
    )


def solution(mesh):
    def program(wavefield, frequencies, velocity, bracket):
        small = fits(mesh, (wavefield.shape, velocity.shape))
        return jax.shard_map(
            per_device if small else per_device_general,
            mesh=mesh,
            in_specs=(
                P("shot", None, "slab", None),
                P("shot"),
                P(None, "slab", None),
                P(None, "slab", None),
            ),
            out_specs=(P("shot", None, "slab", None), P("shot", "slab", None)),
            check_vma=False,
        )(wavefield, frequencies, velocity, bracket)

    return program
```

profile of v0, /device:TPU:13, one launch (start us, length us, event | category | flops | bytes accessed | tf_op | source)
XLA Modules:
  0.0 242.6 jit_solution(8954101756813571109)
XLA Ops:
  0.6 5.4 %forward_lines.1 = f32[16,4,80,128]{3,2,1,0:T(8,128)} custom-call(f32[1,2,128,2048]{3,2,1,0:T(8,128)} %field_ref.1, f32[1,128,2048]{2,1,0:T(8,128)} %speed_ref.1, f32[16,2,8,128]{3,2,1,0:T(8,128)} %constant.16.clone.turn_ref, bf16[768,256]{1,0:T(8,128)(2,1)} %constant.17.clone.table_ref), custom_call_target="tpu_custom_call" | custom-call | tf_op jit(solution)/shard_map/forward_lines/pallas_call | solution.py:385
  6.1 6.6 %all-to-all-start = ((f32[16,4,80,128]{3,2,1,0:T(8,128)}), f32[16,4,80,128]{3,2,1,0:T(8,128)S(1)}, u32[]{:S(2)}, u32[]{:S(2)}) async-start(f32[16,4,80,128]{3,2,1,0:T(8,128)} %forward_lines.1), calls=%async_computation | async-start | bytes 5242880 | tf_op jit(solution)/shard_map/all_to_all | solution.py:657
  13.3 8.4 %phase_factors.1.phase_ref = f32[3,2,128,2048]{3,2,1,0:T(8,128)} custom-call(f32[1]{0:T(128)S(6)} %copy.14.angular_ref), custom_call_target="tpu_custom_call" | custom-call | flops 47185920 | bytes 6291456 | tf_op jit(solution)/shard_map/phase_factors/pallas_call | solution.py:435
  21.6 49.6 %all-to-all-done.in_ref = f32[16,4,80,128]{3,2,1,0:T(8,128)S(1)} async-done(((f32[16,4,80,128]{3,2,1,0:T(8,128)}), f32[16,4,80,128]{3,2,1,0:T(8,128)S(1)}, u32[]{:S(2)}, u32[]{:S(2)}) %all-to-all-start) | async-done | bytes 2621472 | tf_op jit(solution)/shard_map/all_to_all | solution.py:657
  71.3 0.0 copy-start
  71.3 1.5 copy-done
  72.8 18.4 %rows_there_and_back.1 = f32[16,3,2,128,128]{4,3,2,1,0:T(8,128)} custom-call(f32[16,4,80,128]{3,2,1,0:T(8,128)} %copy-done, f32[3,2,128,2048]{3,2,1,0:T(8,128)} %phase_factors.1.phase_ref, f32[16,2,128,128]{3,2,1,0:T(8,128)} %constant.18.clone.ahead_ref, f32[16,2,128,128]{3,2,1,0:T(8,128)} %constant.19.clone.back_ref, ...), custom_call_target="tpu_custom_call" | custom-call | tf_op jit(solution)/shard_map/rows_there_and_back/pallas_call | solution.py:512
  91.1 4.9 %all-to-all-start.1 = ((f32[16,3,2,128,128]{4,3,2,1,0:T(8,128)}), f32[16,3,2,128,128]{4,3,2,1,0:T(8,128)}, u32[]{:S(2)}, u32[]{:S(2)}) async-start(f32[16,3,2,128,128]{4,3,2,1,0:T(8,128)} %rows_there_and_back.1), calls=%async_computation.1 | async-start | bytes 12582912 | tf_op jit(solution)/shard_map/all_to_all | solution.py:657
  96.0 1.1 slice.4.own_ref
  97.1 0.0 copy-start.1
  97.1 1.3 collective-permute-start
  98.4 12.0 %collective-permute-done.other_ref = f32[16,4,16,128]{3,2,1,0:T(8,128)S(1)} collective-permute-done((f32[16,4,16,128]{3,2,1,0:T(8,128)S(1)}, f32[16,4,16,128]{3,2,1,0:T(8,128)S(1)}, u32[]{:S(2)}, u32[]{:S(2)}) %collective-permute-start) | collective-permute-done | bytes 524320 | tf_op jit(solution)/shard_map/ppermute | solution.py:665
  110.5 0.0 copy-done.1
  110.5 0.0 copy-start.2
  110.5 0.8 copy-done.2
  111.3 4.5 %blend_factors.1.blend_ref = f32[3,128,2048]{2,1,0:T(8,128)} custom-call(f32[1]{0:T(128)S(6)} %copy.14.angular_ref, f32[16,4,16,128]{3,2,1,0:T(8,128)} %copy-done.1, f32[16,4,16,128]{3,2,1,0:T(8,128)} %copy-done.2, s32[1,128,2048]{2,1,0:T(8,128)} %bracket_ref.1), custom_call_target="tpu_custom_call" | custom-call | flops 15728640 | bytes 6291456 | tf_op jit(solution)/shard_map/blend_factors/pallas_call | solution.py:569
  115.7 117.7 %all-to-all-done.1.in_ref = f32[16,3,2,128,128]{4,3,2,1,0:T(8,128)} async-done(((f32[16,3,2,128,128]{4,3,2,1,0:T(8,128)}), f32[16,3,2,128,128]{4,3,2,1,0:T(8,128)}, u32[]{:S(2)}, u32[]{:S(2)}) %all-to-all-start.1) | async-done | bytes 6291488 | tf_op jit(solution)/shard_map/all_to_all | solution.py:657
  233.4 9.2 %inverse_lines.1 = (f32[1,2,128,2048]{3,2,1,0:T(8,128)}, f32[1,128,2048]{2,1,0:T(8,128)}) custom-call(f32[16,3,2,128,128]{4,3,2,1,0:T(8,128)} %all-to-all-done.1.in_ref, f32[3,128,2048]{2,1,0:T(8,128)} %blend_factors.1.blend_ref, f32[16,2,8,128]{3,2,1,0:T(8,128)} %constant.22.clone.turn_ref, bf16[768,256]{1,0:T(8,128)(2,1)} %constant.23.clone.table_ref), custom_call_target="tpu_custom_call" | custom-call | tf_op jit(solution)/shard_map/inverse_lines/pallas_call | solution.py:630
Async XLA Ops:
  6.1 65.2 %all-to-all-start = ((f32[16,4,80,128]{3,2,1,0:T(8,128)}), f32[16,4,80,128]{3,2,1,0:T(8,128)S(1)}, u32[]{:S(2)}, u32[]{:S(2)}) async-start(f32[16,4,80,128]{3,2,1,0:T(8,128)} %forward_lines.1), calls=%async_computation | async-start | bytes 5242880 | tf_op jit(solution)/shard_map/all_to_all | solution.py:657
  71.3 1.5 copy-start
  91.1 142.3 %all-to-all-start.1 = ((f32[16,3,2,128,128]{4,3,2,1,0:T(8,128)}), f32[16,3,2,128,128]{4,3,2,1,0:T(8,128)}, u32[]{:S(2)}, u32[]{:S(2)}) async-start(f32[16,3,2,128,128]{4,3,2,1,0:T(8,128)} %rows_there_and_back.1), calls=%async_computation.1 | async-start | bytes 12582912 | tf_op jit(solution)/shard_map/all_to_all | solution.py:657
  97.1 13.3 %copy-start.1 = (f32[16,4,16,128]{3,2,1,0:T(8,128)}, f32[16,4,16,128]{3,2,1,0:T(8,128)S(1)}, u32[]{:S(2)}) copy-start(f32[16,4,16,128]{3,2,1,0:T(8,128)S(1)} %slice.4.own_ref) | copy-start | bytes 1572868
  97.1 13.3 %collective-permute-start = (f32[16,4,16,128]{3,2,1,0:T(8,128)S(1)}, f32[16,4,16,128]{3,2,1,0:T(8,128)S(1)}, u32[]{:S(2)}, u32[]{:S(2)}) collective-permute-start(f32[16,4,16,128]{3,2,1,0:T(8,128)S(1)} %slice.4.own_ref), channel_id=1, source_target_pairs={{0,16},{16,0},{1,17},{17,1},{2,18},{18,2},{3,19},{19,3},{4,20},{20... | collective-permute-start | bytes 1572872 | tf_op jit(solution)/shard_map/ppermute | solution.py:665
  110.5 0.8 copy-start.2
where the time goes:
time: 243 us
  waiting for transfers between devices  179 us (74%)
  Pallas kernels  45.9 us (19%)
  starting transfers between devices  12.7 us (5%)
  local copies, waits for them, and re-layouts  3.38 us (1%)
    all_to_all x2, waiting for transfers between devices, exchange(): lax.all_to_all(values, 'slab', split_axis=0, concat_axis=0, tiled=True)  167 us
    pallas_call x1, Pallas kernels, rows_call(): pl.pallas_call(rows_kernel, grid=(count,), in_specs=[pl.BlockSpec((radix,...  18.4 us
    ppermute x1, waiting for transfers between devices, per_device(): other = lax.ppermute(own, 'shot', [(0, 1), (1, 0)])  12 us
    all_to_all x2, starting transfers between devices, exchange(): lax.all_to_all(values, 'slab', split_axis=0, concat_axis=0, tiled=True)  11.5 us
    pallas_call x1, Pallas kernels, finish_call(): pl.pallas_call(finish_kernel, grid=(blocks,), in_specs=[pl.BlockSpec((rad...  9.21 us
    pallas_call x1, Pallas kernels, phase_call(): pl.pallas_call(phase_kernel, in_specs=[pl.BlockSpec(memory_space=pltpu.SM...  8.37 us
    pallas_call x1, Pallas kernels, lines_call(): pl.pallas_call(lines_kernel, grid=(blocks,), in_specs=[pl.BlockSpec((1, 2...  5.44 us
  transfers between devices with their start and end apart: 3, of which 3 were waited for; matrix products, arithmetic and copies ran while one was open for 0% of the time, Pallas kernels for 5%

commit v1 on v0

--- a/solution.py
+++ b/solution.py
@@ -232,6 +232,7 @@
 blocks = lane // row_block
 piece = 2 * row_block + row_block // 2
 vmem_bytes = 56 * 1024 * 1024
+rows_vmem_bytes = 50 * 1024 * 1024
 
 
 def split_table(table):
@@ -251,8 +252,8 @@
     return np.concatenate([upper, upper, lower], axis=0)
 
 
-def left_table(direction):
-    upper, lower = split_table(line_matrices(direction).T)
+def left_table(direction, scale):
+    upper, lower = split_table(line_matrices(direction).T * scale)
     return np.concatenate([upper, upper, lower], axis=1)
 
 
@@ -266,9 +267,10 @@
     return np.ascontiguousarray(np.broadcast_to(table, (radix, 2, 8, lane))).astype(np.float32)
 
 
-def sublane_twiddle(direction, scale):
-    table = twiddle(direction, scale)[:, :, :, None]
-    return np.ascontiguousarray(np.broadcast_to(table, (radix, 2, lane, lane))).astype(np.float32)
+def column_twiddle(direction):
+    table = np.zeros((lane, lane), np.float32)
+    table[:, : 2 * radix] = twiddle(direction, 1.0).reshape(2 * radix, lane).T
+    return table
 
 
 def root_series(offset, degree):
@@ -291,6 +293,10 @@
 
 def times(left, right):
     return left[0] * right[0] - left[1] * right[1], left[0] * right[1] + left[1] * right[0]
+
+
+def conjugate_times(left, right):
+    return left[0] * right[0] + left[1] * right[1], left[1] * right[0] - left[0] * right[1]
 
 
 def quarter(values, direction):
@@ -443,99 +449,116 @@
     )(frequencies)
 
 
-def rows_kernel(in_ref, phase_ref, ahead_ref, back_ref, ahead_table_ref, back_table_ref, out_ref, work_ref, spec_ref):
-    @pl.when(pl.program_id(0) == 0)
-    def _():
-        def rows(index, carry):
-            group = index // (row_block // 8)
-            local = pl.multiple_of((index % (row_block // 8)) * 8, 8)
+def rows_kernel(
+    in_ref, phase_ref, column_ref, ahead_table_ref, back_table_ref, out_ref,
+    work_ref, spec_ref, turn_ref, factor_ref, field_ref, factor_sem, field_sem,
+):
+    count = len(ref_speeds)
+
+    def factor_copy(j):
+        return pltpu.make_async_copy(phase_ref.at[j], factor_ref.at[j], factor_sem.at[j])
+
+    def field_copy(j):
+        return pltpu.make_async_copy(field_ref.at[j % 2], out_ref.at[:, j], field_sem.at[j % 2])
+
+    for j in range(count):
+        factor_copy(j).start()
+
+    def rows(index, carry):
+        group = index // (row_block // 8)
+        local = pl.multiple_of((index % (row_block // 8)) * 8, 8)
+        here = pl.ds(pl.multiple_of(index * 8, 8), 8)
+        there = pl.ds(pl.multiple_of(index * 8 + lane, 8), 8)
+        columns = column_ref[here, :]
+        parts = sixteen(
+            [
+                (in_ref[s, group, pl.ds(local, 8), :], in_ref[s, group, pl.ds(local + row_block, 8), :])
+                for s in range(radix)
+            ],
+            -1,
+        )
+        for k in range(radix):
+            turn = tuple(
+                jnp.broadcast_to(columns[:, 2 * k + part : 2 * k + part + 1], (8, lane)) for part in range(2)
+            )
+            turn_ref[k, 0, here, :] = turn[0]
+            turn_ref[k, 1, here, :] = turn[1]
+            re, im = times(parts[k], turn)
+            work_ref[here, tile(k)] = re
+            work_ref[there, tile(k)] = im
+        return carry
+
+    lax.fori_loop(0, lane // 8, rows, 0)
+
+    def pairs(index, carry):
+        columns = pl.ds(pl.multiple_of(index * 2 * lane, 2 * lane), 2 * lane)
+        spec_ref[:, columns] = left_product(ahead_table_ref[...], work_ref[:, columns])
+        return carry
+
+    lax.fori_loop(0, radix // 2, pairs, 0, unroll=True)
+
+    for j in range(count):
+        factor_copy(j).wait()
+
+        def shifted(index, carry):
+            columns = pl.ds(pl.multiple_of(index * 2 * lane, 2 * lane), 2 * lane)
+            re, im = times(
+                (spec_ref[0:lane, columns], spec_ref[lane : 2 * lane, columns]),
+                (factor_ref[j, 0, :, columns], factor_ref[j, 1, :, columns]),
+            )
+            work_ref[:, columns] = left_product(back_table_ref[...], jnp.concatenate([re, im], axis=0))
+            return carry
+
+        lax.fori_loop(0, radix // 2, shifted, 0, unroll=True)
+        if j >= 2:
+            field_copy(j - 2).wait()
+
+        def back(index, carry):
             here = pl.ds(pl.multiple_of(index * 8, 8), 8)
             there = pl.ds(pl.multiple_of(index * 8 + lane, 8), 8)
             parts = sixteen(
                 [
-                    (in_ref[s, group, pl.ds(local, 8), :], in_ref[s, group, pl.ds(local + row_block, 8), :])
-                    for s in range(radix)
+                    conjugate_times(
+                        (work_ref[here, tile(k)], work_ref[there, tile(k)]),
+                        (turn_ref[k, 0, here, :], turn_ref[k, 1, here, :]),
+                    )
+                    for k in range(radix)
                 ],
-                -1,
+                1,
             )
-            for k in range(radix):
-                re, im = times(parts[k], (ahead_ref[k, 0, here, :], ahead_ref[k, 1, here, :]))
-                work_ref[here, tile(k)] = re
-                work_ref[there, tile(k)] = im
+            for s in range(radix):
+                field_ref[j % 2, s, 0, here, :] = parts[s][0]
+                field_ref[j % 2, s, 1, here, :] = parts[s][1]
             return carry
 
-        lax.fori_loop(0, lane // 8, rows, 0)
-
-        def pairs(index, carry):
-            columns = pl.ds(pl.multiple_of(index * 2 * lane, 2 * lane), 2 * lane)
-            spec_ref[:, columns] = left_product(ahead_table_ref[...], work_ref[:, columns])
-            return carry
-
-        lax.fori_loop(0, radix // 2, pairs, 0)
-
-    def shifted(index, carry):
-        columns = pl.ds(pl.multiple_of(index * 2 * lane, 2 * lane), 2 * lane)
-        re, im = times(
-            (spec_ref[0:lane, columns], spec_ref[lane : 2 * lane, columns]),
-            (phase_ref[0, 0, :, columns], phase_ref[0, 1, :, columns]),
-        )
-        work_ref[:, columns] = left_product(back_table_ref[...], jnp.concatenate([re, im], axis=0))
-        return carry
-
-    lax.fori_loop(0, radix // 2, shifted, 0)
-
-    def back(index, carry):
-        here = pl.ds(pl.multiple_of(index * 8, 8), 8)
-        there = pl.ds(pl.multiple_of(index * 8 + lane, 8), 8)
-        parts = sixteen(
-            [
-                times(
-                    (work_ref[here, tile(k)], work_ref[there, tile(k)]),
-                    (back_ref[k, 0, here, :], back_ref[k, 1, here, :]),
-                )
-                for k in range(radix)
-            ],
-            1,
-        )
-        for s in range(radix):
-            out_ref[s, 0, 0, here, :] = parts[s][0]
-            out_ref[s, 0, 1, here, :] = parts[s][1]
-        return carry
-
-    lax.fori_loop(0, lane // 8, back, 0)
+        lax.fori_loop(0, lane // 8, back, 0)
+        field_copy(j).start()
+
+    for j in range(count - 2, count):
+        field_copy(j).wait()
 
 
 def rows_call(arrived, phase):
     count = len(ref_speeds)
-    whole4 = lambda j: (0, 0, 0, 0)
-    whole2 = lambda j: (0, 0)
+    in_vmem = pl.BlockSpec(memory_space=pltpu.VMEM)
+    in_hbm = pl.BlockSpec(memory_space=pltpu.HBM)
     return pl.pallas_call(
         rows_kernel,
-        grid=(count,),
-        in_specs=[
-            pl.BlockSpec((radix, blocks, piece, lane), whole4),
-            pl.BlockSpec((1, 2, lane, full), lambda j: (j, 0, 0, 0)),
-            pl.BlockSpec((radix, 2, lane, lane), whole4),
-            pl.BlockSpec((radix, 2, lane, lane), whole4),
-            pl.BlockSpec((2 * lane, 6 * lane), whole2),
-            pl.BlockSpec((2 * lane, 6 * lane), whole2),
-        ],
-        out_specs=pl.BlockSpec((radix, 1, 2, lane, lane), lambda j: (0, j, 0, 0, 0)),
+        in_specs=[in_vmem, in_hbm, in_vmem, in_vmem, in_vmem],
+        out_specs=in_hbm,
         out_shape=jax.ShapeDtypeStruct((radix, count, 2, lane, lane), jnp.float32),
         scratch_shapes=[
             pltpu.VMEM((2 * lane, full), jnp.float32),
             pltpu.VMEM((2 * lane, full), jnp.float32),
+            pltpu.VMEM((radix, 2, lane, lane), jnp.float32),
+            pltpu.VMEM((count, 2, lane, full), jnp.float32),
+            pltpu.VMEM((2, radix, 2, lane, lane), jnp.float32),
+            pltpu.SemaphoreType.DMA((count,)),
+            pltpu.SemaphoreType.DMA((2,)),
         ],
-        compiler_params=pltpu.CompilerParams(vmem_limit_bytes=vmem_bytes),
+        compiler_params=pltpu.CompilerParams(vmem_limit_bytes=rows_vmem_bytes),
         name="rows_there_and_back",
-    )(
-        arrived,
-        phase,
-        sublane_twiddle(-1, 1.0),
-        sublane_twiddle(1, 1.0 / full),
-        left_table(-1),
-        left_table(1),
-    )
+    )(arrived, phase, column_twiddle(-1), left_table(-1, 1.0), left_table(1, 1.0 / full))
 
 
 def blend_kernel(angular_ref, own_ref, other_ref, bracket_ref, out_ref, tile_ref):

time: 243 us -> 234 us (0.963)
  Pallas kernels: 45.9 us -> 38.1 us
  local copies, waits for them, and re-layouts: 3.38 us -> 0.85 us
    pallas_call x1, Pallas kernels: 18.4 us -> 10.6 us  [rows_call(): pl.pallas_call(rows_kernel, in_specs=[in_vmem, in_hbm, in_vmem, in_vmem,...]
  transfers between devices with their start and end apart: 3 -> 3, of which waited for: 3 -> 3; matrix products, arithmetic and copies ran while one was open for 0% -> 0% of each run, Pallas kernels for 5% -> 6%
where the time goes in v1:
time: 234 us; the launch traced here: 233 us
  waiting for transfers between devices  180 us (77%)
  Pallas kernels  38.1 us (16%)
  starting transfers between devices  12.8 us (5%)
    all_to_all x2, waiting for transfers between devices, exchange(): lax.all_to_all(values, 'slab', split_axis=0, concat_axis=0, tiled=True)  168 us
    ppermute x1, waiting for transfers between devices, per_device(): other = lax.ppermute(own, 'shot', [(0, 1), (1, 0)])  12 us
    all_to_all x2, starting transfers between devices, exchange(): lax.all_to_all(values, 'slab', split_axis=0, concat_axis=0, tiled=True)  11.5 us
    pallas_call x1, Pallas kernels, rows_call(): pl.pallas_call(rows_kernel, in_specs=[in_vmem, in_hbm, in_vmem, in_vmem,...  10.6 us
    pallas_call x1, Pallas kernels, finish_call(): pl.pallas_call(finish_kernel, grid=(blocks,), in_specs=[pl.BlockSpec((rad...  9.2 us
    pallas_call x1, Pallas kernels, phase_call(): pl.pallas_call(phase_kernel, in_specs=[pl.BlockSpec(memory_space=pltpu.SM...  8.38 us
    pallas_call x1, Pallas kernels, lines_call(): pl.pallas_call(lines_kernel, grid=(blocks,), in_specs=[pl.BlockSpec((1, 2...  5.42 us
  transfers between devices with their start and end apart: 3, of which 3 were waited for; matrix products, arithmetic and copies ran while one was open for 0% of the time, Pallas kernels for 6%

profile of v1, /device:TPU:13, one launch (start us, length us, event | category | flops | bytes accessed | tf_op | source)
XLA Modules:
  0.0 233.4 jit_solution(12757477207640556033)
XLA Ops:
  0.6 5.4 %forward_lines.1 = f32[16,4,80,128]{3,2,1,0:T(8,128)} custom-call(f32[1,2,128,2048]{3,2,1,0:T(8,128)} %field_ref.1, f32[1,128,2048]{2,1,0:T(8,128)} %speed_ref.1, f32[16,2,8,128]{3,2,1,0:T(8,128)} %constant.14.clone.turn_ref, bf16[768,256]{1,0:T(8,128)(2,1)} %constant.15.clone.table_ref), custom_call_target="tpu_custom_call" | custom-call | tf_op jit(solution)/shard_map/forward_lines/pallas_call | solution.py:391
  6.0 6.6 %all-to-all-start = ((f32[16,4,80,128]{3,2,1,0:T(8,128)}), f32[16,4,80,128]{3,2,1,0:T(8,128)S(1)}, u32[]{:S(2)}, u32[]{:S(2)}) async-start(f32[16,4,80,128]{3,2,1,0:T(8,128)} %forward_lines.1), calls=%async_computation | async-start | bytes 5242880 | tf_op jit(solution)/shard_map/all_to_all | solution.py:680
  13.3 0.0 copy-start
  13.3 0.0 copy-start.1
  13.3 0.0 copy-start.2
  13.3 8.4 %phase_factors.1.phase_ref = f32[3,2,128,2048]{3,2,1,0:T(8,128)} custom-call(f32[1]{0:T(128)S(6)} %copy.13.angular_ref), custom_call_target="tpu_custom_call" | custom-call | flops 47185920 | bytes 6291456 | tf_op jit(solution)/shard_map/phase_factors/pallas_call | solution.py:441
  21.7 49.6 %all-to-all-done.in_ref = f32[16,4,80,128]{3,2,1,0:T(8,128)S(1)} async-done(((f32[16,4,80,128]{3,2,1,0:T(8,128)}), f32[16,4,80,128]{3,2,1,0:T(8,128)S(1)}, u32[]{:S(2)}, u32[]{:S(2)}) %all-to-all-start) | async-done | bytes 2621472 | tf_op jit(solution)/shard_map/all_to_all | solution.py:680
  71.3 0.0 copy-done
  71.3 0.0 copy-done.1
  71.3 0.0 copy-done.2
  71.3 10.6 %rows_there_and_back.1 = f32[16,3,2,128,128]{4,3,2,1,0:T(8,128)} custom-call(f32[16,4,80,128]{3,2,1,0:T(8,128)S(1)} %all-to-all-done.in_ref, f32[3,2,128,2048]{3,2,1,0:T(8,128)} %phase_factors.1.phase_ref, f32[128,128]{1,0:T(8,128)S(1)} %copy-done.2, bf16[256,768]{1,0:T(8,128)(2,1)S(1)} %copy-done, bf16[256,768]{1,0:T(8,128)(2,1)S(1)} %copy-done.1), custom_call_target="tpu_custom_call" | custom-call | tf_op jit(solution)/shard_map/rows_there_and_back/pallas_call | solution.py:545
  81.9 4.9 %all-to-all-start.1 = ((f32[16,3,2,128,128]{4,3,2,1,0:T(8,128)}), f32[16,3,2,128,128]{4,3,2,1,0:T(8,128)}, u32[]{:S(2)}, u32[]{:S(2)}) async-start(f32[16,3,2,128,128]{4,3,2,1,0:T(8,128)} %rows_there_and_back.1), calls=%async_computation.1 | async-start | bytes 12582912 | tf_op jit(solution)/shard_map/all_to_all | solution.py:680
  86.9 0.0 copy-start.3
  86.9 1.3 collective-permute-start
  88.2 12.0 %collective-permute-done.other_ref = f32[16,4,16,128]{3,2,1,0:T(8,128)S(1)} collective-permute-done((f32[16,4,16,128]{3,2,1,0:T(8,128)S(1)}, f32[16,4,16,128]{3,2,1,0:T(8,128)S(1)}, u32[]{:S(2)}, u32[]{:S(2)}) %collective-permute-start) | collective-permute-done | bytes 524320 | tf_op jit(solution)/shard_map/ppermute | solution.py:688
  100.2 0.0 copy-done.3
  100.2 0.0 copy-start.4
  100.2 0.8 copy-done.4
  101.0 4.5 %blend_factors.1.blend_ref = f32[3,128,2048]{2,1,0:T(8,128)} custom-call(f32[1]{0:T(128)S(6)} %copy.13.angular_ref, f32[16,4,16,128]{3,2,1,0:T(8,128)} %copy-done.3, f32[16,4,16,128]{3,2,1,0:T(8,128)} %copy-done.4, s32[1,128,2048]{2,1,0:T(8,128)} %bracket_ref.1), custom_call_target="tpu_custom_call" | custom-call | flops 15728640 | bytes 6291456 | tf_op jit(solution)/shard_map/blend_factors/pallas_call | solution.py:592
  105.5 118.8 %all-to-all-done.1.in_ref = f32[16,3,2,128,128]{4,3,2,1,0:T(8,128)} async-done(((f32[16,3,2,128,128]{4,3,2,1,0:T(8,128)}), f32[16,3,2,128,128]{4,3,2,1,0:T(8,128)}, u32[]{:S(2)}, u32[]{:S(2)}) %all-to-all-start.1) | async-done | bytes 6291488 | tf_op jit(solution)/shard_map/all_to_all | solution.py:680
  224.2 9.2 %inverse_lines.1 = (f32[1,2,128,2048]{3,2,1,0:T(8,128)}, f32[1,128,2048]{2,1,0:T(8,128)}) custom-call(f32[16,3,2,128,128]{4,3,2,1,0:T(8,128)} %all-to-all-done.1.in_ref, f32[3,128,2048]{2,1,0:T(8,128)} %blend_factors.1.blend_ref, f32[16,2,8,128]{3,2,1,0:T(8,128)} %constant.19.clone.turn_ref, bf16[768,256]{1,0:T(8,128)(2,1)} %constant.20.clone.table_ref), custom_call_target="tpu_custom_call" | custom-call | tf_op jit(solution)/shard_map/inverse_lines/pallas_call | solution.py:653
  (1 shorter events, 0.0 us)
Async XLA Ops:
  6.0 65.2 %all-to-all-start = ((f32[16,4,80,128]{3,2,1,0:T(8,128)}), f32[16,4,80,128]{3,2,1,0:T(8,128)S(1)}, u32[]{:S(2)}, u32[]{:S(2)}) async-start(f32[16,4,80,128]{3,2,1,0:T(8,128)} %forward_lines.1), calls=%async_computation | async-start | bytes 5242880 | tf_op jit(solution)/shard_map/all_to_all | solution.py:680
  13.3 58.0 %copy-start = (bf16[256,768]{1,0:T(8,128)(2,1)S(1)}, bf16[256,768]{1,0:T(8,128)(2,1)}, u32[]{:S(2)}) copy-start(bf16[256,768]{1,0:T(8,128)(2,1)} %constant.17.clone.ahead_table_ref) | copy-start | bytes 1179652
  13.3 58.0 %copy-start.1 = (bf16[256,768]{1,0:T(8,128)(2,1)S(1)}, bf16[256,768]{1,0:T(8,128)(2,1)}, u32[]{:S(2)}) copy-start(bf16[256,768]{1,0:T(8,128)(2,1)} %constant.18.clone.back_table_ref) | copy-start | bytes 1179652
  13.3 58.0 %copy-start.2 = (f32[128,128]{1,0:T(8,128)S(1)}, f32[128,128]{1,0:T(8,128)}, u32[]{:S(2)}) copy-start(f32[128,128]{1,0:T(8,128)} %constant.16.clone.column_ref) | copy-start | bytes 196612
  81.9 142.3 %all-to-all-start.1 = ((f32[16,3,2,128,128]{4,3,2,1,0:T(8,128)}), f32[16,3,2,128,128]{4,3,2,1,0:T(8,128)}, u32[]{:S(2)}, u32[]{:S(2)}) async-start(f32[16,3,2,128,128]{4,3,2,1,0:T(8,128)} %rows_there_and_back.1), calls=%async_computation.1 | async-start | bytes 12582912 | tf_op jit(solution)/shard_map/all_to_all | solution.py:680
  86.9 13.3 %copy-start.3 = (f32[16,4,16,128]{3,2,1,0:T(8,128)}, f32[16,4,16,128]{3,2,1,0:T(8,128)S(1)}, u32[]{:S(2)}) copy-start(f32[16,4,16,128]{3,2,1,0:T(8,128)S(1)} %slice.4.own_ref) | copy-start | bytes 1572868
  86.9 13.3 %collective-permute-start = (f32[16,4,16,128]{3,2,1,0:T(8,128)S(1)}, f32[16,4,16,128]{3,2,1,0:T(8,128)S(1)}, u32[]{:S(2)}, u32[]{:S(2)}) collective-permute-start(f32[16,4,16,128]{3,2,1,0:T(8,128)S(1)} %slice.4.own_ref), channel_id=1, source_target_pairs={{0,16},{16,0},{1,17},{17,1},{2,18},{18,2},{3,19},{19,3},{4,20},{20... | collective-permute-start | bytes 1572872 | tf_op jit(solution)/shard_map/ppermute | solution.py:688
  100.2 0.8 copy-start.4

commit v2 on v1

--- a/solution.py
+++ b/solution.py
@@ -228,11 +228,12 @@
 radix = 16
 lane = 128
 full = radix * lane
-row_block = 32
+row_block = 64
 blocks = lane // row_block
-piece = 2 * row_block + row_block // 2
+piece = 2 * row_block
 vmem_bytes = 56 * 1024 * 1024
 rows_vmem_bytes = 50 * 1024 * 1024
+phase_vmem_bytes = 56 * 1024 * 1024
 
 
 def split_table(table):
@@ -252,11 +253,6 @@
     return np.concatenate([upper, upper, lower], axis=0)
 
 
-def left_table(direction, scale):
-    upper, lower = split_table(line_matrices(direction).T * scale)
-    return np.concatenate([upper, upper, lower], axis=1)
-
-
 def twiddle(direction, scale):
     angles = 2.0 * np.pi / full * np.outer(np.arange(radix), np.arange(lane))
     return np.stack([np.cos(angles), direction * np.sin(angles)], axis=1) * scale
@@ -267,21 +263,15 @@
     return np.ascontiguousarray(np.broadcast_to(table, (radix, 2, 8, lane))).astype(np.float32)
 
 
-def column_twiddle(direction):
-    table = np.zeros((lane, lane), np.float32)
-    table[:, : 2 * radix] = twiddle(direction, 1.0).reshape(2 * radix, lane).T
-    return table
-
-
-def root_series(offset, degree):
+def root_series(offset, degree, end):
     nodes = np.polynomial.chebyshev.Chebyshev.interpolate(
-        lambda q: np.sinc(np.sqrt(q) / np.pi) if offset else np.cos(np.sqrt(q)), degree, domain=[0.0, 9.0]
+        lambda q: np.sinc(np.sqrt(q) / np.pi) if offset else np.cos(np.sqrt(q)), degree, domain=[0.0, end]
     )
     return [float(value) for value in nodes.convert(kind=np.polynomial.Polynomial).coef]
 
 
-cos_series = root_series(0, 7)
-sinc_series = root_series(1, 6)
+cos_series, sinc_series = root_series(0, 7, 9.0), root_series(1, 6, 9.0)
+circle_cos, circle_sin = root_series(0, 8, np.pi**2), root_series(1, 7, np.pi**2)
 
 
 def horner(series, argument):
@@ -361,9 +351,7 @@
     return slice(index * lane, (index + 1) * lane)
 
 
-def lines_kernel(field_ref, speed_ref, turn_ref, table_ref, out_ref, work_ref):
-    step = pl.program_id(0)
-
+def lines_kernel(field_ref, turn_ref, table_ref, out_ref, work_ref):
     def rows(index, carry):
         here = pl.ds(pl.multiple_of(index * 8, 8), 8)
         parts = sixteen(
@@ -375,25 +363,20 @@
             work_ref[k, here, lane : 2 * lane] = im
         return carry
 
-    lax.fori_loop(0, row_block // 8, rows, 0)
+    lax.fori_loop(0, row_block // 8, rows, 0, unroll=True)
     lines = right_product(work_ref[...].reshape(radix * row_block, 2 * lane), table_ref[...])
-    half = row_block // 2
-    begin = lax.axis_index("shot") * (lane // 2) + step * half
-    speed_rows = pl.ds(pl.multiple_of(begin, 8), half)
     for k in range(radix):
         block = lines[k * row_block : (k + 1) * row_block]
         out_ref[k, 0, 0:row_block] = block[:, 0:lane]
         out_ref[k, 0, row_block : 2 * row_block] = block[:, lane : 2 * lane]
-        out_ref[k, 0, 2 * row_block : piece] = speed_ref[0, speed_rows, tile(k)]
-
-
-def lines_call(wavefield, velocity):
+
+
+def lines_call(wavefield):
     return pl.pallas_call(
         lines_kernel,
         grid=(blocks,),
         in_specs=[
             pl.BlockSpec((1, 2, row_block, full), lambda g: (0, 0, g, 0)),
-            pl.BlockSpec((1, lane, full), lambda g: (0, 0, 0)),
             pl.BlockSpec((radix, 2, 8, lane), lambda g: (0, 0, 0, 0)),
             pl.BlockSpec((6 * lane, 2 * lane), lambda g: (0, 0)),
         ],
@@ -402,7 +385,7 @@
         scratch_shapes=[pltpu.VMEM((radix, row_block, 2 * lane), jnp.float32)],
         compiler_params=pltpu.CompilerParams(vmem_limit_bytes=vmem_bytes),
         name="forward_lines",
-    )(wavefield, velocity, lane_twiddle(-1, 1.0), right_table(-1))
+    )(wavefield, lane_twiddle(-1, 1.0), right_table(-1))
 
 
 def phase_kernel(angular_ref, out_ref):
@@ -441,17 +424,39 @@
     return pl.pallas_call(
         phase_kernel,
         in_specs=[pl.BlockSpec(memory_space=pltpu.SMEM)],
-        out_specs=pl.BlockSpec((count, 2, lane, full), lambda: (0, 0, 0, 0)),
+        out_specs=pl.BlockSpec(memory_space=pltpu.VMEM),
         out_shape=jax.ShapeDtypeStruct((count, 2, lane, full), jnp.float32),
-        compiler_params=pltpu.CompilerParams(vmem_limit_bytes=vmem_bytes),
+        compiler_params=pltpu.CompilerParams(vmem_limit_bytes=phase_vmem_bytes),
         cost_estimate=pl.CostEstimate(flops=60 * count * lane * full, bytes_accessed=8 * count * lane * full, transcendentals=0),
         name="phase_factors",
     )(frequencies)
 
 
+def circle(index, modulus):
+    half = modulus // 2
+    angle = (((index + half) & (modulus - 1)) - half).astype(jnp.float32) * (2.0 * math.pi / modulus)
+    square = angle * angle
+    return horner(circle_cos, square), angle * horner(circle_sin, square)
+
+
+def build_matrices(ahead_table_ref, back_table_ref):
+    row = lax.broadcasted_iota(jnp.int32, (lane, lane), 0)
+    column = lax.broadcasted_iota(jnp.int32, (lane, lane), 1)
+    cosine, sine = circle(row * column, lane)
+    for table_ref, direction, scale in ((ahead_table_ref, -1.0, 1.0), (back_table_ref, 1.0, 1.0 / full)):
+        cos_now, sin_now = cosine * scale, sine * (direction * scale)
+        for top, blocks_now in enumerate(((cos_now, -sin_now), (sin_now, cos_now))):
+            here = slice(top * lane, (top + 1) * lane)
+            for place, values in enumerate(blocks_now):
+                upper, lower = halves(values)
+                for third, part in enumerate((upper, upper, lower)):
+                    table_ref[here, tile(2 * third + place)] = part
+
+
 def rows_kernel(
-    in_ref, phase_ref, column_ref, ahead_table_ref, back_table_ref, out_ref,
-    work_ref, spec_ref, turn_ref, factor_ref, field_ref, factor_sem, field_sem,
+    in_ref, phase_ref, out_ref,
+    work_ref, spec_ref, turn_ref, column_ref, ahead_table_ref, back_table_ref,
+    factor_ref, field_ref, factor_sem, field_sem,
 ):
     count = len(ref_speeds)
 
@@ -463,13 +468,20 @@
 
     for j in range(count):
         factor_copy(j).start()
+
+    row = lax.broadcasted_iota(jnp.int32, (lane, lane), 0)
+    power = lax.broadcasted_iota(jnp.int32, (lane, lane), 1) & (radix - 1)
+    cosine, sine = circle(row * power, full)
+    column_ref[0] = cosine
+    column_ref[1] = -sine
+    build_matrices(ahead_table_ref, back_table_ref)
 
     def rows(index, carry):
         group = index // (row_block // 8)
         local = pl.multiple_of((index % (row_block // 8)) * 8, 8)
         here = pl.ds(pl.multiple_of(index * 8, 8), 8)
         there = pl.ds(pl.multiple_of(index * 8 + lane, 8), 8)
-        columns = column_ref[here, :]
+        columns = (column_ref[0, here, :], column_ref[1, here, :])
         parts = sixteen(
             [
                 (in_ref[s, group, pl.ds(local, 8), :], in_ref[s, group, pl.ds(local + row_block, 8), :])
@@ -478,60 +490,69 @@
             -1,
         )
         for k in range(radix):
-            turn = tuple(
-                jnp.broadcast_to(columns[:, 2 * k + part : 2 * k + part + 1], (8, lane)) for part in range(2)
-            )
+            turn = tuple(jnp.broadcast_to(part[:, k : k + 1], (8, lane)) for part in columns)
             turn_ref[k, 0, here, :] = turn[0]
             turn_ref[k, 1, here, :] = turn[1]
             re, im = times(parts[k], turn)
-            work_ref[here, tile(k)] = re
-            work_ref[there, tile(k)] = im
+            work_ref[0, here, tile(k)] = re
+            work_ref[0, there, tile(k)] = im
         return carry
 
-    lax.fori_loop(0, lane // 8, rows, 0)
-
-    def pairs(index, carry):
-        columns = pl.ds(pl.multiple_of(index * 2 * lane, 2 * lane), 2 * lane)
-        spec_ref[:, columns] = left_product(ahead_table_ref[...], work_ref[:, columns])
+    lax.fori_loop(0, lane // 8, rows, 0, unroll=2)
+
+    def shifted(j, columns, spectrum):
+        re, im = times(
+            (spectrum[0:lane], spectrum[lane : 2 * lane]),
+            (factor_ref[j, 0, :, columns], factor_ref[j, 1, :, columns]),
+        )
+        work_ref[(j + 1) % 2, :, columns] = left_product(back_table_ref[...], jnp.concatenate([re, im], axis=0))
+
+    def back(j, index):
+        here = pl.ds(pl.multiple_of(index * 8, 8), 8)
+        there = pl.ds(pl.multiple_of(index * 8 + lane, 8), 8)
+        parts = sixteen(
+            [
+                conjugate_times(
+                    (work_ref[(j + 1) % 2, here, tile(k)], work_ref[(j + 1) % 2, there, tile(k)]),
+                    (turn_ref[k, 0, here, :], turn_ref[k, 1, here, :]),
+                )
+                for k in range(radix)
+            ],
+            1,
+        )
+        for s in range(radix):
+            field_ref[j % 2, s, 0, here, :] = parts[s][0]
+            field_ref[j % 2, s, 1, here, :] = parts[s][1]
+
+    def pair_columns(index):
+        return pl.ds(pl.multiple_of(index * 2 * lane, 2 * lane), 2 * lane)
+
+    factor_copy(0).wait()
+
+    def first(index, carry):
+        columns = pair_columns(index)
+        spectrum = left_product(ahead_table_ref[...], work_ref[0, :, columns])
+        spec_ref[:, columns] = spectrum
+        shifted(0, columns, spectrum)
         return carry
 
-    lax.fori_loop(0, radix // 2, pairs, 0, unroll=True)
+    lax.fori_loop(0, radix // 2, first, 0, unroll=True)
 
     for j in range(count):
-        factor_copy(j).wait()
-
-        def shifted(index, carry):
-            columns = pl.ds(pl.multiple_of(index * 2 * lane, 2 * lane), 2 * lane)
-            re, im = times(
-                (spec_ref[0:lane, columns], spec_ref[lane : 2 * lane, columns]),
-                (factor_ref[j, 0, :, columns], factor_ref[j, 1, :, columns]),
-            )
-            work_ref[:, columns] = left_product(back_table_ref[...], jnp.concatenate([re, im], axis=0))
-            return carry
-
-        lax.fori_loop(0, radix // 2, shifted, 0, unroll=True)
+        if j + 1 < count:
+            factor_copy(j + 1).wait()
         if j >= 2:
             field_copy(j - 2).wait()
 
-        def back(index, carry):
-            here = pl.ds(pl.multiple_of(index * 8, 8), 8)
-            there = pl.ds(pl.multiple_of(index * 8 + lane, 8), 8)
-            parts = sixteen(
-                [
-                    conjugate_times(
-                        (work_ref[here, tile(k)], work_ref[there, tile(k)]),
-                        (turn_ref[k, 0, here, :], turn_ref[k, 1, here, :]),
-                    )
-                    for k in range(radix)
-                ],
-                1,
-            )
-            for s in range(radix):
-                field_ref[j % 2, s, 0, here, :] = parts[s][0]
-                field_ref[j % 2, s, 1, here, :] = parts[s][1]
+        def both(index, carry):
+            if j + 1 < count:
+                columns = pair_columns(index)
+                shifted(j + 1, columns, spec_ref[:, columns])
+            back(j, 2 * index)
+            back(j, 2 * index + 1)
             return carry
 
-        lax.fori_loop(0, lane // 8, back, 0)
+        lax.fori_loop(0, radix // 2, both, 0, unroll=True)
         field_copy(j).start()
 
     for j in range(count - 2, count):
@@ -544,13 +565,16 @@
     in_hbm = pl.BlockSpec(memory_space=pltpu.HBM)
     return pl.pallas_call(
         rows_kernel,
-        in_specs=[in_vmem, in_hbm, in_vmem, in_vmem, in_vmem],
+        in_specs=[in_vmem, in_hbm],
         out_specs=in_hbm,
         out_shape=jax.ShapeDtypeStruct((radix, count, 2, lane, lane), jnp.float32),
         scratch_shapes=[
-            pltpu.VMEM((2 * lane, full), jnp.float32),
+            pltpu.VMEM((2, 2 * lane, full), jnp.float32),
             pltpu.VMEM((2 * lane, full), jnp.float32),
             pltpu.VMEM((radix, 2, lane, lane), jnp.float32),
+            pltpu.VMEM((2, lane, lane), jnp.float32),
+            pltpu.VMEM((2 * lane, 6 * lane), jnp.bfloat16),
+            pltpu.VMEM((2 * lane, 6 * lane), jnp.bfloat16),
             pltpu.VMEM((count, 2, lane, full), jnp.float32),
             pltpu.VMEM((2, radix, 2, lane, lane), jnp.float32),
             pltpu.SemaphoreType.DMA((count,)),
@@ -558,60 +582,58 @@
         ],
         compiler_params=pltpu.CompilerParams(vmem_limit_bytes=rows_vmem_bytes),
         name="rows_there_and_back",
-    )(arrived, phase, column_twiddle(-1), left_table(-1, 1.0), left_table(1, 1.0 / full))
-
-
-def blend_kernel(angular_ref, own_ref, other_ref, bracket_ref, out_ref, tile_ref):
-    shot = lax.axis_index("shot")
-    half = row_block // 2
-    for d in range(radix):
-        for g in range(blocks):
-            own = pl.ds(pl.multiple_of(shot * (lane // 2) + g * half, 8), half)
-            other = pl.ds(pl.multiple_of((1 - shot) * (lane // 2) + g * half, 8), half)
-            tile_ref[own, :] = own_ref[d, g]
-            tile_ref[other, :] = other_ref[d, g]
-        speed = jnp.transpose(tile_ref[...])
-        lower = bracket_ref[0, :, tile(d)]
-        first = lower == 0
-        low = jnp.where(first, ref_speeds[0], ref_speeds[1])
-        width = jnp.where(first, 1.0 / (ref_speeds[1] - ref_speeds[0]), 1.0 / (ref_speeds[2] - ref_speeds[1]))
-        fraction = (speed - low) * width
-        low_slowness = jnp.where(first, 1.0 / ref_speeds[0], 1.0 / ref_speeds[1])
-        high_slowness = jnp.where(first, 1.0 / ref_speeds[1], 1.0 / ref_speeds[2])
-        residual = 1.0 / speed - ((1.0 - fraction) * low_slowness + fraction * high_slowness)
-        angle = angular_ref[0] * step_length * residual
-        square = angle * angle
-        cosine = horner([1.0, -1 / 2, 1 / 24, -1 / 720, 1 / 40320], square)
-        sine = angle * horner([1.0, -1 / 6, 1 / 120, -1 / 5040, 1 / 362880], square)
-        out_ref[0, :, tile(d)] = fraction + jnp.where(first, 0.0, 1.0)
-        out_ref[1, :, tile(d)] = cosine
-        out_ref[2, :, tile(d)] = sine
-
-
-def blend_call(frequencies, own, other, bracket):
+    )(arrived, phase)
+
+
+def blend_kernel(angular_ref, bracket_ref, *refs):
+    speed_refs, out_ref = refs[:-1], refs[-1]
+    device = lax.axis_index("slab")
+    for k, speed_ref in enumerate(speed_refs):
+        for side in range(2):
+            source = device ^ (k + side * (radix // 2))
+            there = pl.ds(pl.multiple_of(source * lane, lane), lane)
+            speed = jnp.transpose(speed_ref[side])
+            first = bracket_ref[0, :, there] == 0
+            low = jnp.where(first, ref_speeds[0], ref_speeds[1])
+            width = jnp.where(first, 1.0 / (ref_speeds[1] - ref_speeds[0]), 1.0 / (ref_speeds[2] - ref_speeds[1]))
+            fraction = (speed - low) * width
+            low_slowness = jnp.where(first, 1.0 / ref_speeds[0], 1.0 / ref_speeds[1])
+            high_slowness = jnp.where(first, 1.0 / ref_speeds[1], 1.0 / ref_speeds[2])
+            residual = 1.0 / speed - ((1.0 - fraction) * low_slowness + fraction * high_slowness)
+            angle = angular_ref[0] * step_length * residual
+            square = angle * angle
+            cosine = horner([1.0, -1 / 2, 1 / 24, -1 / 720, 1 / 40320], square)
+            sine = angle * horner([1.0, -1 / 6, 1 / 120, -1 / 5040, 1 / 362880], square)
+            out_ref[0, :, there] = fraction + jnp.where(first, 0.0, 1.0)
+            out_ref[1, :, there] = cosine
+            out_ref[2, :, there] = sine
+
+
+def blend_call(frequencies, bracket, speeds):
     return pl.pallas_call(
         blend_kernel,
         in_specs=[
             pl.BlockSpec(memory_space=pltpu.SMEM),
-            pl.BlockSpec((radix, blocks, row_block // 2, lane), lambda: (0, 0, 0, 0)),
-            pl.BlockSpec((radix, blocks, row_block // 2, lane), lambda: (0, 0, 0, 0)),
             pl.BlockSpec((1, lane, full), lambda: (0, 0, 0)),
-        ],
+        ]
+        + [pl.BlockSpec((2, lane, lane), lambda: (0, 0, 0))] * len(speeds),
         out_specs=pl.BlockSpec((3, lane, full), lambda: (0, 0, 0)),
         out_shape=jax.ShapeDtypeStruct((3, lane, full), jnp.float32),
-        scratch_shapes=[pltpu.VMEM((lane, lane), jnp.float32)],
         compiler_params=pltpu.CompilerParams(vmem_limit_bytes=vmem_bytes),
         cost_estimate=pl.CostEstimate(flops=60 * lane * full, bytes_accessed=24 * lane * full, transcendentals=0),
         name="blend_factors",
-    )(frequencies, own, other, bracket)
-
-
-def finish_kernel(in_ref, blend_ref, turn_ref, table_ref, out_ref, image_ref, work_ref, wave_ref):
+    )(frequencies, bracket, *speeds)
+
+
+strip = 32
+
+
+def finish_kernel(in_ref, blend_ref, turn_ref, table_ref, out_ref, image_ref, work_ref):
     count = len(ref_speeds)
     for j in range(count):
         values = jnp.concatenate([in_ref[:, j, 0], in_ref[:, j, 1]], axis=2)
-        product = right_product(values.reshape(radix * row_block, 2 * lane), table_ref[...])
-        work_ref[j] = product.reshape(radix, row_block, 2 * lane)
+        product = right_product(values.reshape(radix * strip, 2 * lane), table_ref[...])
+        work_ref[j] = product.reshape(radix, strip, 2 * lane)
 
     def rows(index, carry):
         here = pl.ds(pl.multiple_of(index * 8, 8), 8)
@@ -627,49 +649,47 @@
                 1,
             )
             for s in range(radix):
-                wave_ref[j, 0, :, tile(s)] = parts[s][0]
-                wave_ref[j, 1, :, tile(s)] = parts[s][1]
-        for s in range(radix):
-            place = blend_ref[0, here, tile(s)]
-            weights_now = (
-                jnp.maximum(1.0 - place, 0.0),
-                1.0 - jnp.abs(place - 1.0),
-                jnp.maximum(place - 1.0, 0.0),
-            )
-            mixed = [
-                sum(weights_now[j] * wave_ref[j, part, :, tile(s)] for j in range(count)) for part in range(2)
-            ]
-            re, im = times(mixed, (blend_ref[1, here, tile(s)], blend_ref[2, here, tile(s)]))
-            out_ref[0, 0, here, tile(s)] = re
-            out_ref[0, 1, here, tile(s)] = im
-            image_ref[0, here, tile(s)] = re
+                place = blend_ref[0, here, tile(s)]
+                if j == 0:
+                    weight = jnp.maximum(1.0 - place, 0.0)
+                elif j == 1:
+                    weight = 1.0 - jnp.abs(place - 1.0)
+                else:
+                    weight = jnp.maximum(place - 1.0, 0.0)
+                re, im = parts[s][0] * weight, parts[s][1] * weight
+                if j > 0:
+                    re, im = re + out_ref[0, 0, here, tile(s)], im + out_ref[0, 1, here, tile(s)]
+                if j == count - 1:
+                    re, im = times((re, im), (blend_ref[1, here, tile(s)], blend_ref[2, here, tile(s)]))
+                    image_ref[0, here, tile(s)] = re
+                out_ref[0, 0, here, tile(s)] = re
+                out_ref[0, 1, here, tile(s)] = im
         return carry
 
-    lax.fori_loop(0, row_block // 8, rows, 0)
+    lax.fori_loop(0, strip // 8, rows, 0, unroll=True)
 
 
 def finish_call(returned, blend):
     count = len(ref_speeds)
     return pl.pallas_call(
         finish_kernel,
-        grid=(blocks,),
+        grid=(lane // strip,),
         in_specs=[
-            pl.BlockSpec((radix, count, 2, row_block, lane), lambda g: (0, 0, 0, g, 0)),
-            pl.BlockSpec((3, row_block, full), lambda g: (0, g, 0)),
+            pl.BlockSpec((radix, count, 2, strip, lane), lambda g: (0, 0, 0, g, 0)),
+            pl.BlockSpec((3, strip, full), lambda g: (0, g, 0)),
             pl.BlockSpec((radix, 2, 8, lane), lambda g: (0, 0, 0, 0)),
             pl.BlockSpec((6 * lane, 2 * lane), lambda g: (0, 0)),
         ],
         out_specs=[
-            pl.BlockSpec((1, 2, row_block, full), lambda g: (0, 0, g, 0)),
-            pl.BlockSpec((1, row_block, full), lambda g: (0, g, 0)),
+            pl.BlockSpec((1, 2, strip, full), lambda g: (0, 0, g, 0)),
+            pl.BlockSpec((1, strip, full), lambda g: (0, g, 0)),
         ],
         out_shape=[
             jax.ShapeDtypeStruct((1, 2, lane, full), jnp.float32),
             jax.ShapeDtypeStruct((1, lane, full), jnp.float32),
         ],
         scratch_shapes=[
-            pltpu.VMEM((count, radix, row_block, 2 * lane), jnp.float32),
-            pltpu.VMEM((count, 2, 8, full), jnp.float32),
+            pltpu.VMEM((count, radix, strip, 2 * lane), jnp.float32),
         ],
         compiler_params=pltpu.CompilerParams(vmem_limit_bytes=vmem_bytes),
         name="inverse_lines",
@@ -680,14 +700,43 @@
     return lax.all_to_all(values, "slab", split_axis=0, concat_axis=0, tiled=True)
 
 
+def partners(distance):
+    return [(index, index ^ distance) for index in range(radix)]
+
+
+def speeds_there(velocity):
+    shot, device = lax.axis_index("shot"), lax.axis_index("slab")
+    half = radix // 2
+    other_half = (1 - device // half) * (half * lane)
+    sent = lax.dynamic_slice(velocity[0], (shot * (lane // 2), other_half), (lane // 2, half * lane))
+    return sent
+
+
+def speeds_here(velocity, arrived):
+    shot, device = lax.axis_index("shot"), lax.axis_index("slab")
+    half = radix // 2
+    place = device % half
+    swapped = lax.ppermute(arrived, "shot", [(0, 1), (1, 0)])
+    far = jnp.where(shot == 0, jnp.concatenate([arrived, swapped]), jnp.concatenate([swapped, arrived]))
+    near = lax.dynamic_slice(velocity[0], (0, device // half * (half * lane)), (lane, half * lane))
+    both = jnp.stack([near, far])
+    tiles = []
+    for k in range(half):
+        part = lax.dynamic_slice(both, (0, 0, (place ^ k) * lane), (2, lane, lane))
+        tiles.append(lax.ppermute(part, "slab", partners(k)) if k else part)
+    return tiles
+
+
 def per_device(wavefield, frequencies, velocity, bracket):
-    sent = lines_call(wavefield, velocity)
+    sent = lines_call(wavefield)
     phase = phase_call(frequencies)
     arrived = exchange(sent)
-    own = arrived[:, :, 2 * row_block :, :]
-    other = lax.ppermute(own, "shot", [(0, 1), (1, 0)])
-    returned = exchange(rows_call(arrived, phase))
-    blend = blend_call(frequencies, own, other, bracket)
+    speed_sent, _, _ = lax.optimization_barrier((speeds_there(velocity), phase, arrived))
+    speed_arrived = lax.ppermute(speed_sent, "slab", partners(radix // 2))
+    fields = rows_call(arrived, phase)
+    speed_arrived, fields = lax.optimization_barrier((speed_arrived, fields))
+    returned = exchange(fields)
+    blend = blend_call(frequencies, bracket, speeds_here(velocity, speed_arrived))
     propagated, image = finish_call(returned, blend)
     return propagated, image
 

time: 234 us -> 227 us (0.970); the launches traced: 233 us -> 224 us
  waiting for transfers between devices: 180 us -> 160 us
  starting transfers between devices: 12.8 us -> 24.7 us
  Pallas kernels: 38.1 us -> 35.2 us
    all_to_all x2, waiting for transfers between devices: 168 us -> 56.9 us  [exchange(): lax.all_to_all(values, 'slab', split_axis=0, concat_axis=0, tiled=True)]
    ppermute x1 -> x9, waiting for transfers between devices: 12 us -> 103 us  [the longest x7 95.8 us: speeds_here(): tiles.append(lax.ppermute(part, 'slab', partners(k)) if k else part)]
    ppermute x1 -> x9, starting transfers between devices: 1.28 us -> 10.5 us  [the longest x7 8.19 us: speeds_here(): tiles.append(lax.ppermute(part, 'slab', partners(k)) if k else part)]
    all_to_all x2, starting transfers between devices: 11.5 us -> 14.2 us  [exchange(): lax.all_to_all(values, 'slab', split_axis=0, concat_axis=0, tiled=True)]
  transfers between devices with their start and end apart: 3 -> 11, of which waited for: 3 -> 9; matrix products, arithmetic and copies ran while one was open for 0% -> 1% of each run, Pallas kernels for 6% -> 10%
where the time goes in v2:
time: 227 us; the launch traced here: 224 us
  waiting for transfers between devices  160 us (70%)
  Pallas kernels  35.2 us (16%)
  starting transfers between devices  24.7 us (11%)
    ppermute x7, waiting for transfers between devices, speeds_here(): tiles.append(lax.ppermute(part, 'slab', partners(k)) if k else part)  95.8 us
    all_to_all x2, waiting for transfers between devices, exchange(): lax.all_to_all(values, 'slab', split_axis=0, concat_axis=0, tiled=True)  56.9 us
    all_to_all x2, starting transfers between devices, exchange(): lax.all_to_all(values, 'slab', split_axis=0, concat_axis=0, tiled=True)  14.2 us
    pallas_call x1, Pallas kernels, rows_call(): pl.pallas_call(rows_kernel, in_specs=[in_vmem, in_hbm], out_specs=in_hbm,...  9.7 us
    pallas_call x1, Pallas kernels, finish_call(): pl.pallas_call(finish_kernel, grid=(lane // strip,), in_specs=[pl.BlockSp...  8.59 us
    pallas_call x1, Pallas kernels, phase_call(): pl.pallas_call(phase_kernel, in_specs=[pl.BlockSpec(memory_space=pltpu.SM...  8.34 us
    ppermute x7, starting transfers between devices, speeds_here(): tiles.append(lax.ppermute(part, 'slab', partners(k)) if k else part)  8.19 us
    ppermute x1, waiting for transfers between devices, speeds_here(): swapped = lax.ppermute(arrived, 'shot', [(0, 1), (1, 0)])  6.6 us
  transfers between devices with their start and end apart: 11, of which 9 were waited for; matrix products, arithmetic and copies ran while one was open for 1% of the time, Pallas kernels for 10%

profile of v2, /device:TPU:13, one launch (start us, length us, event | category | flops | bytes accessed | tf_op | source)
XLA Modules:
  0.0 224.0 jit_solution(1451412331420403289)
XLA Ops:
  0.6 0.0 copy-start
  0.6 4.0 %forward_lines.1 = f32[16,2,128,128]{3,2,1,0:T(8,128)} custom-call(f32[1,2,128,2048]{3,2,1,0:T(8,128)} %field_ref.1, f32[16,2,8,128]{3,2,1,0:T(8,128)} %constant.67.clone.turn_ref, bf16[768,256]{1,0:T(8,128)(2,1)} %constant.68.clone.table_ref), custom_call_target="tpu_custom_call" | custom-call | tf_op jit(solution)/shard_map/forward_lines/pallas_call | solution.py:375
  4.6 6.6 %all-to-all-start = ((f32[16,2,128,128]{3,2,1,0:T(8,128)}), f32[16,2,128,128]{3,2,1,0:T(8,128)S(1)}, u32[]{:S(2)}, u32[]{:S(2)}) async-start(f32[16,2,128,128]{3,2,1,0:T(8,128)} %forward_lines.1), calls=%async_computation | async-start | bytes 4194304 | tf_op jit(solution)/shard_map/all_to_all | solution.py:700
  11.8 8.3 %phase_factors.1.phase_ref = f32[3,2,128,2048]{3,2,1,0:T(8,128)} custom-call(f32[1]{0:T(128)S(6)} %copy.10.angular_ref), custom_call_target="tpu_custom_call" | custom-call | flops 47185920 | bytes 6291456 | tf_op jit(solution)/shard_map/phase_factors/pallas_call | solution.py:424
  20.2 0.0 copy-done
  20.2 38.4 %all-to-all-done.in_ref = f32[16,2,128,128]{3,2,1,0:T(8,128)S(1)} async-done(((f32[16,2,128,128]{3,2,1,0:T(8,128)}), f32[16,2,128,128]{3,2,1,0:T(8,128)S(1)}, u32[]{:S(2)}, u32[]{:S(2)}) %all-to-all-start) | async-done | bytes 2097184 | tf_op jit(solution)/shard_map/all_to_all | solution.py:700
  58.6 1.1 collective-permute-start
  59.7 9.7 %rows_there_and_back.1 = f32[16,3,2,128,128]{4,3,2,1,0:T(8,128)} custom-call(f32[16,2,128,128]{3,2,1,0:T(8,128)S(1)} %all-to-all-done.in_ref, f32[3,2,128,2048]{3,2,1,0:T(8,128)} %phase_factors.1.phase_ref), custom_call_target="tpu_custom_call" | custom-call | tf_op jit(solution)/shard_map/rows_there_and_back/pallas_call | solution.py:566
  69.4 0.9 collective-permute-done
  70.3 7.6 %all-to-all-start.1 = ((f32[16,3,2,128,128]{4,3,2,1,0:T(8,128)}), f32[16,3,2,128,128]{4,3,2,1,0:T(8,128)}, u32[]{:S(2)}, u32[]{:S(2)}) async-start(f32[16,3,2,128,128]{4,3,2,1,0:T(8,128)} %rows_there_and_back.1), calls=%async_computation.1 | async-start | bytes 12582912 | tf_op jit(solution)/shard_map/all_to_all | solution.py:700
  78.0 1.2 collective-permute-start.1
  79.2 6.6 %collective-permute-done.1 = f32[64,1024]{1,0:T(8,128)S(1)} collective-permute-done((f32[64,1024]{1,0:T(8,128)}, f32[64,1024]{1,0:T(8,128)S(1)}, u32[]{:S(2)}, u32[]{:S(2)}) %collective-permute-start.1) | collective-permute-done | bytes 262176 | tf_op jit(solution)/shard_map/ppermute | solution.py:719
  85.8 1.1 maximum_select_fusion
  86.9 0.8 fusion
  87.7 1.1 collective-permute-start.2
  88.8 0.3 collective-permute-start.3
  89.0 1.4 collective-permute-start.4
  90.4 0.3 collective-permute-start.5
  90.7 1.7 collective-permute-start.6
  92.4 0.0 collective-permute-done.2.refs_1_
  92.4 0.0 copy-start.1
  92.4 0.0 collective-permute-start.7
  92.4 23.2 %collective-permute-done.3.refs_2_ = f32[2,128,128]{2,1,0:T(8,128)S(1)} collective-permute-done((f32[2,128,128]{2,1,0:T(8,128)S(1)}, f32[2,128,128]{2,1,0:T(8,128)S(1)}, u32[]{:S(2)}, u32[]{:S(2)}) %collective-permute-start.3) | collective-permute-done | bytes 131104 | tf_op jit(solution)/shard_map/ppermute | solution.py:726
  115.6 0.0 copy-start.2
  115.6 3.5 %collective-permute-start.8 = (f32[2,128,128]{2,1,0:T(8,128)S(1)}, f32[2,128,128]{2,1,0:T(8,128)S(1)}, u32[]{:S(2)}, u32[]{:S(2)}) collective-permute-start(f32[2,128,128]{2,1,0:T(8,128)S(1)} %get-tuple-element.8), channel_id=1, source_target_pairs={{0,7},{1,6},{2,5},{3,4},{4,3},{5,2},{6,1},{7,0},{8,15},{9,14},{10,... | collective-permute-start | bytes 393224 | tf_op jit(solution)/shard_map/ppermute | solution.py:726
  119.2 0.0 collective-permute-done.4.refs_3_
  119.2 0.0 copy-start.3
  119.2 65.2 %collective-permute-done.5.refs_4_ = f32[2,128,128]{2,1,0:T(8,128)S(1)} collective-permute-done((f32[2,128,128]{2,1,0:T(8,128)S(1)}, f32[2,128,128]{2,1,0:T(8,128)S(1)}, u32[]{:S(2)}, u32[]{:S(2)}) %collective-permute-start.5) | collective-permute-done | bytes 131104 | tf_op jit(solution)/shard_map/ppermute | solution.py:726
  184.3 0.0 copy-start.4
  184.3 3.8 %collective-permute-done.6.refs_5_ = f32[2,128,128]{2,1,0:T(8,128)S(1)} collective-permute-done((f32[2,128,128]{2,1,0:T(8,128)S(1)}, f32[2,128,128]{2,1,0:T(8,128)S(1)}, u32[]{:S(2)}, u32[]{:S(2)}) %collective-permute-start.6) | collective-permute-done | bytes 131104 | tf_op jit(solution)/shard_map/ppermute | solution.py:726
  188.1 0.0 copy-start.5
  188.1 0.9 collective-permute-done.7.refs_6_
  188.9 0.0 copy-start.6
  188.9 2.8 %collective-permute-done.8.refs_7_ = f32[2,128,128]{2,1,0:T(8,128)S(1)} collective-permute-done((f32[2,128,128]{2,1,0:T(8,128)S(1)}, f32[2,128,128]{2,1,0:T(8,128)S(1)}, u32[]{:S(2)}, u32[]{:S(2)}) %collective-permute-start.8) | collective-permute-done | bytes 131104 | tf_op jit(solution)/shard_map/ppermute | solution.py:726
  191.8 0.0 copy-start.7
  191.8 0.0 copy-done.1
  191.8 0.0 copy-done.2
  191.8 0.0 copy-done.3
  191.8 0.0 copy-done.4
  191.8 0.0 copy-done.5
  191.8 0.0 copy-done.6
  191.8 0.6 copy-done.7
  192.4 4.6 %blend_factors.1.blend_ref = f32[3,128,2048]{2,1,0:T(8,128)} custom-call(f32[1]{0:T(128)S(6)} %copy.10.angular_ref, s32[1,128,2048]{2,1,0:T(8,128)} %bracket_ref.1, f32[2,128,128]{2,1,0:T(8,128)} %get-tuple-element.9.refs_0_, f32[2,128,128]{2,1,0:T(8,128)} %copy-done.1, f32[2,128,128]{2,1,0:T(8,128)} %copy-done.2, f32[2,128,128]{2,1,0:T(8,128)} %copy-done.3, ...), custom_call_target="tpu_custom_call" | custom-call | flops 15728640 | bytes 6291456 | tf_op jit(solution)/shard_map/blend_factors/pallas_call | solution.py:613
  197.0 18.4 %all-to-all-done.1.in_ref = f32[16,3,2,128,128]{4,3,2,1,0:T(8,128)} async-done(((f32[16,3,2,128,128]{4,3,2,1,0:T(8,128)}), f32[16,3,2,128,128]{4,3,2,1,0:T(8,128)}, u32[]{:S(2)}, u32[]{:S(2)}) %all-to-all-start.1) | async-done | bytes 6291488 | tf_op jit(solution)/shard_map/all_to_all | solution.py:700
  215.4 8.6 %inverse_lines.1 = (f32[1,2,128,2048]{3,2,1,0:T(8,128)}, f32[1,128,2048]{2,1,0:T(8,128)}) custom-call(f32[16,3,2,128,128]{4,3,2,1,0:T(8,128)} %all-to-all-done.1.in_ref, f32[3,128,2048]{2,1,0:T(8,128)} %blend_factors.1.blend_ref, f32[16,2,8,128]{3,2,1,0:T(8,128)} %constant.69.clone.turn_ref, bf16[768,256]{1,0:T(8,128)(2,1)} %constant.70.clone.table_ref), custom_call_target="tpu_custom_call" | custom-call | tf_op jit(solution)/shard_map/inverse_lines/pallas_call | solution.py:674
  (3 shorter events, 0.1 us)
Async XLA Ops:
  0.6 19.5 %copy-start = (f32[1,128,2048]{2,1,0:T(8,128)S(1)}, f32[1,128,2048]{2,1,0:T(8,128)}, u32[]{:S(2)}) copy-start(f32[1,128,2048]{2,1,0:T(8,128)} %param.10) | copy-start | bytes 3145732
  4.6 54.0 %all-to-all-start = ((f32[16,2,128,128]{3,2,1,0:T(8,128)}), f32[16,2,128,128]{3,2,1,0:T(8,128)S(1)}, u32[]{:S(2)}, u32[]{:S(2)}) async-start(f32[16,2,128,128]{3,2,1,0:T(8,128)} %forward_lines.1), calls=%async_computation | async-start | bytes 4194304 | tf_op jit(solution)/shard_map/all_to_all | solution.py:700
  58.6 11.8 %collective-permute-start = (f32[64,1024]{1,0:T(8,128)S(1)}, f32[64,1024]{1,0:T(8,128)}, u32[]{:S(2)}, u32[]{:S(2)}) collective-permute-start(f32[64,1024]{1,0:T(8,128)S(1)} %dynamic-slice_bitcast_fusion), channel_id=1, source_target_pairs={{0,8},{1,9},{2,10},{3,11},{4,12},{5,13},{6,14},{7,15},{8,0},{9,1},... | collective-permute-start | bytes 786440 | tf_op jit(solution)/shard_map/ppermute | solution.py:735
  70.3 145.1 %all-to-all-start.1 = ((f32[16,3,2,128,128]{4,3,2,1,0:T(8,128)}), f32[16,3,2,128,128]{4,3,2,1,0:T(8,128)}, u32[]{:S(2)}, u32[]{:S(2)}) async-start(f32[16,3,2,128,128]{4,3,2,1,0:T(8,128)} %rows_there_and_back.1), calls=%async_computation.1 | async-start | bytes 12582912 | tf_op jit(solution)/shard_map/all_to_all | solution.py:700
  78.0 7.8 %collective-permute-start.1 = (f32[64,1024]{1,0:T(8,128)}, f32[64,1024]{1,0:T(8,128)S(1)}, u32[]{:S(2)}, u32[]{:S(2)}) collective-permute-start(f32[64,1024]{1,0:T(8,128)} %collective-permute-done), channel_id=1, source_target_pairs={{0,16},{16,0},{1,17},{17,1},{2,18},{18,2},{3,19},{19,3},{4,20},{20... | collective-permute-start | bytes 786440 | tf_op jit(solution)/shard_map/ppermute | solution.py:719
  87.7 4.7 %collective-permute-start.2 = (f32[2,128,128]{2,1,0:T(8,128)S(1)}, f32[2,128,128]{2,1,0:T(8,128)S(1)}, u32[]{:S(2)}, u32[]{:S(2)}) collective-permute-start(f32[2,128,128]{2,1,0:T(8,128)S(1)} %get-tuple-element.10), channel_id=1, source_target_pairs={{0,1},{1,0},{2,3},{3,2},{4,5},{5,4},{6,7},{7,6},{8,9},{9,8},{10,11... | collective-permute-start | bytes 393224 | tf_op jit(solution)/shard_map/ppermute | solution.py:726
  88.8 26.9 %collective-permute-start.3 = (f32[2,128,128]{2,1,0:T(8,128)S(1)}, f32[2,128,128]{2,1,0:T(8,128)S(1)}, u32[]{:S(2)}, u32[]{:S(2)}) collective-permute-start(f32[2,128,128]{2,1,0:T(8,128)S(1)} %get-tuple-element.11), channel_id=1, source_target_pairs={{0,2},{1,3},{2,0},{3,1},{4,6},{5,7},{6,4},{7,5},{8,10},{9,11},{10,... | collective-permute-start | bytes 393224 | tf_op jit(solution)/shard_map/ppermute | solution.py:726
  89.0 30.1 %collective-permute-start.4 = (f32[2,128,128]{2,1,0:T(8,128)S(1)}, f32[2,128,128]{2,1,0:T(8,128)S(1)}, u32[]{:S(2)}, u32[]{:S(2)}) collective-permute-start(f32[2,128,128]{2,1,0:T(8,128)S(1)} %get-tuple-element.12), channel_id=1, source_target_pairs={{0,3},{1,2},{2,1},{3,0},{4,7},{5,6},{6,5},{7,4},{8,11},{9,10},{10,... | collective-permute-start | bytes 393224 | tf_op jit(solution)/shard_map/ppermute | solution.py:726
  90.4 93.9 %collective-permute-start.5 = (f32[2,128,128]{2,1,0:T(8,128)S(1)}, f32[2,128,128]{2,1,0:T(8,128)S(1)}, u32[]{:S(2)}, u32[]{:S(2)}) collective-permute-start(f32[2,128,128]{2,1,0:T(8,128)S(1)} %get-tuple-element.13), channel_id=1, source_target_pairs={{0,4},{1,5},{2,6},{3,7},{4,0},{5,1},{6,2},{7,3},{8,12},{9,13},{10,... | collective-permute-start | bytes 393224 | tf_op jit(solution)/shard_map/ppermute | solution.py:726
  90.7 97.4 %collective-permute-start.6 = (f32[2,128,128]{2,1,0:T(8,128)S(1)}, f32[2,128,128]{2,1,0:T(8,128)S(1)}, u32[]{:S(2)}, u32[]{:S(2)}) collective-permute-start(f32[2,128,128]{2,1,0:T(8,128)S(1)} %get-tuple-element.15), channel_id=1, source_target_pairs={{0,5},{1,4},{2,7},{3,6},{4,1},{5,0},{6,3},{7,2},{8,13},{9,12},{10,... | collective-permute-start | bytes 393224 | tf_op jit(solution)/shard_map/ppermute | solution.py:726
  92.4 99.4 %copy-start.1 = (f32[2,128,128]{2,1,0:T(8,128)}, f32[2,128,128]{2,1,0:T(8,128)S(1)}, u32[]{:S(2)}) copy-start(f32[2,128,128]{2,1,0:T(8,128)S(1)} %collective-permute-done.2.refs_1_) | copy-start | bytes 393220
  92.4 96.6 %collective-permute-start.7 = (f32[2,128,128]{2,1,0:T(8,128)S(1)}, f32[2,128,128]{2,1,0:T(8,128)S(1)}, u32[]{:S(2)}, u32[]{:S(2)}) collective-permute-start(f32[2,128,128]{2,1,0:T(8,128)S(1)} %get-tuple-element.14), channel_id=1, source_target_pairs={{0,6},{1,7},{2,4},{3,5},{4,2},{5,3},{6,0},{7,1},{8,14},{9,15},{10,... | collective-permute-start | bytes 393224 | tf_op jit(solution)/shard_map/ppermute | solution.py:726
  115.6 76.1 %copy-start.2 = (f32[2,128,128]{2,1,0:T(8,128)}, f32[2,128,128]{2,1,0:T(8,128)S(1)}, u32[]{:S(2)}) copy-start(f32[2,128,128]{2,1,0:T(8,128)S(1)} %collective-permute-done.3.refs_2_) | copy-start | bytes 393220
  115.6 76.1 %collective-permute-start.8 = (f32[2,128,128]{2,1,0:T(8,128)S(1)}, f32[2,128,128]{2,1,0:T(8,128)S(1)}, u32[]{:S(2)}, u32[]{:S(2)}) collective-permute-start(f32[2,128,128]{2,1,0:T(8,128)S(1)} %get-tuple-element.8), channel_id=1, source_target_pairs={{0,7},{1,6},{2,5},{3,4},{4,3},{5,2},{6,1},{7,0},{8,15},{9,14},{10,... | collective-permute-start | bytes 393224 | tf_op jit(solution)/shard_map/ppermute | solution.py:726
  119.2 72.6 %copy-start.3 = (f32[2,128,128]{2,1,0:T(8,128)}, f32[2,128,128]{2,1,0:T(8,128)S(1)}, u32[]{:S(2)}) copy-start(f32[2,128,128]{2,1,0:T(8,128)S(1)} %collective-permute-done.4.refs_3_) | copy-start | bytes 393220
  184.3 7.4 %copy-start.4 = (f32[2,128,128]{2,1,0:T(8,128)}, f32[2,128,128]{2,1,0:T(8,128)S(1)}, u32[]{:S(2)}) copy-start(f32[2,128,128]{2,1,0:T(8,128)S(1)} %collective-permute-done.5.refs_4_) | copy-start | bytes 393220
  188.1 3.7 %copy-start.5 = (f32[2,128,128]{2,1,0:T(8,128)}, f32[2,128,128]{2,1,0:T(8,128)S(1)}, u32[]{:S(2)}) copy-start(f32[2,128,128]{2,1,0:T(8,128)S(1)} %collective-permute-done.6.refs_5_) | copy-start | bytes 393220
  188.9 2.8 %copy-start.6 = (f32[2,128,128]{2,1,0:T(8,128)}, f32[2,128,128]{2,1,0:T(8,128)S(1)}, u32[]{:S(2)}) copy-start(f32[2,128,128]{2,1,0:T(8,128)S(1)} %collective-permute-done.7.refs_6_) | copy-start | bytes 393220
  191.8 0.7 copy-start.7

commit v3 on v2

--- a/solution.py
+++ b/solution.py
@@ -1,3 +1,4 @@
+import functools
 import math
 
 import jax
@@ -229,11 +230,14 @@
 lane = 128
 full = radix * lane
 row_block = 64
+half_radix = radix // 2
+far = radix // 2 + radix // 4
 blocks = lane // row_block
 piece = 2 * row_block
 vmem_bytes = 56 * 1024 * 1024
 rows_vmem_bytes = 50 * 1024 * 1024
 phase_vmem_bytes = 56 * 1024 * 1024
+finish_vmem_bytes = 48 * 1024 * 1024
 
 
 def split_table(table):
@@ -351,7 +355,7 @@
     return slice(index * lane, (index + 1) * lane)
 
 
-def lines_kernel(field_ref, turn_ref, table_ref, out_ref, work_ref):
+def lines_kernel(field_ref, turn_ref, table_ref, even_ref, odd_ref, work_ref):
     def rows(index, carry):
         here = pl.ds(pl.multiple_of(index * 8, 8), 8)
         parts = sixteen(
@@ -367,8 +371,10 @@
     lines = right_product(work_ref[...].reshape(radix * row_block, 2 * lane), table_ref[...])
     for k in range(radix):
         block = lines[k * row_block : (k + 1) * row_block]
-        out_ref[k, 0, 0:row_block] = block[:, 0:lane]
-        out_ref[k, 0, row_block : 2 * row_block] = block[:, lane : 2 * lane]
+        for half in range(2):
+            out_ref = (even_ref, odd_ref)[k % 2]
+            out_ref[half * half_radix + k // 2, 0, 0:row_block] = block[:, 0:lane]
+            out_ref[half * half_radix + k // 2, 0, row_block : 2 * row_block] = block[:, lane : 2 * lane]
 
 
 def lines_call(wavefield):
@@ -380,8 +386,8 @@
             pl.BlockSpec((radix, 2, 8, lane), lambda g: (0, 0, 0, 0)),
             pl.BlockSpec((6 * lane, 2 * lane), lambda g: (0, 0)),
         ],
-        out_specs=pl.BlockSpec((radix, 1, piece, lane), lambda g: (0, g, 0, 0)),
-        out_shape=jax.ShapeDtypeStruct((radix, blocks, piece, lane), jnp.float32),
+        out_specs=[pl.BlockSpec((radix, 1, piece, lane), lambda g: (0, g, 0, 0))] * 2,
+        out_shape=[jax.ShapeDtypeStruct((radix, blocks, piece, lane), jnp.float32)] * 2,
         scratch_shapes=[pltpu.VMEM((radix, row_block, 2 * lane), jnp.float32)],
         compiler_params=pltpu.CompilerParams(vmem_limit_bytes=vmem_bytes),
         name="forward_lines",
@@ -389,11 +395,14 @@
 
 
 def phase_kernel(angular_ref, out_ref):
-    device = lax.axis_index("slab")
+    place = lax.axis_index("slab") % half_radix
     scale = 2.0 * math.pi / full
-    column = lax.broadcasted_iota(jnp.int32, (32, lane), 1) * radix + device
-    second = jnp.minimum(column, full - column).astype(jnp.float32) * scale
-    second = second * second
+    lanes = lax.broadcasted_iota(jnp.int32, (32, lane), 1) * radix + place * 2
+    seconds = []
+    for c in range(2):
+        column = lanes + c
+        second = jnp.minimum(column, full - column).astype(jnp.float32) * scale
+        seconds.append(second * second)
     row = lax.broadcasted_iota(jnp.int32, (32, lane), 0)
     squares = []
     for speed in ref_speeds:
@@ -407,13 +416,14 @@
         there = pl.ds(pl.multiple_of(k * lane, lane), lane)
         position = (row + begin) * radix + k
         first = jnp.minimum(position, full - position).astype(jnp.float32) * scale
-        wave_square = first * first + second
-        for j in range(len(ref_speeds)):
-            vertical = squares[j] - wave_square
-            root = jnp.sqrt(jnp.abs(vertical))
-            moving = vertical >= 0.0
-            out_ref[j, 0, here, there] = jnp.where(moving, horner(cos_series, vertical), jnp.exp(-root))
-            out_ref[j, 1, here, there] = jnp.where(moving, root * horner(sinc_series, vertical), 0.0)
+        for c in range(2):
+            wave_square = first * first + seconds[c]
+            for j in range(len(ref_speeds)):
+                vertical = squares[j] - wave_square
+                root = jnp.sqrt(jnp.abs(vertical))
+                moving = vertical >= 0.0
+                out_ref[c, j, 0, here, there] = jnp.where(moving, horner(cos_series, vertical), jnp.exp(-root))
+                out_ref[c, j, 1, here, there] = jnp.where(moving, root * horner(sinc_series, vertical), 0.0)
         return carry
 
     lax.fori_loop(0, radix * 4, chunk, 0)
@@ -425,9 +435,9 @@
         phase_kernel,
         in_specs=[pl.BlockSpec(memory_space=pltpu.SMEM)],
         out_specs=pl.BlockSpec(memory_space=pltpu.VMEM),
-        out_shape=jax.ShapeDtypeStruct((count, 2, lane, full), jnp.float32),
+        out_shape=jax.ShapeDtypeStruct((2, count, 2, lane, full), jnp.float32),
         compiler_params=pltpu.CompilerParams(vmem_limit_bytes=phase_vmem_bytes),
-        cost_estimate=pl.CostEstimate(flops=60 * count * lane * full, bytes_accessed=8 * count * lane * full, transcendentals=0),
+        cost_estimate=pl.CostEstimate(flops=120 * count * lane * full, bytes_accessed=16 * count * lane * full, transcendentals=0),
         name="phase_factors",
     )(frequencies)
 
@@ -454,20 +464,21 @@
 
 
 def rows_kernel(
-    in_ref, phase_ref, out_ref,
+    c, in_ref, phase_ref, out_ref,
     work_ref, spec_ref, turn_ref, column_ref, ahead_table_ref, back_table_ref,
     factor_ref, field_ref, factor_sem, field_sem,
 ):
+    begin = lax.axis_index("slab") // half_radix * half_radix
     count = len(ref_speeds)
 
-    def factor_copy(j):
-        return pltpu.make_async_copy(phase_ref.at[j], factor_ref.at[j], factor_sem.at[j])
-
-    def field_copy(j):
-        return pltpu.make_async_copy(field_ref.at[j % 2], out_ref.at[:, j], field_sem.at[j % 2])
-
-    for j in range(count):
-        factor_copy(j).start()
+    def factor_copy(t):
+        return pltpu.make_async_copy(phase_ref.at[c, t], factor_ref.at[t], factor_sem.at[t])
+
+    def field_copy(t):
+        return pltpu.make_async_copy(field_ref.at[t % 2], out_ref.at[:, t], field_sem.at[t % 2])
+
+    for t in range(count):
+        factor_copy(t).start()
 
     row = lax.broadcasted_iota(jnp.int32, (lane, lane), 0)
     power = lax.broadcasted_iota(jnp.int32, (lane, lane), 1) & (radix - 1)
@@ -476,53 +487,52 @@
     column_ref[1] = -sine
     build_matrices(ahead_table_ref, back_table_ref)
 
-    def rows(index, carry):
-        group = index // (row_block // 8)
-        local = pl.multiple_of((index % (row_block // 8)) * 8, 8)
+    for block in range(blocks):
+
+        def rows(index, carry):
+            local = pl.multiple_of(index * 8, 8)
+            pair = (pl.ds(local, 8), pl.ds(local + row_block, 8))
+            here = pl.ds(pl.multiple_of(local + block * row_block, 8), 8)
+            there = pl.ds(pl.multiple_of(local + block * row_block + lane, 8), 8)
+            parts = sixteen([tuple(in_ref[begin ^ s, block, rows_now, :] for rows_now in pair) for s in range(radix)], -1)
+            columns = (column_ref[0, here, :], column_ref[1, here, :])
+            for k in range(radix):
+                turn = tuple(jnp.broadcast_to(part[:, k : k + 1], (8, lane)) for part in columns)
+                turn_ref[k, 0, here, :] = turn[0]
+                turn_ref[k, 1, here, :] = turn[1]
+                re, im = times(parts[k], turn)
+                work_ref[0, here, tile(k)] = re
+                work_ref[0, there, tile(k)] = im
+            return carry
+
+        lax.fori_loop(0, row_block // 8, rows, 0, unroll=2)
+
+    def shifted(t, columns, spectrum):
+        re, im = times(
+            (spectrum[0:lane], spectrum[lane : 2 * lane]),
+            (factor_ref[t, 0, :, columns], factor_ref[t, 1, :, columns]),
+        )
+        work_ref[(t + 1) % 2, :, columns] = left_product(
+            back_table_ref[...], jnp.concatenate([re, im], axis=0)
+        )
+
+    def back(t, index):
         here = pl.ds(pl.multiple_of(index * 8, 8), 8)
         there = pl.ds(pl.multiple_of(index * 8 + lane, 8), 8)
-        columns = (column_ref[0, here, :], column_ref[1, here, :])
-        parts = sixteen(
-            [
-                (in_ref[s, group, pl.ds(local, 8), :], in_ref[s, group, pl.ds(local + row_block, 8), :])
-                for s in range(radix)
-            ],
-            -1,
-        )
-        for k in range(radix):
-            turn = tuple(jnp.broadcast_to(part[:, k : k + 1], (8, lane)) for part in columns)
-            turn_ref[k, 0, here, :] = turn[0]
-            turn_ref[k, 1, here, :] = turn[1]
-            re, im = times(parts[k], turn)
-            work_ref[0, here, tile(k)] = re
-            work_ref[0, there, tile(k)] = im
-        return carry
-
-    lax.fori_loop(0, lane // 8, rows, 0, unroll=2)
-
-    def shifted(j, columns, spectrum):
-        re, im = times(
-            (spectrum[0:lane], spectrum[lane : 2 * lane]),
-            (factor_ref[j, 0, :, columns], factor_ref[j, 1, :, columns]),
-        )
-        work_ref[(j + 1) % 2, :, columns] = left_product(back_table_ref[...], jnp.concatenate([re, im], axis=0))
-
-    def back(j, index):
-        here = pl.ds(pl.multiple_of(index * 8, 8), 8)
-        there = pl.ds(pl.multiple_of(index * 8 + lane, 8), 8)
+        slot = (t + 1) % 2
         parts = sixteen(
             [
                 conjugate_times(
-                    (work_ref[(j + 1) % 2, here, tile(k)], work_ref[(j + 1) % 2, there, tile(k)]),
+                    (work_ref[slot, here, tile(k)], work_ref[slot, there, tile(k)]),
                     (turn_ref[k, 0, here, :], turn_ref[k, 1, here, :]),
                 )
                 for k in range(radix)
             ],
             1,
         )
-        for s in range(radix):
-            field_ref[j % 2, s, 0, here, :] = parts[s][0]
-            field_ref[j % 2, s, 1, here, :] = parts[s][1]
+        for s in range(half_radix):
+            field_ref[t % 2, s, 0, here, :] = parts[s][0]
+            field_ref[t % 2, s, 1, here, :] = parts[s][1]
 
     def pair_columns(index):
         return pl.ds(pl.multiple_of(index * 2 * lane, 2 * lane), 2 * lane)
@@ -538,36 +548,36 @@
 
     lax.fori_loop(0, radix // 2, first, 0, unroll=True)
 
-    for j in range(count):
-        if j + 1 < count:
-            factor_copy(j + 1).wait()
-        if j >= 2:
-            field_copy(j - 2).wait()
+    for t in range(count):
+        if t + 1 < count:
+            factor_copy(t + 1).wait()
+        if t >= 2:
+            field_copy(t - 2).wait()
 
         def both(index, carry):
-            if j + 1 < count:
+            if t + 1 < count:
                 columns = pair_columns(index)
-                shifted(j + 1, columns, spec_ref[:, columns])
-            back(j, 2 * index)
-            back(j, 2 * index + 1)
+                shifted(t + 1, columns, spec_ref[:, columns])
+            back(t, 2 * index)
+            back(t, 2 * index + 1)
             return carry
 
         lax.fori_loop(0, radix // 2, both, 0, unroll=True)
-        field_copy(j).start()
-
-    for j in range(count - 2, count):
-        field_copy(j).wait()
-
-
-def rows_call(arrived, phase):
+        field_copy(t).start()
+
+    for t in range(count - 2, count):
+        field_copy(t).wait()
+
+
+def rows_call(c, arrived, phase):
     count = len(ref_speeds)
     in_vmem = pl.BlockSpec(memory_space=pltpu.VMEM)
     in_hbm = pl.BlockSpec(memory_space=pltpu.HBM)
     return pl.pallas_call(
-        rows_kernel,
+        functools.partial(rows_kernel, c),
         in_specs=[in_vmem, in_hbm],
         out_specs=in_hbm,
-        out_shape=jax.ShapeDtypeStruct((radix, count, 2, lane, lane), jnp.float32),
+        out_shape=jax.ShapeDtypeStruct((half_radix, count, 2, lane, lane), jnp.float32),
         scratch_shapes=[
             pltpu.VMEM((2, 2 * lane, full), jnp.float32),
             pltpu.VMEM((2 * lane, full), jnp.float32),
@@ -575,24 +585,29 @@
             pltpu.VMEM((2, lane, lane), jnp.float32),
             pltpu.VMEM((2 * lane, 6 * lane), jnp.bfloat16),
             pltpu.VMEM((2 * lane, 6 * lane), jnp.bfloat16),
-            pltpu.VMEM((count, 2, lane, full), jnp.float32),
-            pltpu.VMEM((2, radix, 2, lane, lane), jnp.float32),
-            pltpu.SemaphoreType.DMA((count,)),
+            pltpu.VMEM((3, 2, lane, full), jnp.float32),
+            pltpu.VMEM((2, half_radix, 2, lane, lane), jnp.float32),
+            pltpu.SemaphoreType.DMA((3,)),
             pltpu.SemaphoreType.DMA((2,)),
         ],
         compiler_params=pltpu.CompilerParams(vmem_limit_bytes=rows_vmem_bytes),
+        cost_estimate=pl.CostEstimate(
+            flops=8 * 2 * 2 * lane * 6 * lane * full, bytes_accessed=28 * 8 * lane * full, transcendentals=0
+        ),
         name="rows_there_and_back",
     )(arrived, phase)
 
 
-def blend_kernel(angular_ref, bracket_ref, *refs):
-    speed_refs, out_ref = refs[:-1], refs[-1]
-    device = lax.axis_index("slab")
-    for k, speed_ref in enumerate(speed_refs):
-        for side in range(2):
-            source = device ^ (k + side * (radix // 2))
+def blend_kernel(angular_ref, bracket_ref, far_ref, swapped_ref, *refs):
+    near_refs, out_ref, tile_ref = refs[:-2], refs[-2], refs[-1]
+    shot, device = lax.axis_index("shot"), lax.axis_index("slab")
+    half = lane // 2
+    for k in range(half_radix):
+        tile_ref[pl.ds(pl.multiple_of(shot * half, half), half), :] = far_ref[k]
+        tile_ref[pl.ds(pl.multiple_of((1 - shot) * half, half), half), :] = swapped_ref[k]
+        for source, speed in ((device ^ k, near_refs[k][0:lane, :]), (device ^ far ^ k, tile_ref[...])):
             there = pl.ds(pl.multiple_of(source * lane, lane), lane)
-            speed = jnp.transpose(speed_ref[side])
+            speed = jnp.transpose(speed)
             first = bracket_ref[0, :, there] == 0
             low = jnp.where(first, ref_speeds[0], ref_speeds[1])
             width = jnp.where(first, 1.0 / (ref_speeds[1] - ref_speeds[0]), 1.0 / (ref_speeds[2] - ref_speeds[1]))
@@ -609,16 +624,14 @@
             out_ref[2, :, there] = sine
 
 
-def blend_call(frequencies, bracket, speeds):
+def blend_call(frequencies, bracket, *speeds):
+    in_vmem = pl.BlockSpec(memory_space=pltpu.VMEM)
     return pl.pallas_call(
         blend_kernel,
-        in_specs=[
-            pl.BlockSpec(memory_space=pltpu.SMEM),
-            pl.BlockSpec((1, lane, full), lambda: (0, 0, 0)),
-        ]
-        + [pl.BlockSpec((2, lane, lane), lambda: (0, 0, 0))] * len(speeds),
-        out_specs=pl.BlockSpec((3, lane, full), lambda: (0, 0, 0)),
+        in_specs=[pl.BlockSpec(memory_space=pltpu.SMEM)] + [in_vmem] * (1 + len(speeds)),
+        out_specs=in_vmem,
         out_shape=jax.ShapeDtypeStruct((3, lane, full), jnp.float32),
+        scratch_shapes=[pltpu.VMEM((lane, lane), jnp.float32)],
         compiler_params=pltpu.CompilerParams(vmem_limit_bytes=vmem_bytes),
         cost_estimate=pl.CostEstimate(flops=60 * lane * full, bytes_accessed=24 * lane * full, transcendentals=0),
         name="blend_factors",
@@ -628,12 +641,15 @@
 strip = 32
 
 
-def finish_kernel(in_ref, blend_ref, turn_ref, table_ref, out_ref, image_ref, work_ref):
+def finish_kernel(even_ref, odd_ref, blend_ref, turn_ref, table_ref, out_ref, image_ref, work_ref):
     count = len(ref_speeds)
     for j in range(count):
-        values = jnp.concatenate([in_ref[:, j, 0], in_ref[:, j, 1]], axis=2)
-        product = right_product(values.reshape(radix * strip, 2 * lane), table_ref[...])
-        work_ref[j] = product.reshape(radix, strip, 2 * lane)
+        for c, in_ref in enumerate((even_ref, odd_ref)):
+            values = jnp.concatenate([in_ref[:, j, 0], in_ref[:, j, 1]], axis=2)
+            product = right_product(values.reshape(half_radix * strip, 2 * lane), table_ref[...])
+            product = product.reshape(half_radix, strip, 2 * lane)
+            for i in range(half_radix):
+                work_ref[j, 2 * i + c] = product[i]
 
     def rows(index, carry):
         here = pl.ds(pl.multiple_of(index * 8, 8), 8)
@@ -669,13 +685,14 @@
     lax.fori_loop(0, strip // 8, rows, 0, unroll=True)
 
 
-def finish_call(returned, blend):
+def finish_call(even, odd, blend):
     count = len(ref_speeds)
     return pl.pallas_call(
         finish_kernel,
         grid=(lane // strip,),
         in_specs=[
-            pl.BlockSpec((radix, count, 2, strip, lane), lambda g: (0, 0, 0, g, 0)),
+            pl.BlockSpec((half_radix, count, 2, strip, lane), lambda g: (0, 0, 0, g, 0)),
+            pl.BlockSpec((half_radix, count, 2, strip, lane), lambda g: (0, 0, 0, g, 0)),
             pl.BlockSpec((3, strip, full), lambda g: (0, g, 0)),
             pl.BlockSpec((radix, 2, 8, lane), lambda g: (0, 0, 0, 0)),
             pl.BlockSpec((6 * lane, 2 * lane), lambda g: (0, 0)),
@@ -691,53 +708,51 @@
         scratch_shapes=[
             pltpu.VMEM((count, radix, strip, 2 * lane), jnp.float32),
         ],
-        compiler_params=pltpu.CompilerParams(vmem_limit_bytes=vmem_bytes),
+        compiler_params=pltpu.CompilerParams(vmem_limit_bytes=finish_vmem_bytes),
         name="inverse_lines",
-    )(returned, blend, lane_twiddle(1, 1.0 / full), right_table(1))
-
-
-def exchange(values):
-    return lax.all_to_all(values, "slab", split_axis=0, concat_axis=0, tiled=True)
+    )(even, odd, blend, lane_twiddle(1, 1.0 / full), right_table(1))
+
+
+def exchange(values, group):
+    groups = [list(range(begin, begin + group)) for begin in range(0, radix, group)]
+    return lax.all_to_all(values, "slab", split_axis=0, concat_axis=0, tiled=True, axis_index_groups=groups)
 
 
 def partners(distance):
     return [(index, index ^ distance) for index in range(radix)]
 
 
-def speeds_there(velocity):
+def speeds_near(velocity):
     shot, device = lax.axis_index("shot"), lax.axis_index("slab")
-    half = radix // 2
-    other_half = (1 - device // half) * (half * lane)
-    sent = lax.dynamic_slice(velocity[0], (shot * (lane // 2), other_half), (lane // 2, half * lane))
-    return sent
-
-
-def speeds_here(velocity, arrived):
-    shot, device = lax.axis_index("shot"), lax.axis_index("slab")
-    half = radix // 2
-    place = device % half
-    swapped = lax.ppermute(arrived, "shot", [(0, 1), (1, 0)])
-    far = jnp.where(shot == 0, jnp.concatenate([arrived, swapped]), jnp.concatenate([swapped, arrived]))
-    near = lax.dynamic_slice(velocity[0], (0, device // half * (half * lane)), (lane, half * lane))
-    both = jnp.stack([near, far])
     tiles = []
-    for k in range(half):
-        part = lax.dynamic_slice(both, (0, 0, (place ^ k) * lane), (2, lane, lane))
-        tiles.append(lax.ppermute(part, "slab", partners(k)) if k else part)
+    for k in range(half_radix):
+        near = lax.dynamic_slice(velocity[0], (0, (device ^ k) * lane), (lane, lane))
+        beyond = lax.dynamic_slice(velocity[0], (shot * (lane // 2), (device ^ k ^ far) * lane), (lane // 2, lane))
+        both = jnp.concatenate([near, beyond])
+        tiles.append(lax.ppermute(both, "slab", partners(k)) if k else both)
     return tiles
 
 
 def per_device(wavefield, frequencies, velocity, bracket):
-    sent = lines_call(wavefield)
+    even, odd = lines_call(wavefield)
+    velocity, even, odd = lax.optimization_barrier((velocity, even, odd))
+    even = exchange(even, radix)
+    speeds = speeds_near(velocity)
+    beyond = jnp.stack([tile_now[lane:] for tile_now in speeds])
     phase = phase_call(frequencies)
-    arrived = exchange(sent)
-    speed_sent, _, _ = lax.optimization_barrier((speeds_there(velocity), phase, arrived))
-    speed_arrived = lax.ppermute(speed_sent, "slab", partners(radix // 2))
-    fields = rows_call(arrived, phase)
-    speed_arrived, fields = lax.optimization_barrier((speed_arrived, fields))
-    returned = exchange(fields)
-    blend = blend_call(frequencies, bracket, speeds_here(velocity, speed_arrived))
-    propagated, image = finish_call(returned, blend)
+    beyond, phase, even, odd = lax.optimization_barrier((beyond, phase, even, odd))
+    odd = exchange(odd, radix)
+    even = rows_call(0, even, phase)
+    even, odd = lax.optimization_barrier((even, odd))
+    even = exchange(even, half_radix)
+    beyond, _ = lax.optimization_barrier((beyond, odd))
+    beyond = lax.ppermute(beyond, "slab", partners(far))
+    odd = rows_call(1, odd, phase)
+    beyond, even, odd = lax.optimization_barrier((beyond, even, odd))
+    odd = exchange(odd, half_radix)
+    swapped = lax.ppermute(beyond, "shot", [(0, 1), (1, 0)])
+    blend = blend_call(frequencies, bracket, beyond, swapped, *speeds)
+    propagated, image = finish_call(even, odd, blend)
     return propagated, image
 
 

time: 227 us -> 213 us (0.938)
  waiting for transfers between devices: 160 us -> 113 us
  Pallas kernels: 35.2 us -> 51.2 us
  starting transfers between devices: 24.7 us -> 38.8 us
  local copies, waits for them, and re-layouts: 0.69 us -> 3.69 us
    ppermute x9, waiting for transfers between devices: 103 us -> 25.3 us  [the longest x7 20.1 us: speeds_near(): tiles.append(lax.ppermute(both, 'slab', partners(k)) if k else both)]
    all_to_all x2 -> x4, waiting for transfers between devices: 56.9 us -> 87.5 us  [exchange(): lax.all_to_all(values, 'slab', split_axis=0, concat_axis=0, tiled=True, a...]
    all_to_all x2 -> x4, starting transfers between devices: 14.2 us -> 29.1 us  [exchange(): lax.all_to_all(values, 'slab', split_axis=0, concat_axis=0, tiled=True, a...]
    pallas_call x1 -> x2, Pallas kernels: 9.7 us -> 19.6 us  [rows_call(): pl.pallas_call(functools.partial(rows_kernel, c), in_specs=[in_vmem, in_h...]
    pallas_call x1, Pallas kernels: 8.34 us -> 14.5 us  [phase_call(): pl.pallas_call(phase_kernel, in_specs=[pl.BlockSpec(memory_space=pltpu.SM...]
  transfers between devices with their start and end apart: 11 -> 13, of which waited for: 9 -> 9; matrix products, arithmetic and copies ran while one was open for 1% -> 1% of each run, Pallas kernels for 10% -> 18%
where the time goes in v3:
time: 213 us; the launch traced here: 209 us
  waiting for transfers between devices  113 us (53%)
  Pallas kernels  51.2 us (24%)
  starting transfers between devices  38.8 us (18%)
  local copies, waits for them, and re-layouts  3.69 us (2%)
    all_to_all x4, waiting for transfers between devices, exchange(): lax.all_to_all(values, 'slab', split_axis=0, concat_axis=0, tiled=True, a...  87.5 us
    all_to_all x4, starting transfers between devices, exchange(): lax.all_to_all(values, 'slab', split_axis=0, concat_axis=0, tiled=True, a...  29.1 us
    ppermute x7, waiting for transfers between devices, speeds_near(): tiles.append(lax.ppermute(both, 'slab', partners(k)) if k else both)  20.1 us
    pallas_call x2, Pallas kernels, rows_call(): pl.pallas_call(functools.partial(rows_kernel, c), in_specs=[in_vmem, in_h...  19.6 us
    pallas_call x1, Pallas kernels, phase_call(): pl.pallas_call(phase_kernel, in_specs=[pl.BlockSpec(memory_space=pltpu.SM...  14.5 us
    pallas_call x1, Pallas kernels, finish_call(): pl.pallas_call(finish_kernel, grid=(lane // strip,), in_specs=[pl.BlockSp...  8.17 us
    ppermute x7, starting transfers between devices, speeds_near(): tiles.append(lax.ppermute(both, 'slab', partners(k)) if k else both)  6.98 us
    ppermute x1, waiting for transfers between devices, per_device(): swapped = lax.ppermute(beyond, 'shot', [(0, 1), (1, 0)])  5.13 us
  transfers between devices with their start and end apart: 13, of which 9 were waited for; matrix products, arithmetic and copies ran while one was open for 1% of the time, Pallas kernels for 18%

profile of v3, /device:TPU:13, one launch (start us, length us, event | category | flops | bytes accessed | tf_op | source)
XLA Modules:
  0.0 209.5 jit_solution(5401322121722970950)
XLA Ops:
  0.6 0.0 copy-start.2
  0.6 4.3 %forward_lines.1 = (f32[16,2,128,128]{3,2,1,0:T(8,128)}, f32[16,2,128,128]{3,2,1,0:T(8,128)}) custom-call(f32[1,2,128,2048]{3,2,1,0:T(8,128)} %field_ref.1, f32[16,2,8,128]{3,2,1,0:T(8,128)} %constant.57.clone.turn_ref, bf16[768,256]{1,0:T(8,128)(2,1)} %constant.58.clone.table_ref), custom_call_target="tpu_custom_call" | custom-call | tf_op jit(solution)/shard_map/forward_lines/pallas_call | solution.py:381
  5.0 6.6 %all-to-all-start = ((f32[16,2,128,128]{3,2,1,0:T(8,128)}), f32[16,2,128,128]{3,2,1,0:T(8,128)S(1)}, u32[]{:S(2)}, u32[]{:S(2)}) async-start(f32[16,2,128,128]{3,2,1,0:T(8,128)} %get-tuple-element.20), calls=%async_computation | async-start | bytes 4194304 | tf_op jit(solution)/shard_map/all_to_all | solution.py:718
  11.5 0.0 copy-done.2
  11.5 0.7 dynamic-slice_bitcast_fusion.15
  12.2 0.7 dynamic-slice_bitcast_fusion
  12.9 0.4 collective-permute-start
  13.3 0.3 collective-permute-start.1
  13.7 1.6 collective-permute-start.2
  15.3 0.3 collective-permute-start.3
  15.6 1.5 collective-permute-start.4
  17.8 14.5 %phase_factors.1.phase_ref = f32[2,3,2,128,2048]{4,3,2,1,0:T(8,128)} custom-call(f32[1]{0:T(128)S(6)} %copy.17.angular_ref), custom_call_target="tpu_custom_call" | custom-call | flops 94371840 | bytes 12582912 | tf_op jit(solution)/shard_map/phase_factors/pallas_call | solution.py:434
  32.2 0.0 collective-permute-done.refs_1_
  32.3 0.0 copy-start.4
  32.3 0.1 collective-permute-start.5
  32.4 0.0 collective-permute-done.1.refs_2_
  32.4 2.7 %collective-permute-start.6 = (f32[192,128]{1,0:T(8,128)S(1)}, f32[192,128]{1,0:T(8,128)S(1)}, u32[]{:S(2)}, u32[]{:S(2)}) collective-permute-start(f32[192,128]{1,0:T(8,128)S(1)} %pad_maximum_fusion.6), channel_id=1, source_target_pairs={{0,7},{1,6},{2,5},{3,4},{4,3},{5,2},{6,1},{7,0},{8,15},{9,14},{10,... | collective-permute-start | bytes 294920 | tf_op jit(solution)/shard_map/ppermute | solution.py:732
  35.1 0.0 collective-permute-done.2.refs_3_
  35.1 14.0 %collective-permute-done.3.refs_4_ = f32[192,128]{1,0:T(8,128)S(1)} collective-permute-done((f32[192,128]{1,0:T(8,128)S(1)}, f32[192,128]{1,0:T(8,128)S(1)}, u32[]{:S(2)}, u32[]{:S(2)}) %collective-permute-start.3) | collective-permute-done | bytes 98336 | tf_op jit(solution)/shard_map/ppermute | solution.py:732
  49.2 3.0 %collective-permute-done.4.refs_5_ = f32[192,128]{1,0:T(8,128)S(1)} collective-permute-done((f32[192,128]{1,0:T(8,128)S(1)}, f32[192,128]{1,0:T(8,128)S(1)}, u32[]{:S(2)}, u32[]{:S(2)}) %collective-permute-start.4) | collective-permute-done | bytes 98336 | tf_op jit(solution)/shard_map/ppermute | solution.py:732
  52.2 0.9 collective-permute-done.5.refs_6_
  53.2 2.1 %collective-permute-done.6.refs_7_ = f32[192,128]{1,0:T(8,128)S(1)} collective-permute-done((f32[192,128]{1,0:T(8,128)S(1)}, f32[192,128]{1,0:T(8,128)S(1)}, u32[]{:S(2)}, u32[]{:S(2)}) %collective-permute-start.6) | collective-permute-done | bytes 98336 | tf_op jit(solution)/shard_map/ppermute | solution.py:732
  55.3 0.0 copy-done.4
  55.3 0.0 copy-done.5
  55.3 0.0 copy-done.6
  55.3 0.0 copy-done.7
  55.3 0.0 copy-done.8
  55.3 0.0 copy-done.9
  55.3 0.0 copy-start.10
  55.3 0.6 copy-done.10
  56.0 4.4 %all-to-all-done.in_ref = f32[16,2,128,128]{3,2,1,0:T(8,128)S(1)} async-done(((f32[16,2,128,128]{3,2,1,0:T(8,128)}), f32[16,2,128,128]{3,2,1,0:T(8,128)S(1)}, u32[]{:S(2)}, u32[]{:S(2)}) %all-to-all-start) | async-done | bytes 2097184 | tf_op jit(solution)/shard_map/all_to_all | solution.py:718
  60.4 4.3 %all-to-all-start.1 = ((f32[16,2,128,128]{3,2,1,0:T(8,128)}), f32[16,2,128,128]{3,2,1,0:T(8,128)}, u32[]{:S(2)}, u32[]{:S(2)}) async-start(f32[16,2,128,128]{3,2,1,0:T(8,128)} %get-tuple-element.25), calls=%async_computation.1 | async-start | bytes 4194304 | tf_op jit(solution)/shard_map/all_to_all | solution.py:718
  64.7 9.0 %rows_there_and_back.2 = f32[8,3,2,128,128]{4,3,2,1,0:T(8,128)} custom-call(f32[16,2,128,128]{3,2,1,0:T(8,128)S(1)} %all-to-all-done.in_ref, f32[2,3,2,128,2048]{4,3,2,1,0:T(8,128)} %phase_factors.1.phase_ref), custom_call_target="tpu_custom_call" | custom-call | flops 6442450944 | bytes 58720256 | tf_op jit(solution)/shard_map/rows_there_and_back/pallas_call | solution.py:576
  73.8 38.4 %all-to-all-done.1.in_ref = f32[16,2,128,128]{3,2,1,0:T(8,128)} async-done(((f32[16,2,128,128]{3,2,1,0:T(8,128)}), f32[16,2,128,128]{3,2,1,0:T(8,128)}, u32[]{:S(2)}, u32[]{:S(2)}) %all-to-all-start.1) | async-done | bytes 2097184 | tf_op jit(solution)/shard_map/all_to_all | solution.py:718
  112.1 4.1 %all-to-all-start.2 = ((f32[8,3,2,128,128]{4,3,2,1,0:T(8,128)}), f32[8,3,2,128,128]{4,3,2,1,0:T(8,128)S(1)}, u32[]{:S(2)}, u32[]{:S(2)}) async-start(f32[8,3,2,128,128]{4,3,2,1,0:T(8,128)} %rows_there_and_back.2), calls=%async_computation.2 | async-start | bytes 6291456 | tf_op jit(solution)/shard_map/all_to_all | solution.py:718
  116.2 1.5 collective-permute-start.7
  117.7 10.6 %rows_there_and_back.3 = f32[8,3,2,128,128]{4,3,2,1,0:T(8,128)} custom-call(f32[16,2,128,128]{3,2,1,0:T(8,128)} %all-to-all-done.1.in_ref, f32[2,3,2,128,2048]{4,3,2,1,0:T(8,128)} %phase_factors.1.phase_ref), custom_call_target="tpu_custom_call" | custom-call | flops 6442450944 | bytes 58720256 | tf_op jit(solution)/shard_map/rows_there_and_back/pallas_call | solution.py:576
  128.3 0.0 collective-permute-done.7.far_ref
  128.3 22.9 %all-to-all-done.2.even_ref = f32[8,3,2,128,128]{4,3,2,1,0:T(8,128)S(1)} async-done(((f32[8,3,2,128,128]{4,3,2,1,0:T(8,128)}), f32[8,3,2,128,128]{4,3,2,1,0:T(8,128)S(1)}, u32[]{:S(2)}, u32[]{:S(2)}) %all-to-all-start.2) | async-done | bytes 3145760 | tf_op jit(solution)/shard_map/all_to_all | solution.py:718
  151.1 14.2 %all-to-all-start.3 = ((f32[8,3,2,128,128]{4,3,2,1,0:T(8,128)}), f32[8,3,2,128,128]{4,3,2,1,0:T(8,128)}, u32[]{:S(2)}, u32[]{:S(2)}) async-start(f32[8,3,2,128,128]{4,3,2,1,0:T(8,128)} %rows_there_and_back.3), calls=%async_computation.3 | async-start | bytes 6291456 | tf_op jit(solution)/shard_map/all_to_all | solution.py:718
  165.3 1.2 collective-permute-start.8
  166.5 1.5 pad_maximum_fusion.7.refs_0_
  168.0 5.1 %collective-permute-done.8.swapped_ref = f32[8,64,128]{2,1,0:T(8,128)S(1)} collective-permute-done((f32[8,64,128]{2,1,0:T(8,128)}, f32[8,64,128]{2,1,0:T(8,128)S(1)}, u32[]{:S(2)}, u32[]{:S(2)}) %collective-permute-start.8) | collective-permute-done | bytes 262176 | tf_op jit(solution)/shard_map/ppermute | solution.py:753
  173.2 0.7 copy-done.3
  173.9 4.6 %blend_factors.1.blend_ref = f32[3,128,2048]{2,1,0:T(8,128)} custom-call(f32[1]{0:T(128)S(6)} %copy.17.angular_ref, s32[1,128,2048]{2,1,0:T(8,128)} %bracket_ref.1, f32[8,64,128]{2,1,0:T(8,128)} %collective-permute-done.7.far_ref, f32[8,64,128]{2,1,0:T(8,128)} %copy-done.3, f32[192,128]{1,0:T(8,128)} %pad_maximum_fusion.7.refs_0_, f32[192,128]{1,0:T(8,128)} %copy-done.4, ...), custom_call_target="tpu_custom_call" | custom-call | flops 15728640 | bytes 6291456 | tf_op jit(solution)/shard_map/blend_factors/pallas_call | solution.py:629
  178.5 21.9 %all-to-all-done.3.odd_ref = f32[8,3,2,128,128]{4,3,2,1,0:T(8,128)} async-done(((f32[8,3,2,128,128]{4,3,2,1,0:T(8,128)}), f32[8,3,2,128,128]{4,3,2,1,0:T(8,128)}, u32[]{:S(2)}, u32[]{:S(2)}) %all-to-all-start.3) | async-done | bytes 3145760 | tf_op jit(solution)/shard_map/all_to_all | solution.py:718
  200.4 0.9 copy-done.1
  201.3 8.2 %inverse_lines.1 = (f32[1,2,128,2048]{3,2,1,0:T(8,128)}, f32[1,128,2048]{2,1,0:T(8,128)}) custom-call(f32[8,3,2,128,128]{4,3,2,1,0:T(8,128)S(1)} %all-to-all-done.2.even_ref, f32[8,3,2,128,128]{4,3,2,1,0:T(8,128)} %all-to-all-done.3.odd_ref, f32[3,128,2048]{2,1,0:T(8,128)} %blend_factors.1.blend_ref, f32[16,2,8,128]{3,2,1,0:T(8,128)S(1)} %copy-done.1, ...), custom_call_target="tpu_custom_call" | custom-call | tf_op jit(solution)/shard_map/inverse_lines/pallas_call | solution.py:690
  (23 shorter events, 0.1 us)
Async XLA Ops:
  0.6 10.9 %copy-start.2 = (f32[1,128,2048]{2,1,0:T(8,128)S(1)}, f32[1,128,2048]{2,1,0:T(8,128)}, u32[]{:S(2)}) copy-start(f32[1,128,2048]{2,1,0:T(8,128)} %param.10) | copy-start | bytes 3145732
  5.0 55.4 %all-to-all-start = ((f32[16,2,128,128]{3,2,1,0:T(8,128)}), f32[16,2,128,128]{3,2,1,0:T(8,128)S(1)}, u32[]{:S(2)}, u32[]{:S(2)}) async-start(f32[16,2,128,128]{3,2,1,0:T(8,128)} %get-tuple-element.20), calls=%async_computation | async-start | bytes 4194304 | tf_op jit(solution)/shard_map/all_to_all | solution.py:718
  12.9 19.3 %collective-permute-start = (f32[192,128]{1,0:T(8,128)S(1)}, f32[192,128]{1,0:T(8,128)S(1)}, u32[]{:S(2)}, u32[]{:S(2)}) collective-permute-start(f32[192,128]{1,0:T(8,128)S(1)} %pad_maximum_fusion), channel_id=1, source_target_pairs={{0,1},{1,0},{2,3},{3,2},{4,5},{5,4},{6,7},{7,6},{8,9},{9,8},{10,11... | collective-permute-start | bytes 294920 | tf_op jit(solution)/shard_map/ppermute | solution.py:732
  13.3 19.1 %collective-permute-start.1 = (f32[192,128]{1,0:T(8,128)S(1)}, f32[192,128]{1,0:T(8,128)S(1)}, u32[]{:S(2)}, u32[]{:S(2)}) collective-permute-start(f32[192,128]{1,0:T(8,128)S(1)} %pad_maximum_fusion.1), channel_id=1, source_target_pairs={{0,2},{1,3},{2,0},{3,1},{4,6},{5,7},{6,4},{7,5},{8,10},{9,11},{10,... | collective-permute-start | bytes 294920 | tf_op jit(solution)/shard_map/ppermute | solution.py:732
  13.7 21.4 %collective-permute-start.2 = (f32[192,128]{1,0:T(8,128)S(1)}, f32[192,128]{1,0:T(8,128)S(1)}, u32[]{:S(2)}, u32[]{:S(2)}) collective-permute-start(f32[192,128]{1,0:T(8,128)S(1)} %pad_maximum_fusion.2), channel_id=1, source_target_pairs={{0,3},{1,2},{2,1},{3,0},{4,7},{5,6},{6,5},{7,4},{8,11},{9,10},{10,... | collective-permute-start | bytes 294920 | tf_op jit(solution)/shard_map/ppermute | solution.py:732
  15.3 33.9 %collective-permute-start.3 = (f32[192,128]{1,0:T(8,128)S(1)}, f32[192,128]{1,0:T(8,128)S(1)}, u32[]{:S(2)}, u32[]{:S(2)}) collective-permute-start(f32[192,128]{1,0:T(8,128)S(1)} %pad_maximum_fusion.3), channel_id=1, source_target_pairs={{0,4},{1,5},{2,6},{3,7},{4,0},{5,1},{6,2},{7,3},{8,12},{9,13},{10,... | collective-permute-start | bytes 294920 | tf_op jit(solution)/shard_map/ppermute | solution.py:732
  15.6 36.6 %collective-permute-start.4 = (f32[192,128]{1,0:T(8,128)S(1)}, f32[192,128]{1,0:T(8,128)S(1)}, u32[]{:S(2)}, u32[]{:S(2)}) collective-permute-start(f32[192,128]{1,0:T(8,128)S(1)} %pad_maximum_fusion.4), channel_id=1, source_target_pairs={{0,5},{1,4},{2,7},{3,6},{4,1},{5,0},{6,3},{7,2},{8,13},{9,12},{10,... | collective-permute-start | bytes 294920 | tf_op jit(solution)/shard_map/ppermute | solution.py:732
  32.3 23.0 %copy-start.4 = (f32[192,128]{1,0:T(8,128)}, f32[192,128]{1,0:T(8,128)S(1)}, u32[]{:S(2)}) copy-start(f32[192,128]{1,0:T(8,128)S(1)} %collective-permute-done.refs_1_) | copy-start | bytes 294916
  32.3 20.9 %collective-permute-start.5 = (f32[192,128]{1,0:T(8,128)S(1)}, f32[192,128]{1,0:T(8,128)S(1)}, u32[]{:S(2)}, u32[]{:S(2)}) collective-permute-start(f32[192,128]{1,0:T(8,128)S(1)} %pad_maximum_fusion.5), channel_id=1, source_target_pairs={{0,6},{1,7},{2,4},{3,5},{4,2},{5,3},{6,0},{7,1},{8,14},{9,15},{10,... | collective-permute-start | bytes 294920 | tf_op jit(solution)/shard_map/ppermute | solution.py:732
  32.4 22.9 %copy-start.5 = (f32[192,128]{1,0:T(8,128)}, f32[192,128]{1,0:T(8,128)S(1)}, u32[]{:S(2)}) copy-start(f32[192,128]{1,0:T(8,128)S(1)} %collective-permute-done.1.refs_2_) | copy-start | bytes 294916
  32.4 22.9 %collective-permute-start.6 = (f32[192,128]{1,0:T(8,128)S(1)}, f32[192,128]{1,0:T(8,128)S(1)}, u32[]{:S(2)}, u32[]{:S(2)}) collective-permute-start(f32[192,128]{1,0:T(8,128)S(1)} %pad_maximum_fusion.6), channel_id=1, source_target_pairs={{0,7},{1,6},{2,5},{3,4},{4,3},{5,2},{6,1},{7,0},{8,15},{9,14},{10,... | collective-permute-start | bytes 294920 | tf_op jit(solution)/shard_map/ppermute | solution.py:732
  35.1 20.2 %copy-start.6 = (f32[192,128]{1,0:T(8,128)}, f32[192,128]{1,0:T(8,128)S(1)}, u32[]{:S(2)}) copy-start(f32[192,128]{1,0:T(8,128)S(1)} %collective-permute-done.2.refs_3_) | copy-start | bytes 294916
  49.2 6.1 %copy-start.7 = (f32[192,128]{1,0:T(8,128)}, f32[192,128]{1,0:T(8,128)S(1)}, u32[]{:S(2)}) copy-start(f32[192,128]{1,0:T(8,128)S(1)} %collective-permute-done.3.refs_4_) | copy-start | bytes 294916
  52.2 3.1 %copy-start.8 = (f32[192,128]{1,0:T(8,128)}, f32[192,128]{1,0:T(8,128)S(1)}, u32[]{:S(2)}) copy-start(f32[192,128]{1,0:T(8,128)S(1)} %collective-permute-done.4.refs_5_) | copy-start | bytes 294916
  53.2 2.1 %copy-start.9 = (f32[192,128]{1,0:T(8,128)}, f32[192,128]{1,0:T(8,128)S(1)}, u32[]{:S(2)}) copy-start(f32[192,128]{1,0:T(8,128)S(1)} %collective-permute-done.5.refs_6_) | copy-start | bytes 294916
  55.3 0.7 copy-start.10
  60.4 51.8 %all-to-all-start.1 = ((f32[16,2,128,128]{3,2,1,0:T(8,128)}), f32[16,2,128,128]{3,2,1,0:T(8,128)}, u32[]{:S(2)}, u32[]{:S(2)}) async-start(f32[16,2,128,128]{3,2,1,0:T(8,128)} %get-tuple-element.25), calls=%async_computation.1 | async-start | bytes 4194304 | tf_op jit(solution)/shard_map/all_to_all | solution.py:718
  112.1 39.0 %all-to-all-start.2 = ((f32[8,3,2,128,128]{4,3,2,1,0:T(8,128)}), f32[8,3,2,128,128]{4,3,2,1,0:T(8,128)S(1)}, u32[]{:S(2)}, u32[]{:S(2)}) async-start(f32[8,3,2,128,128]{4,3,2,1,0:T(8,128)} %rows_there_and_back.2), calls=%async_computation.2 | async-start | bytes 6291456 | tf_op jit(solution)/shard_map/all_to_all | solution.py:718
  116.2 12.1 %collective-permute-start.7 = (f32[8,64,128]{2,1,0:T(8,128)S(1)}, f32[8,64,128]{2,1,0:T(8,128)}, u32[]{:S(2)}, u32[]{:S(2)}) collective-permute-start(f32[8,64,128]{2,1,0:T(8,128)S(1)} %fusion), channel_id=1, source_target_pairs={{0,12},{1,13},{2,14},{3,15},{4,8},{5,9},{6,10},{7,11},{8,4},{9,5},... | collective-permute-start | bytes 786440 | tf_op jit(solution)/shard_map/ppermute | solution.py:749
  151.1 49.2 %all-to-all-start.3 = ((f32[8,3,2,128,128]{4,3,2,1,0:T(8,128)}), f32[8,3,2,128,128]{4,3,2,1,0:T(8,128)}, u32[]{:S(2)}, u32[]{:S(2)}) async-start(f32[8,3,2,128,128]{4,3,2,1,0:T(8,128)} %rows_there_and_back.3), calls=%async_computation.3 | async-start | bytes 6291456 | tf_op jit(solution)/shard_map/all_to_all | solution.py:718
  165.3 35.0 %copy-start = (bf16[768,256]{1,0:T(8,128)(2,1)S(1)}, bf16[768,256]{1,0:T(8,128)(2,1)}, u32[]{:S(2)}) copy-start(bf16[768,256]{1,0:T(8,128)(2,1)} %constant.60.clone.table_ref) | copy-start | bytes 1179652
  165.3 7.8 %collective-permute-start.8 = (f32[8,64,128]{2,1,0:T(8,128)}, f32[8,64,128]{2,1,0:T(8,128)S(1)}, u32[]{:S(2)}, u32[]{:S(2)}) collective-permute-start(f32[8,64,128]{2,1,0:T(8,128)} %collective-permute-done.7.far_ref), channel_id=1, source_target_pairs={{0,16},{16,0},{1,17},{17,1},{2,18},{18,2},{3,19},{19,3},{4,20},{20... | collective-permute-start | bytes 786440 | tf_op jit(solution)/shard_map/ppermute | solution.py:753
  173.2 0.7 copy-start.3
  200.4 0.9 copy-start.1

commit v4 on v3

--- a/solution.py
+++ b/solution.py
@@ -231,7 +231,7 @@
 full = radix * lane
 row_block = 64
 half_radix = radix // 2
-far = radix // 2 + radix // 4
+far = half_radix
 blocks = lane // row_block
 piece = 2 * row_block
 vmem_bytes = 56 * 1024 * 1024
@@ -355,41 +355,44 @@
     return slice(index * lane, (index + 1) * lane)
 
 
-def lines_kernel(field_ref, turn_ref, table_ref, even_ref, odd_ref, work_ref):
+def lines_kernel(c, field_ref, turn_ref, table_ref, out_ref, work_ref):
     def rows(index, carry):
         here = pl.ds(pl.multiple_of(index * 8, 8), 8)
         parts = sixteen(
             [(field_ref[0, 0, here, tile(j)], field_ref[0, 1, here, tile(j)]) for j in range(radix)], -1
         )
-        for k in range(radix):
+        for i in range(half_radix):
+            k = 2 * i + c
             re, im = times(parts[k], (turn_ref[k, 0], turn_ref[k, 1]))
-            work_ref[k, here, 0:lane] = re
-            work_ref[k, here, lane : 2 * lane] = im
+            work_ref[i, here, 0:lane] = re
+            work_ref[i, here, lane : 2 * lane] = im
         return carry
 
     lax.fori_loop(0, row_block // 8, rows, 0, unroll=True)
-    lines = right_product(work_ref[...].reshape(radix * row_block, 2 * lane), table_ref[...])
-    for k in range(radix):
-        block = lines[k * row_block : (k + 1) * row_block]
+    lines = right_product(work_ref[...].reshape(half_radix * row_block, 2 * lane), table_ref[...])
+    for i in range(half_radix):
+        block = lines[i * row_block : (i + 1) * row_block]
         for half in range(2):
-            out_ref = (even_ref, odd_ref)[k % 2]
-            out_ref[half * half_radix + k // 2, 0, 0:row_block] = block[:, 0:lane]
-            out_ref[half * half_radix + k // 2, 0, row_block : 2 * row_block] = block[:, lane : 2 * lane]
-
-
-def lines_call(wavefield):
+            out_ref[half * half_radix + i, 0, 0:row_block] = block[:, 0:lane]
+            out_ref[half * half_radix + i, 0, row_block : 2 * row_block] = block[:, lane : 2 * lane]
+
+
+def lines_call(c, wavefield):
     return pl.pallas_call(
-        lines_kernel,
+        functools.partial(lines_kernel, c),
         grid=(blocks,),
         in_specs=[
             pl.BlockSpec((1, 2, row_block, full), lambda g: (0, 0, g, 0)),
             pl.BlockSpec((radix, 2, 8, lane), lambda g: (0, 0, 0, 0)),
             pl.BlockSpec((6 * lane, 2 * lane), lambda g: (0, 0)),
         ],
-        out_specs=[pl.BlockSpec((radix, 1, piece, lane), lambda g: (0, g, 0, 0))] * 2,
-        out_shape=[jax.ShapeDtypeStruct((radix, blocks, piece, lane), jnp.float32)] * 2,
-        scratch_shapes=[pltpu.VMEM((radix, row_block, 2 * lane), jnp.float32)],
+        out_specs=pl.BlockSpec((radix, 1, piece, lane), lambda g: (0, g, 0, 0)),
+        out_shape=jax.ShapeDtypeStruct((radix, blocks, piece, lane), jnp.float32),
+        scratch_shapes=[pltpu.VMEM((half_radix, row_block, 2 * lane), jnp.float32)],
         compiler_params=pltpu.CompilerParams(vmem_limit_bytes=vmem_bytes),
+        cost_estimate=pl.CostEstimate(
+            flops=2 * lane * full * 6 * lane * 2, bytes_accessed=16 * lane * full, transcendentals=0
+        ),
         name="forward_lines",
     )(wavefield, lane_twiddle(-1, 1.0), right_table(-1))
 
@@ -449,18 +452,35 @@
     return horner(circle_cos, square), angle * horner(circle_sin, square)
 
 
-def build_matrices(ahead_table_ref, back_table_ref):
+def put_matrix(table_ref, cosine, sine, turned_over):
+    for top, blocks_now in enumerate(((cosine, sine), (-sine, cosine))):
+        for place, values in enumerate(blocks_now):
+            upper, lower = halves(values)
+            for third, part in enumerate((upper, upper, lower)):
+                if turned_over:
+                    table_ref[tile(place), tile(2 * third + top)] = part
+                else:
+                    table_ref[tile(2 * third + top), tile(place)] = part
+
+
+def unit_matrix():
     row = lax.broadcasted_iota(jnp.int32, (lane, lane), 0)
     column = lax.broadcasted_iota(jnp.int32, (lane, lane), 1)
-    cosine, sine = circle(row * column, lane)
-    for table_ref, direction, scale in ((ahead_table_ref, -1.0, 1.0), (back_table_ref, 1.0, 1.0 / full)):
-        cos_now, sin_now = cosine * scale, sine * (direction * scale)
-        for top, blocks_now in enumerate(((cos_now, -sin_now), (sin_now, cos_now))):
-            here = slice(top * lane, (top + 1) * lane)
-            for place, values in enumerate(blocks_now):
-                upper, lower = halves(values)
-                for third, part in enumerate((upper, upper, lower)):
-                    table_ref[here, tile(2 * third + place)] = part
+    return circle(row * column, lane)
+
+
+def build_matrices(ahead_table_ref, back_table_ref):
+    cosine, sine = unit_matrix()
+    put_matrix(ahead_table_ref, cosine, -sine, True)
+    put_matrix(back_table_ref, cosine * (1.0 / full), sine * (1.0 / full), True)
+
+
+def build_turns(turn_ref, direction, scale):
+    for k in range(radix):
+        place = lax.broadcasted_iota(jnp.int32, (8, lane), 1)
+        cosine, sine = circle(place * k, full)
+        turn_ref[k, 0] = cosine * scale
+        turn_ref[k, 1] = sine * (direction * scale)
 
 
 def rows_kernel(
@@ -641,8 +661,14 @@
 strip = 32
 
 
-def finish_kernel(even_ref, odd_ref, blend_ref, turn_ref, table_ref, out_ref, image_ref, work_ref):
+def finish_kernel(even_ref, odd_ref, blend_ref, out_ref, image_ref, work_ref, turn_ref, table_ref):
     count = len(ref_speeds)
+
+    @pl.when(pl.program_id(0) == 0)
+    def _():
+        build_turns(turn_ref, 1.0, 1.0 / full)
+        put_matrix(table_ref, *unit_matrix(), False)
+
     for j in range(count):
         for c, in_ref in enumerate((even_ref, odd_ref)):
             values = jnp.concatenate([in_ref[:, j, 0], in_ref[:, j, 1]], axis=2)
@@ -694,8 +720,6 @@
             pl.BlockSpec((half_radix, count, 2, strip, lane), lambda g: (0, 0, 0, g, 0)),
             pl.BlockSpec((half_radix, count, 2, strip, lane), lambda g: (0, 0, 0, g, 0)),
             pl.BlockSpec((3, strip, full), lambda g: (0, g, 0)),
-            pl.BlockSpec((radix, 2, 8, lane), lambda g: (0, 0, 0, 0)),
-            pl.BlockSpec((6 * lane, 2 * lane), lambda g: (0, 0)),
         ],
         out_specs=[
             pl.BlockSpec((1, 2, strip, full), lambda g: (0, 0, g, 0)),
@@ -707,10 +731,12 @@
         ],
         scratch_shapes=[
             pltpu.VMEM((count, radix, strip, 2 * lane), jnp.float32),
+            pltpu.VMEM((radix, 2, 8, lane), jnp.float32),
+            pltpu.VMEM((6 * lane, 2 * lane), jnp.bfloat16),
         ],
         compiler_params=pltpu.CompilerParams(vmem_limit_bytes=finish_vmem_bytes),
         name="inverse_lines",
-    )(even, odd, blend, lane_twiddle(1, 1.0 / full), right_table(1))
+    )(even, odd, blend)
 
 
 def exchange(values, group):
@@ -734,9 +760,10 @@
 
 
 def per_device(wavefield, frequencies, velocity, bracket):
-    even, odd = lines_call(wavefield)
-    velocity, even, odd = lax.optimization_barrier((velocity, even, odd))
+    even = lines_call(0, wavefield)
+    velocity, even, wavefield = lax.optimization_barrier((velocity, even, wavefield))
     even = exchange(even, radix)
+    odd = lines_call(1, wavefield)
     speeds = speeds_near(velocity)
     beyond = jnp.stack([tile_now[lane:] for tile_now in speeds])
     phase = phase_call(frequencies)

time: 213 us -> 209 us (0.981)
  starting transfers between devices: 38.8 us -> 30.3 us
  Pallas kernels: 51.2 us -> 53.7 us
  local copies, waits for them, and re-layouts: 3.69 us -> 5.93 us
    ppermute x1, waiting for transfers between devices: 0.01 us -> 29.7 us  [per_device(): beyond = lax.ppermute(beyond, 'slab', partners(far))]
    all_to_all x4, waiting for transfers between devices: 87.5 us -> 65.3 us  [exchange(): lax.all_to_all(values, 'slab', split_axis=0, concat_axis=0, tiled=True, a...]
    all_to_all x4, starting transfers between devices: 29.1 us -> 19.8 us  [exchange(): lax.all_to_all(values, 'slab', split_axis=0, concat_axis=0, tiled=True, a...]
    ppermute x7, waiting for transfers between devices: 20.1 us -> 13.7 us  [speeds_near(): tiles.append(lax.ppermute(both, 'slab', partners(k)) if k else both)]
    pallas_call x1 -> x2, Pallas kernels: 4.34 us -> 6.58 us  [lines_call(): pl.pallas_call(functools.partial(lines_kernel, c), grid=(blocks,), in_spe...]
    unnamed x28 -> x26, local copies, waits for them, and re-layouts: 2.31 us -> 4.55 us
  transfers between devices with their start and end apart: 13 -> 13, of which waited for: 9 -> 9; matrix products, arithmetic and copies ran while one was open for 1% -> 3% of each run, Pallas kernels for 18% -> 20%
where the time goes in v4:
time: 209 us; the launch traced here: 206 us
  waiting for transfers between devices  114 us (55%)
  Pallas kernels  53.7 us (26%)
  starting transfers between devices  30.3 us (14%)
  local copies, waits for them, and re-layouts  5.93 us (3%)
    all_to_all x4, waiting for transfers between devices, exchange(): lax.all_to_all(values, 'slab', split_axis=0, concat_axis=0, tiled=True, a...  65.3 us
    ppermute x1, waiting for transfers between devices, per_device(): beyond = lax.ppermute(beyond, 'slab', partners(far))  29.7 us
    all_to_all x4, starting transfers between devices, exchange(): lax.all_to_all(values, 'slab', split_axis=0, concat_axis=0, tiled=True, a...  19.8 us
    pallas_call x2, Pallas kernels, rows_call(): pl.pallas_call(functools.partial(rows_kernel, c), in_specs=[in_vmem, in_h...  19.6 us
    pallas_call x1, Pallas kernels, phase_call(): pl.pallas_call(phase_kernel, in_specs=[pl.BlockSpec(memory_space=pltpu.SM...  14.5 us
    ppermute x7, waiting for transfers between devices, speeds_near(): tiles.append(lax.ppermute(both, 'slab', partners(k)) if k else both)  13.7 us
    pallas_call x1, Pallas kernels, finish_call(): pl.pallas_call(finish_kernel, grid=(lane // strip,), in_specs=[pl.BlockSp...  8.43 us
    ppermute x7, starting transfers between devices, speeds_near(): tiles.append(lax.ppermute(both, 'slab', partners(k)) if k else both)  6.92 us
  transfers between devices with their start and end apart: 13, of which 9 were waited for; matrix products, arithmetic and copies ran while one was open for 3% of the time, Pallas kernels for 20%

profile of v4, /device:TPU:13, one launch (start us, length us, event | category | flops | bytes accessed | tf_op | source)
XLA Modules:
  0.0 206.1 jit_solution(18143247475190069238)
XLA Ops:
  0.6 3.2 %forward_lines.2 = f32[16,2,128,128]{3,2,1,0:T(8,128)} custom-call(f32[1,2,128,2048]{3,2,1,0:T(8,128)} %field_ref.2, f32[16,2,8,128]{3,2,1,0:T(8,128)} %constant.53.clone.turn_ref, bf16[768,256]{1,0:T(8,128)(2,1)} %constant.54.clone.table_ref), custom_call_target="tpu_custom_call" | custom-call | flops 805306368 | bytes 4194304 | tf_op jit(solution)/shard_map/forward_lines/pallas_call | solution.py:381
  3.9 6.7 %all-to-all-start = ((f32[16,2,128,128]{3,2,1,0:T(8,128)}), f32[16,2,128,128]{3,2,1,0:T(8,128)S(1)}, u32[]{:S(2)}, u32[]{:S(2)}) async-start(f32[16,2,128,128]{3,2,1,0:T(8,128)} %forward_lines.2), calls=%async_computation | async-start | bytes 4194304 | tf_op jit(solution)/shard_map/all_to_all | solution.py:744
  10.6 0.7 dynamic-slice_bitcast_fusion.15
  11.2 0.1 dynamic-slice_bitcast_fusion
  11.3 0.4 collective-permute-start
  11.8 0.3 collective-permute-start.1
  12.1 1.6 collective-permute-start.2
  13.7 0.3 collective-permute-start.3
  14.1 1.5 collective-permute-start.4
  16.2 14.5 %phase_factors.1.phase_ref = f32[2,3,2,128,2048]{4,3,2,1,0:T(8,128)} custom-call(f32[1]{0:T(128)S(6)} %copy.17.angular_ref), custom_call_target="tpu_custom_call" | custom-call | flops 94371840 | bytes 12582912 | tf_op jit(solution)/shard_map/phase_factors/pallas_call | solution.py:437
  30.7 3.3 %forward_lines.3 = f32[16,2,128,128]{3,2,1,0:T(8,128)} custom-call(f32[1,2,128,2048]{3,2,1,0:T(8,128)} %field_ref.2, f32[16,2,8,128]{3,2,1,0:T(8,128)} %constant.53.clone.turn_ref, bf16[768,256]{1,0:T(8,128)(2,1)} %constant.54.clone.table_ref), custom_call_target="tpu_custom_call" | custom-call | flops 805306368 | bytes 4194304 | tf_op jit(solution)/shard_map/forward_lines/pallas_call | solution.py:381
  34.0 0.0 collective-permute-done.refs_1_
  34.0 0.1 collective-permute-start.5
  34.2 0.6 fusion.6
  34.8 0.0 collective-permute-done.1.refs_2_
  34.8 2.6 %collective-permute-start.6 = (f32[192,128]{1,0:T(8,128)S(1)}, f32[192,128]{1,0:T(8,128)S(1)}, u32[]{:S(2)}, u32[]{:S(2)}) collective-permute-start(f32[192,128]{1,0:T(8,128)S(1)} %pad_maximum_fusion.6), channel_id=1, source_target_pairs={{0,7},{1,6},{2,5},{3,4},{4,3},{5,2},{6,1},{7,0},{8,15},{9,14},{10,... | collective-permute-start | bytes 294920 | tf_op jit(solution)/shard_map/ppermute | solution.py:758
  37.4 0.6 fusion.5
  38.0 0.0 collective-permute-done.2.refs_3_
  38.0 0.6 fusion.4
  38.7 9.5 %collective-permute-done.3.refs_4_ = f32[192,128]{1,0:T(8,128)S(1)} collective-permute-done((f32[192,128]{1,0:T(8,128)S(1)}, f32[192,128]{1,0:T(8,128)S(1)}, u32[]{:S(2)}, u32[]{:S(2)}) %collective-permute-start.3) | collective-permute-done | bytes 98336 | tf_op jit(solution)/shard_map/ppermute | solution.py:758
  48.2 0.6 fusion.3
  48.8 2.4 %collective-permute-done.4.refs_5_ = f32[192,128]{1,0:T(8,128)S(1)} collective-permute-done((f32[192,128]{1,0:T(8,128)S(1)}, f32[192,128]{1,0:T(8,128)S(1)}, u32[]{:S(2)}, u32[]{:S(2)}) %collective-permute-start.4) | collective-permute-done | bytes 98336 | tf_op jit(solution)/shard_map/ppermute | solution.py:758
  51.2 0.6 fusion.2
  51.9 0.3 collective-permute-done.5.refs_6_
  52.2 0.6 fusion.1
  52.8 1.5 collective-permute-done.6.refs_7_
  54.3 0.6 fusion
  54.9 4.4 %all-to-all-done.in_ref = f32[16,2,128,128]{3,2,1,0:T(8,128)S(1)} async-done(((f32[16,2,128,128]{3,2,1,0:T(8,128)}), f32[16,2,128,128]{3,2,1,0:T(8,128)S(1)}, u32[]{:S(2)}, u32[]{:S(2)}) %all-to-all-start) | async-done | bytes 2097184 | tf_op jit(solution)/shard_map/all_to_all | solution.py:744
  59.4 4.3 %all-to-all-start.1 = ((f32[16,2,128,128]{3,2,1,0:T(8,128)}), f32[16,2,128,128]{3,2,1,0:T(8,128)}, u32[]{:S(2)}, u32[]{:S(2)}) async-start(f32[16,2,128,128]{3,2,1,0:T(8,128)} %forward_lines.3), calls=%async_computation.1 | async-start | bytes 4194304 | tf_op jit(solution)/shard_map/all_to_all | solution.py:744
  63.7 9.0 %rows_there_and_back.2 = f32[8,3,2,128,128]{4,3,2,1,0:T(8,128)} custom-call(f32[16,2,128,128]{3,2,1,0:T(8,128)S(1)} %all-to-all-done.in_ref, f32[2,3,2,128,2048]{4,3,2,1,0:T(8,128)} %phase_factors.1.phase_ref), custom_call_target="tpu_custom_call" | custom-call | flops 6442450944 | bytes 58720256 | tf_op jit(solution)/shard_map/rows_there_and_back/pallas_call | solution.py:596
  72.7 0.0 copy-done.3
  72.7 0.0 copy-done.4
  72.8 0.0 copy-done.5
  72.8 0.0 copy-done.6
  72.8 38.4 %all-to-all-done.1.in_ref = f32[16,2,128,128]{3,2,1,0:T(8,128)} async-done(((f32[16,2,128,128]{3,2,1,0:T(8,128)}), f32[16,2,128,128]{3,2,1,0:T(8,128)}, u32[]{:S(2)}, u32[]{:S(2)}) %all-to-all-start.1) | async-done | bytes 2097184 | tf_op jit(solution)/shard_map/all_to_all | solution.py:744
  111.2 4.1 %all-to-all-start.2 = ((f32[8,3,2,128,128]{4,3,2,1,0:T(8,128)}), f32[8,3,2,128,128]{4,3,2,1,0:T(8,128)S(1)}, u32[]{:S(2)}, u32[]{:S(2)}) async-start(f32[8,3,2,128,128]{4,3,2,1,0:T(8,128)} %rows_there_and_back.2), calls=%async_computation.2 | async-start | bytes 6291456 | tf_op jit(solution)/shard_map/all_to_all | solution.py:744
  115.2 2.4 %collective-permute-start.7 = (f32[8,64,128]{2,1,0:T(8,128)}, f32[8,64,128]{2,1,0:T(8,128)S(1)}, u32[]{:S(2)}, u32[]{:S(2)}) collective-permute-start(f32[8,64,128]{2,1,0:T(8,128)} %fusion), channel_id=1, source_target_pairs={{0,8},{1,9},{2,10},{3,11},{4,12},{5,13},{6,14},{7,15},{8,0},{9,1},... | collective-permute-start | bytes 786440 | tf_op jit(solution)/shard_map/ppermute | solution.py:776
  117.6 10.6 %rows_there_and_back.3 = f32[8,3,2,128,128]{4,3,2,1,0:T(8,128)} custom-call(f32[16,2,128,128]{3,2,1,0:T(8,128)} %all-to-all-done.1.in_ref, f32[2,3,2,128,2048]{4,3,2,1,0:T(8,128)} %phase_factors.1.phase_ref), custom_call_target="tpu_custom_call" | custom-call | flops 6442450944 | bytes 58720256 | tf_op jit(solution)/shard_map/rows_there_and_back/pallas_call | solution.py:596
  128.2 29.7 %collective-permute-done.7.far_ref = f32[8,64,128]{2,1,0:T(8,128)S(1)} collective-permute-done((f32[8,64,128]{2,1,0:T(8,128)}, f32[8,64,128]{2,1,0:T(8,128)S(1)}, u32[]{:S(2)}, u32[]{:S(2)}) %collective-permute-start.7) | collective-permute-done | bytes 262176 | tf_op jit(solution)/shard_map/ppermute | solution.py:776
  157.9 0.0 all-to-all-done.2.even_ref
  157.9 4.7 %all-to-all-start.3 = ((f32[8,3,2,128,128]{4,3,2,1,0:T(8,128)}), f32[8,3,2,128,128]{4,3,2,1,0:T(8,128)}, u32[]{:S(2)}, u32[]{:S(2)}) async-start(f32[8,3,2,128,128]{4,3,2,1,0:T(8,128)} %rows_there_and_back.3), calls=%async_computation.3 | async-start | bytes 6291456 | tf_op jit(solution)/shard_map/all_to_all | solution.py:744
  162.6 1.2 collective-permute-start.8
  163.9 0.6 pad_maximum_fusion.7.refs_0_
  164.5 5.4 %collective-permute-done.8.swapped_ref = f32[8,64,128]{2,1,0:T(8,128)S(1)} collective-permute-done((f32[8,64,128]{2,1,0:T(8,128)S(1)}, f32[8,64,128]{2,1,0:T(8,128)S(1)}, u32[]{:S(2)}, u32[]{:S(2)}) %collective-permute-start.8) | collective-permute-done | bytes 262176 | tf_op jit(solution)/shard_map/ppermute | solution.py:780
  169.9 0.7 copy-done.2
  170.6 4.6 %blend_factors.1.blend_ref = f32[3,128,2048]{2,1,0:T(8,128)} custom-call(f32[1]{0:T(128)S(6)} %copy.17.angular_ref, s32[1,128,2048]{2,1,0:T(8,128)} %bracket_ref.1, f32[8,64,128]{2,1,0:T(8,128)} %copy-done.1, f32[8,64,128]{2,1,0:T(8,128)} %copy-done.2, f32[192,128]{1,0:T(8,128)} %pad_maximum_fusion.7.refs_0_, f32[192,128]{1,0:T(8,128)} %copy-done.3, ...), custom_call_target="tpu_custom_call" | custom-call | flops 15728640 | bytes 6291456 | tf_op jit(solution)/shard_map/blend_factors/pallas_call | solution.py:649
  175.3 22.4 %all-to-all-done.3.odd_ref = f32[8,3,2,128,128]{4,3,2,1,0:T(8,128)} async-done(((f32[8,3,2,128,128]{4,3,2,1,0:T(8,128)}), f32[8,3,2,128,128]{4,3,2,1,0:T(8,128)}, u32[]{:S(2)}, u32[]{:S(2)}) %all-to-all-start.3) | async-done | bytes 3145760 | tf_op jit(solution)/shard_map/all_to_all | solution.py:744
  197.7 8.4 %inverse_lines.1 = (f32[1,2,128,2048]{3,2,1,0:T(8,128)}, f32[1,128,2048]{2,1,0:T(8,128)}) custom-call(f32[8,3,2,128,128]{4,3,2,1,0:T(8,128)S(1)} %all-to-all-done.2.even_ref, f32[8,3,2,128,128]{4,3,2,1,0:T(8,128)} %all-to-all-done.3.odd_ref, f32[3,128,2048]{2,1,0:T(8,128)} %blend_factors.1.blend_ref), custom_call_target="tpu_custom_call" | custom-call | tf_op jit(solution)/shard_map/inverse_lines/pallas_call | solution.py:716
  (22 shorter events, 0.1 us)
Async XLA Ops:
  3.9 6.7 %copy-start = (f32[1,128,2048]{2,1,0:T(8,128)S(1)}, f32[1,128,2048]{2,1,0:T(8,128)}, u32[]{:S(2)}) copy-start(f32[1,128,2048]{2,1,0:T(8,128)} %param.10) | copy-start | bytes 3145732
  3.9 55.5 %all-to-all-start = ((f32[16,2,128,128]{3,2,1,0:T(8,128)}), f32[16,2,128,128]{3,2,1,0:T(8,128)S(1)}, u32[]{:S(2)}, u32[]{:S(2)}) async-start(f32[16,2,128,128]{3,2,1,0:T(8,128)} %forward_lines.2), calls=%async_computation | async-start | bytes 4194304 | tf_op jit(solution)/shard_map/all_to_all | solution.py:744
  11.3 22.7 %collective-permute-start = (f32[192,128]{1,0:T(8,128)S(1)}, f32[192,128]{1,0:T(8,128)S(1)}, u32[]{:S(2)}, u32[]{:S(2)}) collective-permute-start(f32[192,128]{1,0:T(8,128)S(1)} %pad_maximum_fusion), channel_id=1, source_target_pairs={{0,1},{1,0},{2,3},{3,2},{4,5},{5,4},{6,7},{7,6},{8,9},{9,8},{10,11... | collective-permute-start | bytes 294920 | tf_op jit(solution)/shard_map/ppermute | solution.py:758
  11.8 23.0 %collective-permute-start.1 = (f32[192,128]{1,0:T(8,128)S(1)}, f32[192,128]{1,0:T(8,128)S(1)}, u32[]{:S(2)}, u32[]{:S(2)}) collective-permute-start(f32[192,128]{1,0:T(8,128)S(1)} %pad_maximum_fusion.1), channel_id=1, source_target_pairs={{0,2},{1,3},{2,0},{3,1},{4,6},{5,7},{6,4},{7,5},{8,10},{9,11},{10,... | collective-permute-start | bytes 294920 | tf_op jit(solution)/shard_map/ppermute | solution.py:758
  12.1 25.9 %collective-permute-start.2 = (f32[192,128]{1,0:T(8,128)S(1)}, f32[192,128]{1,0:T(8,128)S(1)}, u32[]{:S(2)}, u32[]{:S(2)}) collective-permute-start(f32[192,128]{1,0:T(8,128)S(1)} %pad_maximum_fusion.2), channel_id=1, source_target_pairs={{0,3},{1,2},{2,1},{3,0},{4,7},{5,6},{6,5},{7,4},{8,11},{9,10},{10,... | collective-permute-start | bytes 294920 | tf_op jit(solution)/shard_map/ppermute | solution.py:758
  13.7 34.5 %collective-permute-start.3 = (f32[192,128]{1,0:T(8,128)S(1)}, f32[192,128]{1,0:T(8,128)S(1)}, u32[]{:S(2)}, u32[]{:S(2)}) collective-permute-start(f32[192,128]{1,0:T(8,128)S(1)} %pad_maximum_fusion.3), channel_id=1, source_target_pairs={{0,4},{1,5},{2,6},{3,7},{4,0},{5,1},{6,2},{7,3},{8,12},{9,13},{10,... | collective-permute-start | bytes 294920 | tf_op jit(solution)/shard_map/ppermute | solution.py:758
  14.1 37.2 %collective-permute-start.4 = (f32[192,128]{1,0:T(8,128)S(1)}, f32[192,128]{1,0:T(8,128)S(1)}, u32[]{:S(2)}, u32[]{:S(2)}) collective-permute-start(f32[192,128]{1,0:T(8,128)S(1)} %pad_maximum_fusion.4), channel_id=1, source_target_pairs={{0,5},{1,4},{2,7},{3,6},{4,1},{5,0},{6,3},{7,2},{8,13},{9,12},{10,... | collective-permute-start | bytes 294920 | tf_op jit(solution)/shard_map/ppermute | solution.py:758
  34.0 38.7 %copy-start.3 = (f32[192,128]{1,0:T(8,128)}, f32[192,128]{1,0:T(8,128)S(1)}, u32[]{:S(2)}) copy-start(f32[192,128]{1,0:T(8,128)S(1)} %collective-permute-done.refs_1_) | copy-start | bytes 294916
  34.0 18.2 %collective-permute-start.5 = (f32[192,128]{1,0:T(8,128)S(1)}, f32[192,128]{1,0:T(8,128)S(1)}, u32[]{:S(2)}, u32[]{:S(2)}) collective-permute-start(f32[192,128]{1,0:T(8,128)S(1)} %pad_maximum_fusion.5), channel_id=1, source_target_pairs={{0,6},{1,7},{2,4},{3,5},{4,2},{5,3},{6,0},{7,1},{8,14},{9,15},{10,... | collective-permute-start | bytes 294920 | tf_op jit(solution)/shard_map/ppermute | solution.py:758
  34.8 38.0 %copy-start.4 = (f32[192,128]{1,0:T(8,128)}, f32[192,128]{1,0:T(8,128)S(1)}, u32[]{:S(2)}) copy-start(f32[192,128]{1,0:T(8,128)S(1)} %collective-permute-done.1.refs_2_) | copy-start | bytes 294916
  34.8 19.5 %collective-permute-start.6 = (f32[192,128]{1,0:T(8,128)S(1)}, f32[192,128]{1,0:T(8,128)S(1)}, u32[]{:S(2)}, u32[]{:S(2)}) collective-permute-start(f32[192,128]{1,0:T(8,128)S(1)} %pad_maximum_fusion.6), channel_id=1, source_target_pairs={{0,7},{1,6},{2,5},{3,4},{4,3},{5,2},{6,1},{7,0},{8,15},{9,14},{10,... | collective-permute-start | bytes 294920 | tf_op jit(solution)/shard_map/ppermute | solution.py:758
  38.0 34.7 %copy-start.5 = (f32[192,128]{1,0:T(8,128)}, f32[192,128]{1,0:T(8,128)S(1)}, u32[]{:S(2)}) copy-start(f32[192,128]{1,0:T(8,128)S(1)} %collective-permute-done.2.refs_3_) | copy-start | bytes 294916
  48.2 24.6 %copy-start.6 = (f32[192,128]{1,0:T(8,128)}, f32[192,128]{1,0:T(8,128)S(1)}, u32[]{:S(2)}) copy-start(f32[192,128]{1,0:T(8,128)S(1)} %collective-permute-done.3.refs_4_) | copy-start | bytes 294916
  51.2 21.5 %copy-start.7 = (f32[192,128]{1,0:T(8,128)}, f32[192,128]{1,0:T(8,128)S(1)}, u32[]{:S(2)}) copy-start(f32[192,128]{1,0:T(8,128)S(1)} %collective-permute-done.4.refs_5_) | copy-start | bytes 294916
  52.2 20.6 %copy-start.8 = (f32[192,128]{1,0:T(8,128)}, f32[192,128]{1,0:T(8,128)S(1)}, u32[]{:S(2)}) copy-start(f32[192,128]{1,0:T(8,128)S(1)} %collective-permute-done.5.refs_6_) | copy-start | bytes 294916
  54.3 18.5 %copy-start.9 = (f32[192,128]{1,0:T(8,128)}, f32[192,128]{1,0:T(8,128)S(1)}, u32[]{:S(2)}) copy-start(f32[192,128]{1,0:T(8,128)S(1)} %collective-permute-done.6.refs_7_) | copy-start | bytes 294916
  59.4 51.8 %all-to-all-start.1 = ((f32[16,2,128,128]{3,2,1,0:T(8,128)}), f32[16,2,128,128]{3,2,1,0:T(8,128)}, u32[]{:S(2)}, u32[]{:S(2)}) async-start(f32[16,2,128,128]{3,2,1,0:T(8,128)} %forward_lines.3), calls=%async_computation.1 | async-start | bytes 4194304 | tf_op jit(solution)/shard_map/all_to_all | solution.py:744
  111.2 46.8 %all-to-all-start.2 = ((f32[8,3,2,128,128]{4,3,2,1,0:T(8,128)}), f32[8,3,2,128,128]{4,3,2,1,0:T(8,128)S(1)}, u32[]{:S(2)}, u32[]{:S(2)}) async-start(f32[8,3,2,128,128]{4,3,2,1,0:T(8,128)} %rows_there_and_back.2), calls=%async_computation.2 | async-start | bytes 6291456 | tf_op jit(solution)/shard_map/all_to_all | solution.py:744
  115.2 42.7 %collective-permute-start.7 = (f32[8,64,128]{2,1,0:T(8,128)}, f32[8,64,128]{2,1,0:T(8,128)S(1)}, u32[]{:S(2)}, u32[]{:S(2)}) collective-permute-start(f32[8,64,128]{2,1,0:T(8,128)} %fusion), channel_id=1, source_target_pairs={{0,8},{1,9},{2,10},{3,11},{4,12},{5,13},{6,14},{7,15},{8,0},{9,1},... | collective-permute-start | bytes 786440 | tf_op jit(solution)/shard_map/ppermute | solution.py:776
  157.9 4.7 %copy-start.1 = (f32[8,64,128]{2,1,0:T(8,128)}, f32[8,64,128]{2,1,0:T(8,128)S(1)}, u32[]{:S(2)}) copy-start(f32[8,64,128]{2,1,0:T(8,128)S(1)} %collective-permute-done.7.far_ref) | copy-start | bytes 786436
  157.9 39.8 %all-to-all-start.3 = ((f32[8,3,2,128,128]{4,3,2,1,0:T(8,128)}), f32[8,3,2,128,128]{4,3,2,1,0:T(8,128)}, u32[]{:S(2)}, u32[]{:S(2)}) async-start(f32[8,3,2,128,128]{4,3,2,1,0:T(8,128)} %rows_there_and_back.3), calls=%async_computation.3 | async-start | bytes 6291456 | tf_op jit(solution)/shard_map/all_to_all | solution.py:744
  162.6 7.3 %collective-permute-start.8 = (f32[8,64,128]{2,1,0:T(8,128)S(1)}, f32[8,64,128]{2,1,0:T(8,128)S(1)}, u32[]{:S(2)}, u32[]{:S(2)}) collective-permute-start(f32[8,64,128]{2,1,0:T(8,128)S(1)} %collective-permute-done.7.far_ref), channel_id=1, source_target_pairs={{0,16},{16,0},{1,17},{17,1},{2,18},{18,2},{3,19},{19,3},{4,20},{20... | collective-permute-start | bytes 786440 | tf_op jit(solution)/shard_map/ppermute | solution.py:780
  169.9 0.7 copy-start.2

commit v5 on v4

--- a/solution.py
+++ b/solution.py
@@ -484,18 +484,28 @@
 
 
 def rows_kernel(
-    c, in_ref, phase_ref, out_ref,
-    work_ref, spec_ref, turn_ref, column_ref, ahead_table_ref, back_table_ref,
-    factor_ref, field_ref, factor_sem, field_sem,
+    c, apart, in_ref, phase_ref, *refs,
 ):
+    outs = half_radix if apart else 1
+    out_refs, refs = refs[:outs], refs[outs:]
+    (
+        work_ref, spec_ref, turn_ref, column_ref, ahead_table_ref, back_table_ref,
+        factor_ref, field_ref, factor_sem, field_sem,
+    ) = refs
+    place = lax.axis_index("slab") % half_radix
     begin = lax.axis_index("slab") // half_radix * half_radix
     count = len(ref_speeds)
 
     def factor_copy(t):
         return pltpu.make_async_copy(phase_ref.at[c, t], factor_ref.at[t], factor_sem.at[t])
 
-    def field_copy(t):
-        return pltpu.make_async_copy(field_ref.at[t % 2], out_ref.at[:, t], field_sem.at[t % 2])
+    def field_copies(t):
+        if not apart:
+            return [pltpu.make_async_copy(field_ref.at[t % 2], out_refs[0].at[:, t], field_sem.at[t % 2, 0])]
+        return [
+            pltpu.make_async_copy(field_ref.at[t % 2, place ^ k], out_refs[k].at[t], field_sem.at[t % 2, k])
+            for k in range(half_radix)
+        ]
 
     for t in range(count):
         factor_copy(t).start()
@@ -572,7 +582,8 @@
         if t + 1 < count:
             factor_copy(t + 1).wait()
         if t >= 2:
-            field_copy(t - 2).wait()
+            for copy in field_copies(t - 2):
+                copy.wait()
 
         def both(index, carry):
             if t + 1 < count:
@@ -583,21 +594,25 @@
             return carry
 
         lax.fori_loop(0, radix // 2, both, 0, unroll=True)
-        field_copy(t).start()
+        for copy in field_copies(t):
+            copy.start()
 
     for t in range(count - 2, count):
-        field_copy(t).wait()
-
-
-def rows_call(c, arrived, phase):
+        for copy in field_copies(t):
+            copy.wait()
+
+
+def rows_call(c, apart, arrived, phase):
     count = len(ref_speeds)
     in_vmem = pl.BlockSpec(memory_space=pltpu.VMEM)
     in_hbm = pl.BlockSpec(memory_space=pltpu.HBM)
     return pl.pallas_call(
-        functools.partial(rows_kernel, c),
+        functools.partial(rows_kernel, c, apart),
         in_specs=[in_vmem, in_hbm],
-        out_specs=in_hbm,
-        out_shape=jax.ShapeDtypeStruct((half_radix, count, 2, lane, lane), jnp.float32),
+        out_specs=[in_hbm] * half_radix if apart else in_hbm,
+        out_shape=[jax.ShapeDtypeStruct((count, 2, lane, lane), jnp.float32)] * half_radix
+        if apart
+        else jax.ShapeDtypeStruct((half_radix, count, 2, lane, lane), jnp.float32),
         scratch_shapes=[
             pltpu.VMEM((2, 2 * lane, full), jnp.float32),
             pltpu.VMEM((2 * lane, full), jnp.float32),
@@ -608,7 +623,7 @@
             pltpu.VMEM((3, 2, lane, full), jnp.float32),
             pltpu.VMEM((2, half_radix, 2, lane, lane), jnp.float32),
             pltpu.SemaphoreType.DMA((3,)),
-            pltpu.SemaphoreType.DMA((2,)),
+            pltpu.SemaphoreType.DMA((2, half_radix)),
         ],
         compiler_params=pltpu.CompilerParams(vmem_limit_bytes=rows_vmem_bytes),
         cost_estimate=pl.CostEstimate(
@@ -661,8 +676,10 @@
 strip = 32
 
 
-def finish_kernel(even_ref, odd_ref, blend_ref, out_ref, image_ref, work_ref, turn_ref, table_ref):
+def finish_kernel(odd_ref, blend_ref, *refs):
+    even_refs, (out_ref, image_ref, work_ref, turn_ref, table_ref) = refs[:half_radix], refs[half_radix:]
     count = len(ref_speeds)
+    place = lax.axis_index("slab") % half_radix
 
     @pl.when(pl.program_id(0) == 0)
     def _():
@@ -670,12 +687,13 @@
         put_matrix(table_ref, *unit_matrix(), False)
 
     for j in range(count):
-        for c, in_ref in enumerate((even_ref, odd_ref)):
-            values = jnp.concatenate([in_ref[:, j, 0], in_ref[:, j, 1]], axis=2)
-            product = right_product(values.reshape(half_radix * strip, 2 * lane), table_ref[...])
-            product = product.reshape(half_radix, strip, 2 * lane)
-            for i in range(half_radix):
-                work_ref[j, 2 * i + c] = product[i]
+        odds = jnp.concatenate([odd_ref[:, j, 0], odd_ref[:, j, 1]], axis=2).reshape(half_radix * strip, 2 * lane)
+        evens = jnp.concatenate([jnp.concatenate([ref[j, 0], ref[j, 1]], axis=1) for ref in even_refs], axis=0)
+        odd, even = right_product(odds, table_ref[...]), right_product(evens, table_ref[...])
+        for i in range(half_radix):
+            here = slice(i * strip, (i + 1) * strip)
+            work_ref[j, 2 * i + 1] = odd[here]
+            work_ref[j, 2 * (place ^ i)] = even[here]
 
     def rows(index, carry):
         here = pl.ds(pl.multiple_of(index * 8, 8), 8)
@@ -711,15 +729,15 @@
     lax.fori_loop(0, strip // 8, rows, 0, unroll=True)
 
 
-def finish_call(even, odd, blend):
+def finish_call(evens, odd, blend):
     count = len(ref_speeds)
     return pl.pallas_call(
         finish_kernel,
         grid=(lane // strip,),
         in_specs=[
             pl.BlockSpec((half_radix, count, 2, strip, lane), lambda g: (0, 0, 0, g, 0)),
-            pl.BlockSpec((half_radix, count, 2, strip, lane), lambda g: (0, 0, 0, g, 0)),
             pl.BlockSpec((3, strip, full), lambda g: (0, g, 0)),
+            *[pl.BlockSpec((count, 2, strip, lane), lambda g: (0, 0, g, 0))] * half_radix,
         ],
         out_specs=[
             pl.BlockSpec((1, 2, strip, full), lambda g: (0, 0, g, 0)),
@@ -736,7 +754,7 @@
         ],
         compiler_params=pltpu.CompilerParams(vmem_limit_bytes=finish_vmem_bytes),
         name="inverse_lines",
-    )(even, odd, blend)
+    )(odd, blend, *evens)
 
 
 def exchange(values, group):
@@ -769,17 +787,16 @@
     phase = phase_call(frequencies)
     beyond, phase, even, odd = lax.optimization_barrier((beyond, phase, even, odd))
     odd = exchange(odd, radix)
-    even = rows_call(0, even, phase)
-    even, odd = lax.optimization_barrier((even, odd))
-    even = exchange(even, half_radix)
+    evens = rows_call(0, True, even, phase)
+    evens = [part if k == 0 else lax.ppermute(part, "slab", partners(k)) for k, part in enumerate(evens)]
     beyond, _ = lax.optimization_barrier((beyond, odd))
     beyond = lax.ppermute(beyond, "slab", partners(far))
-    odd = rows_call(1, odd, phase)
-    beyond, even, odd = lax.optimization_barrier((beyond, even, odd))
+    odd = rows_call(1, False, odd, phase)
+    evens, beyond, odd = lax.optimization_barrier((evens, beyond, odd))
     odd = exchange(odd, half_radix)
     swapped = lax.ppermute(beyond, "shot", [(0, 1), (1, 0)])
     blend = blend_call(frequencies, bracket, beyond, swapped, *speeds)
-    propagated, image = finish_call(even, odd, blend)
+    propagated, image = finish_call(evens, odd, blend)
     return propagated, image
 
 

time: 209 us -> 194 us (0.928)
  waiting for transfers between devices: 114 us -> 89.3 us
  local copies, waits for them, and re-layouts: 5.93 us -> 11.4 us
  Pallas kernels: 53.7 us -> 55.9 us
    ppermute x1, waiting for transfers between devices: 29.7 us -> 2.28 us  [per_device(): beyond = lax.ppermute(beyond, 'slab', partners(far))]
    ppermute x0 -> x7, waiting for transfers between devices: none -> 11.9 us  [per_device(): lax.ppermute(part, 'slab', partners(k))]
    all_to_all x4 -> x3, waiting for transfers between devices: 65.3 us -> 56.3 us  [exchange(): lax.all_to_all(values, 'slab', split_axis=0, concat_axis=0, tiled=True, a...]
    ppermute x0 -> x7, starting transfers between devices: none -> 6.19 us  [per_device(): lax.ppermute(part, 'slab', partners(k))]
    unnamed x26 -> x44, local copies, waits for them, and re-layouts: 4.55 us -> 9.46 us
    all_to_all x4 -> x3, starting transfers between devices: 19.8 us -> 16.5 us  [exchange(): lax.all_to_all(values, 'slab', split_axis=0, concat_axis=0, tiled=True, a...]
  transfers between devices with their start and end apart: 13 -> 19, of which waited for: 9 -> 11; matrix products, arithmetic and copies ran while one was open for 3% -> 3% of each run, Pallas kernels for 20% -> 23%
where the time goes in v5:
time: 194 us; the launch traced here: 191 us
  waiting for transfers between devices  89.3 us (46%)
  Pallas kernels  55.9 us (29%)
  starting transfers between devices  32 us (16%)
  local copies, waits for them, and re-layouts  11.4 us (6%)
    all_to_all x3, waiting for transfers between devices, exchange(): lax.all_to_all(values, 'slab', split_axis=0, concat_axis=0, tiled=True, a...  56.3 us
    pallas_call x2, Pallas kernels, rows_call(): pl.pallas_call(functools.partial(rows_kernel, c, apart), in_specs=[in_vme...  21.5 us
    all_to_all x3, starting transfers between devices, exchange(): lax.all_to_all(values, 'slab', split_axis=0, concat_axis=0, tiled=True, a...  16.5 us
    pallas_call x1, Pallas kernels, phase_call(): pl.pallas_call(phase_kernel, in_specs=[pl.BlockSpec(memory_space=pltpu.SM...  14.5 us
    ppermute x7, waiting for transfers between devices, speeds_near(): tiles.append(lax.ppermute(both, 'slab', partners(k)) if k else both)  13.2 us
    ppermute x7, waiting for transfers between devices, per_device(): lax.ppermute(part, 'slab', partners(k))  11.9 us
    unnamed x44, local copies, waits for them, and re-layouts  9.46 us
    pallas_call x1, Pallas kernels, finish_call(): pl.pallas_call(finish_kernel, grid=(lane // strip,), in_specs=[pl.BlockSp...  8.77 us
  transfers between devices with their start and end apart: 19, of which 11 were waited for; matrix products, arithmetic and copies ran while one was open for 3% of the time, Pallas kernels for 23%

profile of v5, /device:TPU:13, one launch (start us, length us, event | category | flops | bytes accessed | tf_op | source)
XLA Modules:
  0.0 190.8 jit_solution(13399323588460264017)
XLA Ops:
  0.6 3.3 %forward_lines.2 = f32[16,2,128,128]{3,2,1,0:T(8,128)} custom-call(f32[1,2,128,2048]{3,2,1,0:T(8,128)} %field_ref.2, f32[16,2,8,128]{3,2,1,0:T(8,128)} %constant.53.clone.turn_ref, bf16[768,256]{1,0:T(8,128)(2,1)} %constant.54.clone.table_ref), custom_call_target="tpu_custom_call" | custom-call | flops 805306368 | bytes 4194304 | tf_op jit(solution)/shard_map/forward_lines/pallas_call | solution.py:381
  3.9 6.7 %all-to-all-start = ((f32[16,2,128,128]{3,2,1,0:T(8,128)}), f32[16,2,128,128]{3,2,1,0:T(8,128)S(1)}, u32[]{:S(2)}, u32[]{:S(2)}) async-start(f32[16,2,128,128]{3,2,1,0:T(8,128)} %forward_lines.2), calls=%async_computation | async-start | bytes 4194304 | tf_op jit(solution)/shard_map/all_to_all | solution.py:762
  10.6 0.7 dynamic-slice_bitcast_fusion.15
  11.3 0.7 dynamic-slice_bitcast_fusion
  12.0 0.4 collective-permute-start
  12.4 0.3 collective-permute-start.1
  12.8 1.6 collective-permute-start.2
  14.7 1.5 collective-permute-start.4
  16.8 14.5 %phase_factors.1.phase_ref = f32[2,3,2,128,2048]{4,3,2,1,0:T(8,128)} custom-call(f32[1]{0:T(128)S(6)} %copy.17.angular_ref), custom_call_target="tpu_custom_call" | custom-call | flops 94371840 | bytes 12582912 | tf_op jit(solution)/shard_map/phase_factors/pallas_call | solution.py:437
  31.3 3.3 %forward_lines.3 = f32[16,2,128,128]{3,2,1,0:T(8,128)} custom-call(f32[1,2,128,2048]{3,2,1,0:T(8,128)} %field_ref.2, f32[16,2,8,128]{3,2,1,0:T(8,128)} %constant.53.clone.turn_ref, bf16[768,256]{1,0:T(8,128)(2,1)} %constant.54.clone.table_ref), custom_call_target="tpu_custom_call" | custom-call | flops 805306368 | bytes 4194304 | tf_op jit(solution)/shard_map/forward_lines/pallas_call | solution.py:381
  34.7 0.6 fusion.6
  35.4 2.6 %collective-permute-start.6 = (f32[192,128]{1,0:T(8,128)S(1)}, f32[192,128]{1,0:T(8,128)S(1)}, u32[]{:S(2)}, u32[]{:S(2)}) collective-permute-start(f32[192,128]{1,0:T(8,128)S(1)} %pad_maximum_fusion.6), channel_id=1, source_target_pairs={{0,7},{1,6},{2,5},{3,4},{4,3},{5,2},{6,1},{7,0},{8,15},{9,14},{10,... | collective-permute-start | bytes 294920 | tf_op jit(solution)/shard_map/ppermute | solution.py:776
  38.0 0.6 fusion.5
  38.6 0.6 fusion.4
  39.2 9.0 %collective-permute-done.3.refs_4_ = f32[192,128]{1,0:T(8,128)S(1)} collective-permute-done((f32[192,128]{1,0:T(8,128)S(1)}, f32[192,128]{1,0:T(8,128)S(1)}, u32[]{:S(2)}, u32[]{:S(2)}) %collective-permute-start.3) | collective-permute-done | bytes 98336 | tf_op jit(solution)/shard_map/ppermute | solution.py:776
  48.2 0.6 fusion.3
  48.9 2.4 %collective-permute-done.4.refs_5_ = f32[192,128]{1,0:T(8,128)S(1)} collective-permute-done((f32[192,128]{1,0:T(8,128)S(1)}, f32[192,128]{1,0:T(8,128)S(1)}, u32[]{:S(2)}, u32[]{:S(2)}) %collective-permute-start.4) | collective-permute-done | bytes 98336 | tf_op jit(solution)/shard_map/ppermute | solution.py:776
  51.3 0.6 fusion.2
  52.2 0.6 fusion.1
  52.9 1.5 collective-permute-done.6.refs_7_
  54.4 0.6 copy-done.17
  55.0 0.6 fusion
  55.6 3.8 %all-to-all-done.in_ref = f32[16,2,128,128]{3,2,1,0:T(8,128)S(1)} async-done(((f32[16,2,128,128]{3,2,1,0:T(8,128)}), f32[16,2,128,128]{3,2,1,0:T(8,128)S(1)}, u32[]{:S(2)}, u32[]{:S(2)}) %all-to-all-start) | async-done | bytes 2097184 | tf_op jit(solution)/shard_map/all_to_all | solution.py:762
  59.4 1.3 copy-done.6
  60.7 4.2 %all-to-all-start.1 = ((f32[16,2,128,128]{3,2,1,0:T(8,128)}), f32[16,2,128,128]{3,2,1,0:T(8,128)S(1)}, u32[]{:S(2)}, u32[]{:S(2)}) async-start(f32[16,2,128,128]{3,2,1,0:T(8,128)} %forward_lines.3), calls=%async_computation.1 | async-start | bytes 4194304 | tf_op jit(solution)/shard_map/all_to_all | solution.py:762
  65.0 12.2 %rows_there_and_back.2 = (f32[3,2,128,128]{3,2,1,0:T(8,128)S(1)}, f32[3,2,128,128]{3,2,1,0:T(8,128)}, f32[3,2,128,128]{3,2,1,0:T(8,128)}, f32[3,2,128,128]{3,2,1...) custom-call(f32[16,2,128,128]{3,2,1,0:T(8,128)} %copy-done.6, ...), custom_call_target="tpu_custom_call" | custom-call | flops 6442450944 | bytes 58720256 | tf_op jit(solution)/shard_map/rows_there_and_back/pallas_call | solution.py:609
  77.1 0.7 copy-done.4
  77.9 0.8 copy-done.5
  78.7 0.4 collective-permute-start.7
  79.3 1.5 collective-permute-start.9
  81.1 1.4 collective-permute-start.11
  82.5 30.4 %all-to-all-done.1.in_ref = f32[16,2,128,128]{3,2,1,0:T(8,128)S(1)} async-done(((f32[16,2,128,128]{3,2,1,0:T(8,128)}), f32[16,2,128,128]{3,2,1,0:T(8,128)S(1)}, u32[]{:S(2)}, u32[]{:S(2)}) %all-to-all-start.1) | async-done | bytes 2097184 | tf_op jit(solution)/shard_map/all_to_all | solution.py:762
  112.9 2.3 %collective-permute-start.13 = (f32[3,2,128,128]{3,2,1,0:T(8,128)}, f32[3,2,128,128]{3,2,1,0:T(8,128)S(1)}, u32[]{:S(2)}, u32[]{:S(2)}) collective-permute-start(f32[3,2,128,128]{3,2,1,0:T(8,128)} %copy-done.4), channel_id=1, source_target_pairs={{0,7},{1,6},{2,5},{3,4},{4,3},{5,2},{6,1},{7,0},{8,15},{9,14},{10,... | collective-permute-start | bytes 1179656 | tf_op jit(solution)/shard_map/ppermute | solution.py:791
  115.3 1.2 collective-permute-start.14
  116.5 9.3 %rows_there_and_back.3 = f32[8,3,2,128,128]{4,3,2,1,0:T(8,128)} custom-call(f32[16,2,128,128]{3,2,1,0:T(8,128)S(1)} %all-to-all-done.1.in_ref, f32[2,3,2,128,2048]{4,3,2,1,0:T(8,128)} %phase_factors.1.phase_ref), custom_call_target="tpu_custom_call" | custom-call | flops 6442450944 | bytes 58720256 | tf_op jit(solution)/shard_map/rows_there_and_back/pallas_call | solution.py:609
  125.8 4.2 %collective-permute-done.12.refs_6_ = f32[3,2,128,128]{3,2,1,0:T(8,128)S(1)} collective-permute-done((f32[3,2,128,128]{3,2,1,0:T(8,128)}, f32[3,2,128,128]{3,2,1,0:T(8,128)S(1)}, u32[]{:S(2)}, u32[]{:S(2)}) %collective-permute-start.12) | collective-permute-done | bytes 393248 | tf_op jit(solution)/shard_map/ppermute | solution.py:791
  130.0 0.7 copy-done
  130.7 7.7 %collective-permute-done.13.refs_7_ = f32[3,2,128,128]{3,2,1,0:T(8,128)S(1)} collective-permute-done((f32[3,2,128,128]{3,2,1,0:T(8,128)}, f32[3,2,128,128]{3,2,1,0:T(8,128)S(1)}, u32[]{:S(2)}, u32[]{:S(2)}) %collective-permute-start.13) | collective-permute-done | bytes 393248 | tf_op jit(solution)/shard_map/ppermute | solution.py:791
  138.4 0.7 copy-done.2
  139.2 2.3 %collective-permute-done.14.far_ref = f32[8,64,128]{2,1,0:T(8,128)S(1)} collective-permute-done((f32[8,64,128]{2,1,0:T(8,128)}, f32[8,64,128]{2,1,0:T(8,128)S(1)}, u32[]{:S(2)}, u32[]{:S(2)}) %collective-permute-start.14) | collective-permute-done | bytes 262176 | tf_op jit(solution)/shard_map/ppermute | solution.py:793
  141.5 5.5 %all-to-all-start.2 = ((f32[8,3,2,128,128]{4,3,2,1,0:T(8,128)}), f32[8,3,2,128,128]{4,3,2,1,0:T(8,128)}, u32[]{:S(2)}, u32[]{:S(2)}) async-start(f32[8,3,2,128,128]{4,3,2,1,0:T(8,128)} %rows_there_and_back.3), calls=%async_computation.2 | async-start | bytes 6291456 | tf_op jit(solution)/shard_map/all_to_all | solution.py:762
  147.0 1.2 collective-permute-start.15
  148.2 0.6 pad_maximum_fusion.7.refs_0_
  148.9 5.8 %collective-permute-done.15.swapped_ref = f32[8,64,128]{2,1,0:T(8,128)S(1)} collective-permute-done((f32[8,64,128]{2,1,0:T(8,128)S(1)}, f32[8,64,128]{2,1,0:T(8,128)S(1)}, u32[]{:S(2)}, u32[]{:S(2)}) %collective-permute-start.15) | collective-permute-done | bytes 262176 | tf_op jit(solution)/shard_map/ppermute | solution.py:797
  154.6 0.7 copy-done.9
  155.3 4.7 %blend_factors.1.blend_ref = f32[3,128,2048]{2,1,0:T(8,128)} custom-call(f32[1]{0:T(128)S(6)} %copy.17.angular_ref, s32[1,128,2048]{2,1,0:T(8,128)} %bracket_ref.1, f32[8,64,128]{2,1,0:T(8,128)} %copy-done.8, f32[8,64,128]{2,1,0:T(8,128)} %copy-done.9, f32[192,128]{1,0:T(8,128)} %pad_maximum_fusion.7.refs_0_, f32[192,128]{1,0:T(8,128)} %copy-done.11, ...), custom_call_target="tpu_custom_call" | custom-call | flops 15728640 | bytes 6291456 | tf_op jit(solution)/shard_map/blend_factors/pallas_call | solution.py:664
  160.0 22.0 %all-to-all-done.2.odd_ref = f32[8,3,2,128,128]{4,3,2,1,0:T(8,128)} async-done(((f32[8,3,2,128,128]{4,3,2,1,0:T(8,128)}), f32[8,3,2,128,128]{4,3,2,1,0:T(8,128)}, u32[]{:S(2)}, u32[]{:S(2)}) %all-to-all-start.2) | async-done | bytes 3145760 | tf_op jit(solution)/shard_map/all_to_all | solution.py:762
  182.0 8.8 %inverse_lines.1 = (f32[1,2,128,2048]{3,2,1,0:T(8,128)}, f32[1,128,2048]{2,1,0:T(8,128)}) custom-call(f32[8,3,2,128,128]{4,3,2,1,0:T(8,128)} %all-to-all-done.2.odd_ref, f32[3,128,2048]{2,1,0:T(8,128)} %blend_factors.1.blend_ref, f32[3,2,128,128]{3,2,1,0:T(8,128)S(1)} %get-tuple-element.46.refs_0_, f32[3,2,128,128]{3,2,1,0:T(8,128)S(1)} %collective-permute-done.7.refs_1_, ...), custom_call_target="tpu_custom_call" | custom-call | tf_op jit(solution)/shard_map/inverse_lines/pallas_call | solution.py:734
  (52 shorter events, 1.5 us)
Async XLA Ops:
  3.9 6.7 %copy-start.7 = (f32[1,128,2048]{2,1,0:T(8,128)S(1)}, f32[1,128,2048]{2,1,0:T(8,128)}, u32[]{:S(2)}) copy-start(f32[1,128,2048]{2,1,0:T(8,128)} %param.10) | copy-start | bytes 3145732
  3.9 55.5 %all-to-all-start = ((f32[16,2,128,128]{3,2,1,0:T(8,128)}), f32[16,2,128,128]{3,2,1,0:T(8,128)S(1)}, u32[]{:S(2)}, u32[]{:S(2)}) async-start(f32[16,2,128,128]{3,2,1,0:T(8,128)} %forward_lines.2), calls=%async_computation | async-start | bytes 4194304 | tf_op jit(solution)/shard_map/all_to_all | solution.py:762
  12.0 22.6 %collective-permute-start = (f32[192,128]{1,0:T(8,128)S(1)}, f32[192,128]{1,0:T(8,128)S(1)}, u32[]{:S(2)}, u32[]{:S(2)}) collective-permute-start(f32[192,128]{1,0:T(8,128)S(1)} %pad_maximum_fusion), channel_id=1, source_target_pairs={{0,1},{1,0},{2,3},{3,2},{4,5},{5,4},{6,7},{7,6},{8,9},{9,8},{10,11... | collective-permute-start | bytes 294920 | tf_op jit(solution)/shard_map/ppermute | solution.py:776
  12.4 23.0 %collective-permute-start.1 = (f32[192,128]{1,0:T(8,128)S(1)}, f32[192,128]{1,0:T(8,128)S(1)}, u32[]{:S(2)}, u32[]{:S(2)}) collective-permute-start(f32[192,128]{1,0:T(8,128)S(1)} %pad_maximum_fusion.1), channel_id=1, source_target_pairs={{0,2},{1,3},{2,0},{3,1},{4,6},{5,7},{6,4},{7,5},{8,10},{9,11},{10,... | collective-permute-start | bytes 294920 | tf_op jit(solution)/shard_map/ppermute | solution.py:776
  12.8 25.8 %collective-permute-start.2 = (f32[192,128]{1,0:T(8,128)S(1)}, f32[192,128]{1,0:T(8,128)S(1)}, u32[]{:S(2)}, u32[]{:S(2)}) collective-permute-start(f32[192,128]{1,0:T(8,128)S(1)} %pad_maximum_fusion.2), channel_id=1, source_target_pairs={{0,3},{1,2},{2,1},{3,0},{4,7},{5,6},{6,5},{7,4},{8,11},{9,10},{10,... | collective-permute-start | bytes 294920 | tf_op jit(solution)/shard_map/ppermute | solution.py:776
  14.3 33.9 %collective-permute-start.3 = (f32[192,128]{1,0:T(8,128)S(1)}, f32[192,128]{1,0:T(8,128)S(1)}, u32[]{:S(2)}, u32[]{:S(2)}) collective-permute-start(f32[192,128]{1,0:T(8,128)S(1)} %pad_maximum_fusion.3), channel_id=1, source_target_pairs={{0,4},{1,5},{2,6},{3,7},{4,0},{5,1},{6,2},{7,3},{8,12},{9,13},{10,... | collective-permute-start | bytes 294920 | tf_op jit(solution)/shard_map/ppermute | solution.py:776
  14.7 36.6 %collective-permute-start.4 = (f32[192,128]{1,0:T(8,128)S(1)}, f32[192,128]{1,0:T(8,128)S(1)}, u32[]{:S(2)}, u32[]{:S(2)}) collective-permute-start(f32[192,128]{1,0:T(8,128)S(1)} %pad_maximum_fusion.4), channel_id=1, source_target_pairs={{0,5},{1,4},{2,7},{3,6},{4,1},{5,0},{6,3},{7,2},{8,13},{9,12},{10,... | collective-permute-start | bytes 294920 | tf_op jit(solution)/shard_map/ppermute | solution.py:776
  34.6 19.7 %copy-start.11 = (f32[192,128]{1,0:T(8,128)}, f32[192,128]{1,0:T(8,128)S(1)}, u32[]{:S(2)}) copy-start(f32[192,128]{1,0:T(8,128)S(1)} %collective-permute-done.refs_1_) | copy-start | bytes 294916
  34.6 17.6 %collective-permute-start.5 = (f32[192,128]{1,0:T(8,128)S(1)}, f32[192,128]{1,0:T(8,128)S(1)}, u32[]{:S(2)}, u32[]{:S(2)}) collective-permute-start(f32[192,128]{1,0:T(8,128)S(1)} %pad_maximum_fusion.5), channel_id=1, source_target_pairs={{0,6},{1,7},{2,4},{3,5},{4,2},{5,3},{6,0},{7,1},{8,14},{9,15},{10,... | collective-permute-start | bytes 294920 | tf_op jit(solution)/shard_map/ppermute | solution.py:776
  35.4 19.0 %copy-start.12 = (f32[192,128]{1,0:T(8,128)}, f32[192,128]{1,0:T(8,128)S(1)}, u32[]{:S(2)}) copy-start(f32[192,128]{1,0:T(8,128)S(1)} %collective-permute-done.1.refs_2_) | copy-start | bytes 294916
  35.4 19.0 %collective-permute-start.6 = (f32[192,128]{1,0:T(8,128)S(1)}, f32[192,128]{1,0:T(8,128)S(1)}, u32[]{:S(2)}, u32[]{:S(2)}) collective-permute-start(f32[192,128]{1,0:T(8,128)S(1)} %pad_maximum_fusion.6), channel_id=1, source_target_pairs={{0,7},{1,6},{2,5},{3,4},{4,3},{5,2},{6,1},{7,0},{8,15},{9,14},{10,... | collective-permute-start | bytes 294920 | tf_op jit(solution)/shard_map/ppermute | solution.py:776
  38.6 15.7 %copy-start.13 = (f32[192,128]{1,0:T(8,128)}, f32[192,128]{1,0:T(8,128)S(1)}, u32[]{:S(2)}) copy-start(f32[192,128]{1,0:T(8,128)S(1)} %collective-permute-done.2.refs_3_) | copy-start | bytes 294916
  48.2 6.1 %copy-start.14 = (f32[192,128]{1,0:T(8,128)}, f32[192,128]{1,0:T(8,128)S(1)}, u32[]{:S(2)}) copy-start(f32[192,128]{1,0:T(8,128)S(1)} %collective-permute-done.3.refs_4_) | copy-start | bytes 294916
  51.3 3.1 %copy-start.15 = (f32[192,128]{1,0:T(8,128)}, f32[192,128]{1,0:T(8,128)S(1)}, u32[]{:S(2)}) copy-start(f32[192,128]{1,0:T(8,128)S(1)} %collective-permute-done.4.refs_5_) | copy-start | bytes 294916
  52.2 2.1 %copy-start.16 = (f32[192,128]{1,0:T(8,128)}, f32[192,128]{1,0:T(8,128)S(1)}, u32[]{:S(2)}) copy-start(f32[192,128]{1,0:T(8,128)S(1)} %collective-permute-done.5.refs_6_) | copy-start | bytes 294916
  54.4 0.6 copy-start.17
  59.4 1.3 copy-start.6
  60.7 52.2 %all-to-all-start.1 = ((f32[16,2,128,128]{3,2,1,0:T(8,128)}), f32[16,2,128,128]{3,2,1,0:T(8,128)S(1)}, u32[]{:S(2)}, u32[]{:S(2)}) async-start(f32[16,2,128,128]{3,2,1,0:T(8,128)} %forward_lines.3), calls=%async_computation.1 | async-start | bytes 4194304 | tf_op jit(solution)/shard_map/all_to_all | solution.py:762
  77.1 0.7 copy-start.4
  77.9 0.8 copy-start.5
  78.7 34.3 %collective-permute-start.7 = (f32[3,2,128,128]{3,2,1,0:T(8,128)}, f32[3,2,128,128]{3,2,1,0:T(8,128)S(1)}, u32[]{:S(2)}, u32[]{:S(2)}) collective-permute-start(f32[3,2,128,128]{3,2,1,0:T(8,128)} %get-tuple-element.34), channel_id=1, source_target_pairs={{0,1},{1,0},{2,3},{3,2},{4,5},{5,4},{6,7},{7,6},{8,9},{9,8},{10,11... | collective-permute-start | bytes 1179656 | tf_op jit(solution)/shard_map/ppermute | solution.py:791
  79.0 33.9 %collective-permute-start.8 = (f32[3,2,128,128]{3,2,1,0:T(8,128)}, f32[3,2,128,128]{3,2,1,0:T(8,128)S(1)}, u32[]{:S(2)}, u32[]{:S(2)}) collective-permute-start(f32[3,2,128,128]{3,2,1,0:T(8,128)} %get-tuple-element.35), channel_id=1, source_target_pairs={{0,2},{1,3},{2,0},{3,1},{4,6},{5,7},{6,4},{7,5},{8,10},{9,11},{10,... | collective-permute-start | bytes 1179656 | tf_op jit(solution)/shard_map/ppermute | solution.py:791
  79.3 36.0 %collective-permute-start.9 = (f32[3,2,128,128]{3,2,1,0:T(8,128)}, f32[3,2,128,128]{3,2,1,0:T(8,128)}, u32[]{:S(2)}, u32[]{:S(2)}) collective-permute-start(f32[3,2,128,128]{3,2,1,0:T(8,128)} %get-tuple-element.36), channel_id=1, source_target_pairs={{0,3},{1,2},{2,1},{3,0},{4,7},{5,6},{6,5},{7,4},{8,11},{9,10},{10,... | collective-permute-start | bytes 1179656 | tf_op jit(solution)/shard_map/ppermute | solution.py:791
  80.8 45.0 %collective-permute-start.10 = (f32[3,2,128,128]{3,2,1,0:T(8,128)}, f32[3,2,128,128]{3,2,1,0:T(8,128)}, u32[]{:S(2)}, u32[]{:S(2)}) collective-permute-start(f32[3,2,128,128]{3,2,1,0:T(8,128)} %get-tuple-element.37), channel_id=1, source_target_pairs={{0,4},{1,5},{2,6},{3,7},{4,0},{5,1},{6,2},{7,3},{8,12},{9,13},{10,... | collective-permute-start | bytes 1179656 | tf_op jit(solution)/shard_map/ppermute | solution.py:791
  81.1 44.7 %collective-permute-start.11 = (f32[3,2,128,128]{3,2,1,0:T(8,128)}, f32[3,2,128,128]{3,2,1,0:T(8,128)}, u32[]{:S(2)}, u32[]{:S(2)}) collective-permute-start(f32[3,2,128,128]{3,2,1,0:T(8,128)} %get-tuple-element.38), channel_id=1, source_target_pairs={{0,5},{1,4},{2,7},{3,6},{4,1},{5,0},{6,3},{7,2},{8,13},{9,12},{10,... | collective-permute-start | bytes 1179656 | tf_op jit(solution)/shard_map/ppermute | solution.py:791
  112.9 17.1 %collective-permute-start.12 = (f32[3,2,128,128]{3,2,1,0:T(8,128)}, f32[3,2,128,128]{3,2,1,0:T(8,128)S(1)}, u32[]{:S(2)}, u32[]{:S(2)}) collective-permute-start(f32[3,2,128,128]{3,2,1,0:T(8,128)} %copy-done.5), channel_id=1, source_target_pairs={{0,6},{1,7},{2,4},{3,5},{4,2},{5,3},{6,0},{7,1},{8,14},{9,15},{10,... | collective-permute-start | bytes 1179656 | tf_op jit(solution)/shard_map/ppermute | solution.py:791
  112.9 25.5 %collective-permute-start.13 = (f32[3,2,128,128]{3,2,1,0:T(8,128)}, f32[3,2,128,128]{3,2,1,0:T(8,128)S(1)}, u32[]{:S(2)}, u32[]{:S(2)}) collective-permute-start(f32[3,2,128,128]{3,2,1,0:T(8,128)} %copy-done.4), channel_id=1, source_target_pairs={{0,7},{1,6},{2,5},{3,4},{4,3},{5,2},{6,1},{7,0},{8,15},{9,14},{10,... | collective-permute-start | bytes 1179656 | tf_op jit(solution)/shard_map/ppermute | solution.py:791
  115.3 26.2 %collective-permute-start.14 = (f32[8,64,128]{2,1,0:T(8,128)}, f32[8,64,128]{2,1,0:T(8,128)S(1)}, u32[]{:S(2)}, u32[]{:S(2)}) collective-permute-start(f32[8,64,128]{2,1,0:T(8,128)} %fusion), channel_id=1, source_target_pairs={{0,8},{1,9},{2,10},{3,11},{4,12},{5,13},{6,14},{7,15},{8,0},{9,1},... | collective-permute-start | bytes 786440 | tf_op jit(solution)/shard_map/ppermute | solution.py:793
  130.0 0.7 copy-start
  138.4 0.7 copy-start.2
  141.5 5.5 %copy-start.8 = (f32[8,64,128]{2,1,0:T(8,128)}, f32[8,64,128]{2,1,0:T(8,128)S(1)}, u32[]{:S(2)}) copy-start(f32[8,64,128]{2,1,0:T(8,128)S(1)} %collective-permute-done.14.far_ref) | copy-start | bytes 786436
  141.5 6.7 %copy-start.10 = (f32[128,128]{1,0:T(8,128)S(1)}, f32[128,128]{1,0:T(8,128)}, u32[]{:S(2)}) copy-start(f32[128,128]{1,0:T(8,128)} %get-tuple-element.54) | copy-start | bytes 196612
  141.5 6.7 %copy-start.18 = (f32[64,128]{1,0:T(8,128)S(1)}, f32[64,128]{1,0:T(8,128)}, u32[]{:S(2)}) copy-start(f32[64,128]{1,0:T(8,128)} %get-tuple-element.62) | copy-start | bytes 98308
  141.5 40.6 %all-to-all-start.2 = ((f32[8,3,2,128,128]{4,3,2,1,0:T(8,128)}), f32[8,3,2,128,128]{4,3,2,1,0:T(8,128)}, u32[]{:S(2)}, u32[]{:S(2)}) async-start(f32[8,3,2,128,128]{4,3,2,1,0:T(8,128)} %rows_there_and_back.3), calls=%async_computation.2 | async-start | bytes 6291456 | tf_op jit(solution)/shard_map/all_to_all | solution.py:762
  147.0 7.6 %collective-permute-start.15 = (f32[8,64,128]{2,1,0:T(8,128)S(1)}, f32[8,64,128]{2,1,0:T(8,128)S(1)}, u32[]{:S(2)}, u32[]{:S(2)}) collective-permute-start(f32[8,64,128]{2,1,0:T(8,128)S(1)} %collective-permute-done.14.far_ref), channel_id=1, source_target_pairs={{0,16},{16,0},{1,17},{17,1},{2,18},{18,2},{3,19},{19,3},{4,20},{20... | collective-permute-start | bytes 786440 | tf_op jit(solution)/shard_map/ppermute | solution.py:797
  148.8 33.2 %copy-start.1 = (f32[3,2,128,128]{3,2,1,0:T(8,128)S(1)}, f32[3,2,128,128]{3,2,1,0:T(8,128)}, u32[]{:S(2)}) copy-start(f32[3,2,128,128]{3,2,1,0:T(8,128)} %copy-done) | copy-start | bytes 1179652
  148.8 33.2 %copy-start.3 = (f32[3,2,128,128]{3,2,1,0:T(8,128)S(1)}, f32[3,2,128,128]{3,2,1,0:T(8,128)}, u32[]{:S(2)}) copy-start(f32[3,2,128,128]{3,2,1,0:T(8,128)} %copy-done.2) | copy-start | bytes 1179652
  154.6 0.7 copy-start.9

commit v6 on v5

--- a/solution.py
+++ b/solution.py
@@ -332,6 +332,16 @@
         outs = quarter([turned(first[b][c], b * c, direction) for b in range(4)], direction)
         for d in range(4):
             result[c + 4 * d] = outs[d]
+    return result
+
+
+def eight(values, direction):
+    first = [quarter([values[2 * a + b] for a in range(4)], direction) for b in range(2)]
+    result = [None] * 8
+    for c in range(4):
+        re, im = turned(first[1][c], 2 * c, direction)
+        result[c] = (first[0][c][0] + re, first[0][c][1] + im)
+        result[c + 4] = (first[0][c][0] - re, first[0][c][1] - im)
     return result
 
 
@@ -676,38 +686,24 @@
 strip = 32
 
 
-def finish_kernel(odd_ref, blend_ref, *refs):
-    even_refs, (out_ref, image_ref, work_ref, turn_ref, table_ref) = refs[:half_radix], refs[half_radix:]
+def add_class(c, blend_ref, work_ref, turn_ref, store):
     count = len(ref_speeds)
-    place = lax.axis_index("slab") % half_radix
-
-    @pl.when(pl.program_id(0) == 0)
-    def _():
-        build_turns(turn_ref, 1.0, 1.0 / full)
-        put_matrix(table_ref, *unit_matrix(), False)
-
-    for j in range(count):
-        odds = jnp.concatenate([odd_ref[:, j, 0], odd_ref[:, j, 1]], axis=2).reshape(half_radix * strip, 2 * lane)
-        evens = jnp.concatenate([jnp.concatenate([ref[j, 0], ref[j, 1]], axis=1) for ref in even_refs], axis=0)
-        odd, even = right_product(odds, table_ref[...]), right_product(evens, table_ref[...])
-        for i in range(half_radix):
-            here = slice(i * strip, (i + 1) * strip)
-            work_ref[j, 2 * i + 1] = odd[here]
-            work_ref[j, 2 * (place ^ i)] = even[here]
 
     def rows(index, carry):
         here = pl.ds(pl.multiple_of(index * 8, 8), 8)
         for j in range(count):
-            parts = sixteen(
+            parts = eight(
                 [
                     times(
-                        (work_ref[j, k, here, 0:lane], work_ref[j, k, here, lane : 2 * lane]),
-                        (turn_ref[k, 0], turn_ref[k, 1]),
+                        (work_ref[j, i, here, 0:lane], work_ref[j, i, here, lane : 2 * lane]),
+                        (turn_ref[2 * i + c, 0], turn_ref[2 * i + c, 1]),
                     )
-                    for k in range(radix)
+                    for i in range(half_radix)
                 ],
                 1,
             )
+            if c:
+                parts = [turned(part, q, 1) for q, part in enumerate(parts)]
             for s in range(radix):
                 place = blend_ref[0, here, tile(s)]
                 if j == 0:
@@ -716,28 +712,101 @@
                     weight = 1.0 - jnp.abs(place - 1.0)
                 else:
                     weight = jnp.maximum(place - 1.0, 0.0)
-                re, im = parts[s][0] * weight, parts[s][1] * weight
-                if j > 0:
-                    re, im = re + out_ref[0, 0, here, tile(s)], im + out_ref[0, 1, here, tile(s)]
-                if j == count - 1:
-                    re, im = times((re, im), (blend_ref[1, here, tile(s)], blend_ref[2, here, tile(s)]))
-                    image_ref[0, here, tile(s)] = re
-                out_ref[0, 0, here, tile(s)] = re
-                out_ref[0, 1, here, tile(s)] = im
+                if c and s >= half_radix:
+                    weight = -weight
+                re, im = parts[s % half_radix][0] * weight, parts[s % half_radix][1] * weight
+                store(j, s, here, re, im)
         return carry
 
     lax.fori_loop(0, strip // 8, rows, 0, unroll=True)
 
 
-def finish_call(evens, odd, blend):
+def start_kernel(blend_ref, *refs):
+    even_refs, (out_ref, work_ref, turn_ref, table_ref) = refs[:half_radix], refs[half_radix:]
+    place = lax.axis_index("slab") % half_radix
+
+    @pl.when(pl.program_id(0) == 0)
+    def _():
+        build_turns(turn_ref, 1.0, 1.0 / full)
+        put_matrix(table_ref, *unit_matrix(), False)
+
+    for j in range(len(ref_speeds)):
+        values = jnp.concatenate([jnp.concatenate([ref[j, 0], ref[j, 1]], axis=1) for ref in even_refs], axis=0)
+        product = right_product(values, table_ref[...])
+        for k in range(half_radix):
+            work_ref[j, place ^ k] = product[k * strip : (k + 1) * strip]
+
+    def store(j, s, here, re, im):
+        if j > 0:
+            re, im = re + out_ref[0, here, tile(s)], im + out_ref[1, here, tile(s)]
+        out_ref[0, here, tile(s)] = re
+        out_ref[1, here, tile(s)] = im
+
+    add_class(0, blend_ref, work_ref, turn_ref, store)
+
+
+def finish_kernel(odd_ref, before_ref, blend_ref, out_ref, image_ref, work_ref, turn_ref, table_ref):
+    count = len(ref_speeds)
+
+    @pl.when(pl.program_id(0) == 0)
+    def _():
+        build_turns(turn_ref, 1.0, 1.0 / full)
+        put_matrix(table_ref, *unit_matrix(), False)
+
+    for j in range(count):
+        values = jnp.concatenate([odd_ref[:, j, 0], odd_ref[:, j, 1]], axis=2)
+        product = right_product(values.reshape(half_radix * strip, 2 * lane), table_ref[...])
+        work_ref[j] = product.reshape(half_radix, strip, 2 * lane)
+
+    def store(j, s, here, re, im):
+        if j == 0:
+            re, im = re + before_ref[0, here, tile(s)], im + before_ref[1, here, tile(s)]
+        else:
+            re, im = re + out_ref[0, 0, here, tile(s)], im + out_ref[0, 1, here, tile(s)]
+        if j == count - 1:
+            re, im = times((re, im), (blend_ref[1, here, tile(s)], blend_ref[2, here, tile(s)]))
+            image_ref[0, here, tile(s)] = re
+        out_ref[0, 0, here, tile(s)] = re
+        out_ref[0, 1, here, tile(s)] = im
+
+    add_class(1, blend_ref, work_ref, turn_ref, store)
+
+
+def class_scratch():
+    return [
+        pltpu.VMEM((len(ref_speeds), half_radix, strip, 2 * lane), jnp.float32),
+        pltpu.VMEM((radix, 2, 8, lane), jnp.float32),
+        pltpu.VMEM((6 * lane, 2 * lane), jnp.bfloat16),
+    ]
+
+
+def start_call(evens, blend):
+    count = len(ref_speeds)
+    return pl.pallas_call(
+        start_kernel,
+        grid=(lane // strip,),
+        in_specs=[pl.BlockSpec((1, strip, full), lambda g: (0, g, 0))]
+        + [pl.BlockSpec((count, 2, strip, lane), lambda g: (0, 0, g, 0))] * half_radix,
+        out_specs=pl.BlockSpec((2, strip, full), lambda g: (0, g, 0)),
+        out_shape=jax.ShapeDtypeStruct((2, lane, full), jnp.float32),
+        scratch_shapes=class_scratch(),
+        compiler_params=pltpu.CompilerParams(vmem_limit_bytes=vmem_bytes),
+        cost_estimate=pl.CostEstimate(
+            flops=count * 2 * lane * full * 6 * lane, bytes_accessed=36 * lane * full, transcendentals=0
+        ),
+        name="inverse_lines_start",
+    )(blend, *evens)
+
+
+def finish_call(odd, before, blend):
     count = len(ref_speeds)
     return pl.pallas_call(
         finish_kernel,
         grid=(lane // strip,),
         in_specs=[
             pl.BlockSpec((half_radix, count, 2, strip, lane), lambda g: (0, 0, 0, g, 0)),
+            pl.BlockSpec((2, strip, full), lambda g: (0, g, 0)),
             pl.BlockSpec((3, strip, full), lambda g: (0, g, 0)),
-            *[pl.BlockSpec((count, 2, strip, lane), lambda g: (0, 0, g, 0))] * half_radix,
         ],
         out_specs=[
             pl.BlockSpec((1, 2, strip, full), lambda g: (0, 0, g, 0)),
@@ -747,14 +816,10 @@
             jax.ShapeDtypeStruct((1, 2, lane, full), jnp.float32),
             jax.ShapeDtypeStruct((1, lane, full), jnp.float32),
         ],
-        scratch_shapes=[
-            pltpu.VMEM((count, radix, strip, 2 * lane), jnp.float32),
-            pltpu.VMEM((radix, 2, 8, lane), jnp.float32),
-            pltpu.VMEM((6 * lane, 2 * lane), jnp.bfloat16),
-        ],
+        scratch_shapes=class_scratch(),
         compiler_params=pltpu.CompilerParams(vmem_limit_bytes=finish_vmem_bytes),
         name="inverse_lines",
-    )(odd, blend, *evens)
+    )(odd, before, blend)
 
 
 def exchange(values, group):
@@ -787,16 +852,19 @@
     phase = phase_call(frequencies)
     beyond, phase, even, odd = lax.optimization_barrier((beyond, phase, even, odd))
     odd = exchange(odd, radix)
-    evens = rows_call(0, True, even, phase)
-    evens = [part if k == 0 else lax.ppermute(part, "slab", partners(k)) for k, part in enumerate(evens)]
+    order = (4, 5, 6, 7, 2, 3, 1, 0)
+    parts = rows_call(0, True, even, phase)
+    moved = {k: lax.ppermute(parts[k], "slab", partners(k)) if k else parts[0] for k in order}
+    evens = [moved[k] for k in range(half_radix)]
+    odd = rows_call(1, False, odd, phase)
     beyond, _ = lax.optimization_barrier((beyond, odd))
     beyond = lax.ppermute(beyond, "slab", partners(far))
-    odd = rows_call(1, False, odd, phase)
     evens, beyond, odd = lax.optimization_barrier((evens, beyond, odd))
     odd = exchange(odd, half_radix)
     swapped = lax.ppermute(beyond, "shot", [(0, 1), (1, 0)])
     blend = blend_call(frequencies, bracket, beyond, swapped, *speeds)
-    propagated, image = finish_call(evens, odd, blend)
+    started = start_call(evens, blend)
+    propagated, image = finish_call(odd, started, blend)
     return propagated, image
 
 

time: 194 us -> 193 us (level)
  Pallas kernels: 55.9 us -> 61.4 us
  waiting for transfers between devices: 89.3 us -> 84.5 us
    all_to_all x3, waiting for transfers between devices: 56.3 us -> 33.4 us  [exchange(): lax.all_to_all(values, 'slab', split_axis=0, concat_axis=0, tiled=True, a...]
    ppermute x7, waiting for transfers between devices: 11.9 us -> 28.5 us  [per_device(): lax.ppermute(parts[k], 'slab', partners(k))]
    pallas_call x0 -> x1, Pallas kernels: none -> 6.31 us  [start_call(): pl.pallas_call(start_kernel, grid=(lane // strip,), in_specs=[pl.BlockSpe...]
    pallas_call x1, Pallas kernels: 8.77 us -> 6.57 us  [finish_call(): pl.pallas_call(finish_kernel, grid=(lane // strip,), in_specs=[pl.BlockSp...]
    unnamed x44 -> x36, local copies, waits for them, and re-layouts: 9.46 us -> 8.88 us
  transfers between devices with their start and end apart: 19 -> 19, of which waited for: 11 -> 12; matrix products, arithmetic and copies ran while one was open for 3% -> 3% of each run, Pallas kernels for 23% -> 27%
where the time goes in v6:
time: 193 us; the launch traced here: 189 us
  waiting for transfers between devices  84.5 us (44%)
  Pallas kernels  61.4 us (32%)
  starting transfers between devices  31 us (16%)
  local copies, waits for them, and re-layouts  10.2 us (5%)
    all_to_all x3, waiting for transfers between devices, exchange(): lax.all_to_all(values, 'slab', split_axis=0, concat_axis=0, tiled=True, a...  33.4 us
    ppermute x7, waiting for transfers between devices, per_device(): lax.ppermute(parts[k], 'slab', partners(k))  28.5 us
    pallas_call x2, Pallas kernels, rows_call(): pl.pallas_call(functools.partial(rows_kernel, c, apart), in_specs=[in_vme...  23 us
    all_to_all x3, starting transfers between devices, exchange(): lax.all_to_all(values, 'slab', split_axis=0, concat_axis=0, tiled=True, a...  15.6 us
    pallas_call x1, Pallas kernels, phase_call(): pl.pallas_call(phase_kernel, in_specs=[pl.BlockSpec(memory_space=pltpu.SM...  14.5 us
    ppermute x7, waiting for transfers between devices, speeds_near(): tiles.append(lax.ppermute(both, 'slab', partners(k)) if k else both)  13.8 us
    unnamed x36, local copies, waits for them, and re-layouts  8.88 us
    ppermute x7, starting transfers between devices, speeds_near(): tiles.append(lax.ppermute(both, 'slab', partners(k)) if k else both)  6.92 us
  transfers between devices with their start and end apart: 19, of which 12 were waited for; matrix products, arithmetic and copies ran while one was open for 3% of the time, Pallas kernels for 27%

profile of v6, /device:TPU:13, one launch (start us, length us, event | category | flops | bytes accessed | tf_op | source)
XLA Modules:
  0.0 189.3 jit_solution(8014004511516156516)
XLA Ops:
  0.6 3.3 %forward_lines.2 = f32[16,2,128,128]{3,2,1,0:T(8,128)} custom-call(f32[1,2,128,2048]{3,2,1,0:T(8,128)} %field_ref.2, f32[16,2,8,128]{3,2,1,0:T(8,128)} %constant.53.clone.turn_ref, bf16[768,256]{1,0:T(8,128)(2,1)} %constant.54.clone.table_ref), custom_call_target="tpu_custom_call" | custom-call | flops 805306368 | bytes 4194304 | tf_op jit(solution)/shard_map/forward_lines/pallas_call | solution.py:391
  3.9 6.7 %all-to-all-start = ((f32[16,2,128,128]{3,2,1,0:T(8,128)}), f32[16,2,128,128]{3,2,1,0:T(8,128)S(1)}, u32[]{:S(2)}, u32[]{:S(2)}) async-start(f32[16,2,128,128]{3,2,1,0:T(8,128)} %forward_lines.2), calls=%async_computation | async-start | bytes 4194304 | tf_op jit(solution)/shard_map/all_to_all | solution.py:827
  10.6 0.7 dynamic-slice_bitcast_fusion.15
  11.3 0.4 collective-permute-start
  11.8 0.3 collective-permute-start.1
  12.1 1.6 collective-permute-start.2
  13.7 0.3 collective-permute-start.3
  14.1 1.5 collective-permute-start.4
  16.2 14.5 %phase_factors.1.phase_ref = f32[2,3,2,128,2048]{4,3,2,1,0:T(8,128)} custom-call(f32[1]{0:T(128)S(6)} %copy.17.angular_ref), custom_call_target="tpu_custom_call" | custom-call | flops 94371840 | bytes 12582912 | tf_op jit(solution)/shard_map/phase_factors/pallas_call | solution.py:447
  30.6 3.3 %forward_lines.3 = f32[16,2,128,128]{3,2,1,0:T(8,128)} custom-call(f32[1,2,128,2048]{3,2,1,0:T(8,128)} %field_ref.2, f32[16,2,8,128]{3,2,1,0:T(8,128)} %constant.53.clone.turn_ref, bf16[768,256]{1,0:T(8,128)(2,1)} %constant.54.clone.table_ref), custom_call_target="tpu_custom_call" | custom-call | flops 805306368 | bytes 4194304 | tf_op jit(solution)/shard_map/forward_lines/pallas_call | solution.py:391
  34.1 0.6 fusion.6
  34.7 2.6 %collective-permute-start.6 = (f32[192,128]{1,0:T(8,128)S(1)}, f32[192,128]{1,0:T(8,128)S(1)}, u32[]{:S(2)}, u32[]{:S(2)}) collective-permute-start(f32[192,128]{1,0:T(8,128)S(1)} %pad_maximum_fusion.6), channel_id=1, source_target_pairs={{0,7},{1,6},{2,5},{3,4},{4,3},{5,2},{6,1},{7,0},{8,15},{9,14},{10,... | collective-permute-start | bytes 294920 | tf_op jit(solution)/shard_map/ppermute | solution.py:841
  37.3 0.6 fusion.5
  37.9 0.6 fusion.4
  38.6 9.6 %collective-permute-done.3.refs_4_ = f32[192,128]{1,0:T(8,128)S(1)} collective-permute-done((f32[192,128]{1,0:T(8,128)S(1)}, f32[192,128]{1,0:T(8,128)S(1)}, u32[]{:S(2)}, u32[]{:S(2)}) %collective-permute-start.3) | collective-permute-done | bytes 98336 | tf_op jit(solution)/shard_map/ppermute | solution.py:841
  48.2 0.6 fusion.3
  48.8 2.4 %collective-permute-done.4.refs_5_ = f32[192,128]{1,0:T(8,128)S(1)} collective-permute-done((f32[192,128]{1,0:T(8,128)S(1)}, f32[192,128]{1,0:T(8,128)S(1)}, u32[]{:S(2)}, u32[]{:S(2)}) %collective-permute-start.4) | collective-permute-done | bytes 98336 | tf_op jit(solution)/shard_map/ppermute | solution.py:841
  51.3 0.7 fusion.2
  52.2 0.6 fusion.1
  52.9 1.5 collective-permute-done.6.refs_7_
  54.3 0.6 fusion
  55.0 4.4 %all-to-all-done.in_ref = f32[16,2,128,128]{3,2,1,0:T(8,128)S(1)} async-done(((f32[16,2,128,128]{3,2,1,0:T(8,128)}), f32[16,2,128,128]{3,2,1,0:T(8,128)S(1)}, u32[]{:S(2)}, u32[]{:S(2)}) %all-to-all-start) | async-done | bytes 2097184 | tf_op jit(solution)/shard_map/all_to_all | solution.py:827
  59.5 1.3 copy-done.2
  60.7 4.2 %all-to-all-start.1 = ((f32[16,2,128,128]{3,2,1,0:T(8,128)}), f32[16,2,128,128]{3,2,1,0:T(8,128)S(1)}, u32[]{:S(2)}, u32[]{:S(2)}) async-start(f32[16,2,128,128]{3,2,1,0:T(8,128)} %forward_lines.3), calls=%async_computation.1 | async-start | bytes 4194304 | tf_op jit(solution)/shard_map/all_to_all | solution.py:827
  65.0 13.7 %rows_there_and_back.2 = (f32[3,2,128,128]{3,2,1,0:T(8,128)S(1)}, f32[3,2,128,128]{3,2,1,0:T(8,128)S(1)}, f32[3,2,128,128]{3,2,1,0:T(8,128)S(1)}, f32[3,2,128,12...) custom-call(f32[16,2,128,128]{3,2,1,0:T(8,128)} %copy-done.2, ...), custom_call_target="tpu_custom_call" | custom-call | flops 6442450944 | bytes 58720256 | tf_op jit(solution)/shard_map/rows_there_and_back/pallas_call | solution.py:619
  78.7 0.7 copy-done.1
  79.4 0.4 collective-permute-start.7
  80.0 1.5 collective-permute-start.9
  81.8 1.4 collective-permute-start.11
  83.3 13.3 %collective-permute-done.8.refs_2_ = f32[3,2,128,128]{3,2,1,0:T(8,128)S(1)} collective-permute-done((f32[3,2,128,128]{3,2,1,0:T(8,128)S(1)}, f32[3,2,128,128]{3,2,1,0:T(8,128)S(1)}, u32[]{:S(2)}, u32[]{:S(2)}) %collective-permute-start.8) | collective-permute-done | bytes 393248 | tf_op jit(solution)/shard_map/ppermute | solution.py:857
  96.6 0.7 copy-done.5
  97.3 2.4 %collective-permute-start.13 = (f32[3,2,128,128]{3,2,1,0:T(8,128)S(1)}, f32[3,2,128,128]{3,2,1,0:T(8,128)}, u32[]{:S(2)}, u32[]{:S(2)}) collective-permute-start(f32[3,2,128,128]{3,2,1,0:T(8,128)S(1)} %get-tuple-element.40), channel_id=1, source_target_pairs={{0,7},{1,6},{2,5},{3,4},{4,3},{5,2},{6,1},{7,0},{8,15},{9,14},{10,... | collective-permute-start | bytes 1179656 | tf_op jit(solution)/shard_map/ppermute | solution.py:857
  99.8 13.1 %all-to-all-done.1.in_ref = f32[16,2,128,128]{3,2,1,0:T(8,128)S(1)} async-done(((f32[16,2,128,128]{3,2,1,0:T(8,128)}), f32[16,2,128,128]{3,2,1,0:T(8,128)S(1)}, u32[]{:S(2)}, u32[]{:S(2)}) %all-to-all-start.1) | async-done | bytes 2097184 | tf_op jit(solution)/shard_map/all_to_all | solution.py:827
  112.9 9.3 %rows_there_and_back.3 = f32[8,3,2,128,128]{4,3,2,1,0:T(8,128)} custom-call(f32[16,2,128,128]{3,2,1,0:T(8,128)S(1)} %all-to-all-done.1.in_ref, f32[2,3,2,128,2048]{4,3,2,1,0:T(8,128)} %phase_factors.1.phase_ref), custom_call_target="tpu_custom_call" | custom-call | flops 6442450944 | bytes 58720256 | tf_op jit(solution)/shard_map/rows_there_and_back/pallas_call | solution.py:619
  122.2 0.9 collective-permute-start.14
  123.2 6.7 %collective-permute-done.12.refs_6_ = f32[3,2,128,128]{3,2,1,0:T(8,128)} collective-permute-done((f32[3,2,128,128]{3,2,1,0:T(8,128)S(1)}, f32[3,2,128,128]{3,2,1,0:T(8,128)}, u32[]{:S(2)}, u32[]{:S(2)}) %collective-permute-start.12) | collective-permute-done | bytes 393248 | tf_op jit(solution)/shard_map/ppermute | solution.py:857
  129.9 8.4 %collective-permute-done.13.refs_7_ = f32[3,2,128,128]{3,2,1,0:T(8,128)} collective-permute-done((f32[3,2,128,128]{3,2,1,0:T(8,128)S(1)}, f32[3,2,128,128]{3,2,1,0:T(8,128)}, u32[]{:S(2)}, u32[]{:S(2)}) %collective-permute-start.13) | collective-permute-done | bytes 393248 | tf_op jit(solution)/shard_map/ppermute | solution.py:857
  138.3 3.1 %collective-permute-done.14.far_ref = f32[8,64,128]{2,1,0:T(8,128)S(1)} collective-permute-done((f32[8,64,128]{2,1,0:T(8,128)}, f32[8,64,128]{2,1,0:T(8,128)S(1)}, u32[]{:S(2)}, u32[]{:S(2)}) %collective-permute-start.14) | collective-permute-done | bytes 262176 | tf_op jit(solution)/shard_map/ppermute | solution.py:861
  141.4 4.7 %all-to-all-start.2 = ((f32[8,3,2,128,128]{4,3,2,1,0:T(8,128)}), f32[8,3,2,128,128]{4,3,2,1,0:T(8,128)S(1)}, u32[]{:S(2)}, u32[]{:S(2)}) async-start(f32[8,3,2,128,128]{4,3,2,1,0:T(8,128)} %rows_there_and_back.3), calls=%async_computation.2 | async-start | bytes 6291456 | tf_op jit(solution)/shard_map/all_to_all | solution.py:827
  146.2 1.2 collective-permute-start.15
  147.4 0.6 pad_maximum_fusion.7.refs_0_
  148.0 5.7 %collective-permute-done.15.swapped_ref = f32[8,64,128]{2,1,0:T(8,128)S(1)} collective-permute-done((f32[8,64,128]{2,1,0:T(8,128)S(1)}, f32[8,64,128]{2,1,0:T(8,128)S(1)}, u32[]{:S(2)}, u32[]{:S(2)}) %collective-permute-start.15) | collective-permute-done | bytes 262176 | tf_op jit(solution)/shard_map/ppermute | solution.py:864
  153.7 0.7 copy-done.7
  154.4 4.6 %blend_factors.1.blend_ref = f32[3,128,2048]{2,1,0:T(8,128)} custom-call(f32[1]{0:T(128)S(6)} %copy.17.angular_ref, s32[1,128,2048]{2,1,0:T(8,128)} %bracket_ref.1, f32[8,64,128]{2,1,0:T(8,128)} %copy-done.6, f32[8,64,128]{2,1,0:T(8,128)} %copy-done.7, f32[192,128]{1,0:T(8,128)} %pad_maximum_fusion.7.refs_0_, f32[192,128]{1,0:T(8,128)} %copy-done.8, ...), custom_call_target="tpu_custom_call" | custom-call | flops 15728640 | bytes 6291456 | tf_op jit(solution)/shard_map/blend_factors/pallas_call | solution.py:674
  159.0 6.3 %inverse_lines_start.1.before_ref = f32[2,128,2048]{2,1,0:T(8,128)} custom-call(f32[3,128,2048]{2,1,0:T(8,128)} %blend_factors.1.blend_ref, f32[3,2,128,128]{3,2,1,0:T(8,128)} %copy-done.1, f32[3,2,128,128]{3,2,1,0:T(8,128)} %copy-done.4, f32[3,2,128,128]{3,2,1,0:T(8,128)} %copy-done.5, f32[3,2,128,128]{3,2,1,0:T(8,128)} %collective-permute-done.9.refs_3_, ...), custom_call_target="tpu_custom_call" | custom-call | flops 1207959552 | bytes 9437184 | tf_op jit(solution)/shard_map/inverse_lines_start/pallas_call | solution.py:785
  165.3 15.8 %all-to-all-done.2.odd_ref = f32[8,3,2,128,128]{4,3,2,1,0:T(8,128)S(1)} async-done(((f32[8,3,2,128,128]{4,3,2,1,0:T(8,128)}), f32[8,3,2,128,128]{4,3,2,1,0:T(8,128)S(1)}, u32[]{:S(2)}, u32[]{:S(2)}) %all-to-all-start.2) | async-done | bytes 3145760 | tf_op jit(solution)/shard_map/all_to_all | solution.py:827
  181.1 1.6 copy-done
  182.7 6.6 %inverse_lines.1 = (f32[1,2,128,2048]{3,2,1,0:T(8,128)}, f32[1,128,2048]{2,1,0:T(8,128)}) custom-call(f32[8,3,2,128,128]{4,3,2,1,0:T(8,128)S(1)} %all-to-all-done.2.odd_ref, f32[2,128,2048]{2,1,0:T(8,128)S(1)} %copy-done, f32[3,128,2048]{2,1,0:T(8,128)} %blend_factors.1.blend_ref), custom_call_target="tpu_custom_call" | custom-call | tf_op jit(solution)/shard_map/inverse_lines/pallas_call | solution.py:803
  (45 shorter events, 1.2 us)
Async XLA Ops:
  3.9 6.7 %copy-start.3 = (f32[1,128,2048]{2,1,0:T(8,128)S(1)}, f32[1,128,2048]{2,1,0:T(8,128)}, u32[]{:S(2)}) copy-start(f32[1,128,2048]{2,1,0:T(8,128)} %param.10) | copy-start | bytes 3145732
  3.9 55.5 %all-to-all-start = ((f32[16,2,128,128]{3,2,1,0:T(8,128)}), f32[16,2,128,128]{3,2,1,0:T(8,128)S(1)}, u32[]{:S(2)}, u32[]{:S(2)}) async-start(f32[16,2,128,128]{3,2,1,0:T(8,128)} %forward_lines.2), calls=%async_computation | async-start | bytes 4194304 | tf_op jit(solution)/shard_map/all_to_all | solution.py:827
  11.3 22.6 %collective-permute-start = (f32[192,128]{1,0:T(8,128)S(1)}, f32[192,128]{1,0:T(8,128)S(1)}, u32[]{:S(2)}, u32[]{:S(2)}) collective-permute-start(f32[192,128]{1,0:T(8,128)S(1)} %pad_maximum_fusion), channel_id=1, source_target_pairs={{0,1},{1,0},{2,3},{3,2},{4,5},{5,4},{6,7},{7,6},{8,9},{9,8},{10,11... | collective-permute-start | bytes 294920 | tf_op jit(solution)/shard_map/ppermute | solution.py:841
  11.8 22.9 %collective-permute-start.1 = (f32[192,128]{1,0:T(8,128)S(1)}, f32[192,128]{1,0:T(8,128)S(1)}, u32[]{:S(2)}, u32[]{:S(2)}) collective-permute-start(f32[192,128]{1,0:T(8,128)S(1)} %pad_maximum_fusion.1), channel_id=1, source_target_pairs={{0,2},{1,3},{2,0},{3,1},{4,6},{5,7},{6,4},{7,5},{8,10},{9,11},{10,... | collective-permute-start | bytes 294920 | tf_op jit(solution)/shard_map/ppermute | solution.py:841
  12.1 25.8 %collective-permute-start.2 = (f32[192,128]{1,0:T(8,128)S(1)}, f32[192,128]{1,0:T(8,128)S(1)}, u32[]{:S(2)}, u32[]{:S(2)}) collective-permute-start(f32[192,128]{1,0:T(8,128)S(1)} %pad_maximum_fusion.2), channel_id=1, source_target_pairs={{0,3},{1,2},{2,1},{3,0},{4,7},{5,6},{6,5},{7,4},{8,11},{9,10},{10,... | collective-permute-start | bytes 294920 | tf_op jit(solution)/shard_map/ppermute | solution.py:841
  13.7 34.5 %collective-permute-start.3 = (f32[192,128]{1,0:T(8,128)S(1)}, f32[192,128]{1,0:T(8,128)S(1)}, u32[]{:S(2)}, u32[]{:S(2)}) collective-permute-start(f32[192,128]{1,0:T(8,128)S(1)} %pad_maximum_fusion.3), channel_id=1, source_target_pairs={{0,4},{1,5},{2,6},{3,7},{4,0},{5,1},{6,2},{7,3},{8,12},{9,13},{10,... | collective-permute-start | bytes 294920 | tf_op jit(solution)/shard_map/ppermute | solution.py:841
  14.1 37.2 %collective-permute-start.4 = (f32[192,128]{1,0:T(8,128)S(1)}, f32[192,128]{1,0:T(8,128)S(1)}, u32[]{:S(2)}, u32[]{:S(2)}) collective-permute-start(f32[192,128]{1,0:T(8,128)S(1)} %pad_maximum_fusion.4), channel_id=1, source_target_pairs={{0,5},{1,4},{2,7},{3,6},{4,1},{5,0},{6,3},{7,2},{8,13},{9,12},{10,... | collective-permute-start | bytes 294920 | tf_op jit(solution)/shard_map/ppermute | solution.py:841
  34.0 25.5 %copy-start.8 = (f32[192,128]{1,0:T(8,128)}, f32[192,128]{1,0:T(8,128)S(1)}, u32[]{:S(2)}) copy-start(f32[192,128]{1,0:T(8,128)S(1)} %collective-permute-done.refs_1_) | copy-start | bytes 294916
  34.0 18.2 %collective-permute-start.5 = (f32[192,128]{1,0:T(8,128)S(1)}, f32[192,128]{1,0:T(8,128)S(1)}, u32[]{:S(2)}, u32[]{:S(2)}) collective-permute-start(f32[192,128]{1,0:T(8,128)S(1)} %pad_maximum_fusion.5), channel_id=1, source_target_pairs={{0,6},{1,7},{2,4},{3,5},{4,2},{5,3},{6,0},{7,1},{8,14},{9,15},{10,... | collective-permute-start | bytes 294920 | tf_op jit(solution)/shard_map/ppermute | solution.py:841
  34.7 24.7 %copy-start.9 = (f32[192,128]{1,0:T(8,128)}, f32[192,128]{1,0:T(8,128)S(1)}, u32[]{:S(2)}) copy-start(f32[192,128]{1,0:T(8,128)S(1)} %collective-permute-done.1.refs_2_) | copy-start | bytes 294916
  34.7 19.6 %collective-permute-start.6 = (f32[192,128]{1,0:T(8,128)S(1)}, f32[192,128]{1,0:T(8,128)S(1)}, u32[]{:S(2)}, u32[]{:S(2)}) collective-permute-start(f32[192,128]{1,0:T(8,128)S(1)} %pad_maximum_fusion.6), channel_id=1, source_target_pairs={{0,7},{1,6},{2,5},{3,4},{4,3},{5,2},{6,1},{7,0},{8,15},{9,14},{10,... | collective-permute-start | bytes 294920 | tf_op jit(solution)/shard_map/ppermute | solution.py:841
  37.9 21.5 %copy-start.10 = (f32[192,128]{1,0:T(8,128)}, f32[192,128]{1,0:T(8,128)S(1)}, u32[]{:S(2)}) copy-start(f32[192,128]{1,0:T(8,128)S(1)} %collective-permute-done.2.refs_3_) | copy-start | bytes 294916
  48.2 11.2 %copy-start.11 = (f32[192,128]{1,0:T(8,128)}, f32[192,128]{1,0:T(8,128)S(1)}, u32[]{:S(2)}) copy-start(f32[192,128]{1,0:T(8,128)S(1)} %collective-permute-done.3.refs_4_) | copy-start | bytes 294916
  51.3 27.4 %copy-start.12 = (f32[192,128]{1,0:T(8,128)}, f32[192,128]{1,0:T(8,128)S(1)}, u32[]{:S(2)}) copy-start(f32[192,128]{1,0:T(8,128)S(1)} %collective-permute-done.4.refs_5_) | copy-start | bytes 294916
  52.2 7.2 %copy-start.13 = (f32[192,128]{1,0:T(8,128)}, f32[192,128]{1,0:T(8,128)S(1)}, u32[]{:S(2)}) copy-start(f32[192,128]{1,0:T(8,128)S(1)} %collective-permute-done.5.refs_6_) | copy-start | bytes 294916
  54.3 5.1 %copy-start.14 = (f32[192,128]{1,0:T(8,128)}, f32[192,128]{1,0:T(8,128)S(1)}, u32[]{:S(2)}) copy-start(f32[192,128]{1,0:T(8,128)S(1)} %collective-permute-done.6.refs_7_) | copy-start | bytes 294916
  59.4 1.3 copy-start.2
  60.7 52.2 %all-to-all-start.1 = ((f32[16,2,128,128]{3,2,1,0:T(8,128)}), f32[16,2,128,128]{3,2,1,0:T(8,128)S(1)}, u32[]{:S(2)}, u32[]{:S(2)}) async-start(f32[16,2,128,128]{3,2,1,0:T(8,128)} %forward_lines.3), calls=%async_computation.1 | async-start | bytes 4194304 | tf_op jit(solution)/shard_map/all_to_all | solution.py:827
  78.6 0.8 copy-start.1
  79.4 3.9 %collective-permute-start.7 = (f32[3,2,128,128]{3,2,1,0:T(8,128)S(1)}, f32[3,2,128,128]{3,2,1,0:T(8,128)S(1)}, u32[]{:S(2)}, u32[]{:S(2)}) collective-permute-start(f32[3,2,128,128]{3,2,1,0:T(8,128)S(1)} %get-tuple-element.34), channel_id=1, source_target_pairs={{0,1},{1,0},{2,3},{3,2},{4,5},{5,4},{6,7},{7,6},{8,9},{9,8},{10,11... | collective-permute-start | bytes 1179656 | tf_op jit(solution)/shard_map/ppermute | solution.py:857
  79.8 16.8 %collective-permute-start.8 = (f32[3,2,128,128]{3,2,1,0:T(8,128)S(1)}, f32[3,2,128,128]{3,2,1,0:T(8,128)S(1)}, u32[]{:S(2)}, u32[]{:S(2)}) collective-permute-start(f32[3,2,128,128]{3,2,1,0:T(8,128)S(1)} %get-tuple-element.35), channel_id=1, source_target_pairs={{0,2},{1,3},{2,0},{3,1},{4,6},{5,7},{6,4},{7,5},{8,10},{9,11},{10,... | collective-permute-start | bytes 1179656 | tf_op jit(solution)/shard_map/ppermute | solution.py:857
  80.0 42.2 %collective-permute-start.9 = (f32[3,2,128,128]{3,2,1,0:T(8,128)}, f32[3,2,128,128]{3,2,1,0:T(8,128)}, u32[]{:S(2)}, u32[]{:S(2)}) collective-permute-start(f32[3,2,128,128]{3,2,1,0:T(8,128)} %get-tuple-element.36), channel_id=1, source_target_pairs={{0,3},{1,2},{2,1},{3,0},{4,7},{5,6},{6,5},{7,4},{8,11},{9,10},{10,... | collective-permute-start | bytes 1179656 | tf_op jit(solution)/shard_map/ppermute | solution.py:857
  81.6 41.6 %collective-permute-start.10 = (f32[3,2,128,128]{3,2,1,0:T(8,128)}, f32[3,2,128,128]{3,2,1,0:T(8,128)}, u32[]{:S(2)}, u32[]{:S(2)}) collective-permute-start(f32[3,2,128,128]{3,2,1,0:T(8,128)} %get-tuple-element.37), channel_id=1, source_target_pairs={{0,4},{1,5},{2,6},{3,7},{4,0},{5,1},{6,2},{7,3},{8,12},{9,13},{10,... | collective-permute-start | bytes 1179656 | tf_op jit(solution)/shard_map/ppermute | solution.py:857
  81.8 41.3 %collective-permute-start.11 = (f32[3,2,128,128]{3,2,1,0:T(8,128)S(1)}, f32[3,2,128,128]{3,2,1,0:T(8,128)}, u32[]{:S(2)}, u32[]{:S(2)}) collective-permute-start(f32[3,2,128,128]{3,2,1,0:T(8,128)S(1)} %get-tuple-element.38), channel_id=1, source_target_pairs={{0,5},{1,4},{2,7},{3,6},{4,1},{5,0},{6,3},{7,2},{8,13},{9,12},{10,... | collective-permute-start | bytes 1179656 | tf_op jit(solution)/shard_map/ppermute | solution.py:857
  83.3 13.3 %copy-start.4 = (f32[3,2,128,128]{3,2,1,0:T(8,128)}, f32[3,2,128,128]{3,2,1,0:T(8,128)S(1)}, u32[]{:S(2)}) copy-start(f32[3,2,128,128]{3,2,1,0:T(8,128)S(1)} %collective-permute-done.7.refs_1_) | copy-start | bytes 1179652
  83.3 46.6 %collective-permute-start.12 = (f32[3,2,128,128]{3,2,1,0:T(8,128)S(1)}, f32[3,2,128,128]{3,2,1,0:T(8,128)}, u32[]{:S(2)}, u32[]{:S(2)}) collective-permute-start(f32[3,2,128,128]{3,2,1,0:T(8,128)S(1)} %get-tuple-element.39), channel_id=1, source_target_pairs={{0,6},{1,7},{2,4},{3,5},{4,2},{5,3},{6,0},{7,1},{8,14},{9,15},{10,... | collective-permute-start | bytes 1179656 | tf_op jit(solution)/shard_map/ppermute | solution.py:857
  96.6 0.7 copy-start.5
  97.3 41.0 %collective-permute-start.13 = (f32[3,2,128,128]{3,2,1,0:T(8,128)S(1)}, f32[3,2,128,128]{3,2,1,0:T(8,128)}, u32[]{:S(2)}, u32[]{:S(2)}) collective-permute-start(f32[3,2,128,128]{3,2,1,0:T(8,128)S(1)} %get-tuple-element.40), channel_id=1, source_target_pairs={{0,7},{1,6},{2,5},{3,4},{4,3},{5,2},{6,1},{7,0},{8,15},{9,14},{10,... | collective-permute-start | bytes 1179656 | tf_op jit(solution)/shard_map/ppermute | solution.py:857
  122.2 19.2 %collective-permute-start.14 = (f32[8,64,128]{2,1,0:T(8,128)}, f32[8,64,128]{2,1,0:T(8,128)S(1)}, u32[]{:S(2)}, u32[]{:S(2)}) collective-permute-start(f32[8,64,128]{2,1,0:T(8,128)} %fusion), channel_id=1, source_target_pairs={{0,8},{1,9},{2,10},{3,11},{4,12},{5,13},{6,14},{7,15},{8,0},{9,1},... | collective-permute-start | bytes 786440 | tf_op jit(solution)/shard_map/ppermute | solution.py:861
  141.4 4.7 %copy-start.6 = (f32[8,64,128]{2,1,0:T(8,128)}, f32[8,64,128]{2,1,0:T(8,128)S(1)}, u32[]{:S(2)}) copy-start(f32[8,64,128]{2,1,0:T(8,128)S(1)} %collective-permute-done.14.far_ref) | copy-start | bytes 786436
  141.4 39.7 %all-to-all-start.2 = ((f32[8,3,2,128,128]{4,3,2,1,0:T(8,128)}), f32[8,3,2,128,128]{4,3,2,1,0:T(8,128)S(1)}, u32[]{:S(2)}, u32[]{:S(2)}) async-start(f32[8,3,2,128,128]{4,3,2,1,0:T(8,128)} %rows_there_and_back.3), calls=%async_computation.2 | async-start | bytes 6291456 | tf_op jit(solution)/shard_map/all_to_all | solution.py:827
  146.2 7.5 %collective-permute-start.15 = (f32[8,64,128]{2,1,0:T(8,128)S(1)}, f32[8,64,128]{2,1,0:T(8,128)S(1)}, u32[]{:S(2)}, u32[]{:S(2)}) collective-permute-start(f32[8,64,128]{2,1,0:T(8,128)S(1)} %collective-permute-done.14.far_ref), channel_id=1, source_target_pairs={{0,16},{16,0},{1,17},{17,1},{2,18},{18,2},{3,19},{19,3},{4,20},{20... | collective-permute-start | bytes 786440 | tf_op jit(solution)/shard_map/ppermute | solution.py:864
  153.7 0.7 copy-start.7
  181.1 1.6 copy-start
